TPU v7x, 32 devices: a whole 2x2x4 slice. The times are simulated.
32 devices in a mesh: ctx: 8 (over z, x), fsdp: 4 (over y, core).
Axes of the slice: x: 2, y: 2, z: 4, core: 2. Of those that a mesh axis runs over, the one named last changes fastest.
Arguments:
- tokens: bfloat16 [4, 4096, 1024], P('fsdp', 'ctx'), may hold values from -6 to 6
- teacher: bfloat16 [4, 4096, 1024], P('fsdp', 'ctx'), may hold values from -6 to 6
- lengths: int32 [4, 2], P('fsdp'), may hold values from 1024 to 2048, as said below
- pair_owner: int32 [8], replicated, may hold values from 0 to 7, each once
- norm_gain: bfloat16 [1024], P('fsdp'), may hold values from 0.5 to 1.5
- in_proj: bfloat16 [1024, 4096], P('fsdp'), may hold values from -0.1875 to 0.1875
- conv_weight: bfloat16 [4, 2048], P(None, 'fsdp'), may hold values from -3 to 3
- conv_bias: bfloat16 [2048], P('fsdp'), may hold values from -1.5 to 1.5
- x_proj: bfloat16 [2048, 96], P('fsdp'), may hold values from -0.125 to 0.125
- dt_proj: bfloat16 [64, 2048], P(None, 'fsdp'), may hold values from -0.75 to 0.75
- dt_bias: bfloat16 [2048], P('fsdp'), may hold values from -12 to -3.5
- a_log: bfloat16 [16, 2048], P(None, 'fsdp'), may hold values from 0 to 2.765625
- skip_scale: bfloat16 [2048], P('fsdp'), may hold values from 0.5 to 1.5
- out_proj: bfloat16 [2048, 1024], P('fsdp'), may hold values from -0.125 to 0.125
Outputs:
- output: bfloat16 [4, 4096, 1024], P('fsdp', 'ctx')
- loss: float32 [], replicated
- grad_tokens: float32 [4, 4096, 1024], P('fsdp', 'ctx')
- grad_norm_gain: float32 [1024], P('fsdp')
- grad_in_proj: float32 [1024, 4096], P('fsdp')
- grad_conv_weight: float32 [4, 2048], P(None, 'fsdp')
- grad_conv_bias: float32 [2048], P('fsdp')
- grad_x_proj: float32 [2048, 96], P('fsdp')
- grad_dt_proj: float32 [64, 2048], P(None, 'fsdp')
- grad_dt_bias: float32 [2048], P('fsdp')
- grad_a_log: float32 [16, 2048], P(None, 'fsdp')
- grad_skip_scale: float32 [2048], P('fsdp')
- grad_out_proj: float32 [2048, 1024], P('fsdp')
Inputs may be any that keep to these rules, and one draw needn't show every extreme that they name: `lengths`: each sequence's valid slots are its first ones, at least half of its 2048 slots; in every group one of the two sequences fills all 2048. `pair_owner`: each index of ctx holds exactly one pair.
All inputs are finite; a program needn't handle non-finite values.
Results may differ from a plain program's by a relative error of at most 0.0095.
Values may be sent and summed in bfloat16 or wider, within the bound.
No kernel may reach another device: no remote copies, remote signals or barrier semaphores. Data moves between devices by JAX's collectives and lax.ppermute only.
A program may use at most 256 MiB of HBM per device.

v0:
```python
import jax
import jax.numpy as jnp
from jax import lax
from jax.sharding import PartitionSpec as P

BLOCK = 32


EPSILON = 1e-05


def run_linear(factors, sources, start, backward):

    def stepper(state_now, item_in):
        factor_now, source_now = item_in
        state_now = factor_now * state_now + source_now
        return (state_now, state_now)

    _, states = lax.scan(stepper, start, (factors, sources), reverse=backward, unroll=True)
    return states


def arrange(values, block_len):
    halves, seq_len, columns = values.shape
    return values.reshape(halves, seq_len // block_len, block_len, columns).transpose(1, 2, 0, 3)


def restore(values):
    block_count, block_len, halves, columns = values.shape
    return values.transpose(2, 0, 1, 3).reshape(halves, block_count * block_len, columns)


def rows_product(left, right):
    return lax.dot_general(
        left, right, (((0,), (0,)), ((), ())), preferred_element_type=jnp.float32
    )


def back_product(left, right):
    return lax.dot_general(
        left, right, (((1,), (1,)), ((), ())), preferred_element_type=jnp.float32
    )


def silu_slope(values):
    sigma = jax.nn.sigmoid(values)
    return sigma * (1.0 + values * (1.0 - sigma))


def sequence_order(gathered, pair_owner):
    return jnp.stack([gathered[pair_owner, 0], gathered[pair_owner[::-1], 1]], axis=1)


def pick_own(values, own_pos):
    return jnp.stack([values[own_pos[0], 0], values[own_pos[1], 1]])


def local(
    tokens,
    teacher,
    lengths,
    pair_owner,
    norm_gain,
    in_proj,
    conv_weight,
    conv_bias,
    x_proj,
    dt_proj,
    dt_bias,
    a_log,
    skip_scale,
    out_proj,
):
    ctx_size = lax.axis_size("ctx")
    fsdp_size = lax.axis_size("fsdp")
    my_index = lax.axis_index("ctx")
    piece_len = tokens.shape[1] // 2
    inner_width = in_proj.shape[1] // 2
    dt_rank = dt_proj.shape[0]
    state_dim = a_log.shape[0]
    tap_count = conv_weight.shape[0]
    block_len = BLOCK
    row_count = 2 * piece_len
    weights = (
        lax.all_gather(norm_gain, "fsdp", axis=0, tiled=True),
        lax.all_gather(in_proj, "fsdp", axis=0, tiled=True),
        lax.all_gather(conv_weight, "fsdp", axis=1, tiled=True),
        lax.all_gather(conv_bias, "fsdp", axis=0, tiled=True),
        lax.all_gather(x_proj, "fsdp", axis=0, tiled=True),
        lax.all_gather(dt_proj, "fsdp", axis=1, tiled=True),
        lax.all_gather(dt_bias, "fsdp", axis=0, tiled=True),
        lax.all_gather(a_log, "fsdp", axis=1, tiled=True),
        lax.all_gather(skip_scale, "fsdp", axis=0, tiled=True),
        lax.all_gather(out_proj, "fsdp", axis=0, tiled=True),
    )
    (
        gain_full,
        weight_in,
        conv_taps,
        conv_shift,
        weight_x,
        weight_dt,
        bias_dt,
        rate_log,
        skip_full,
        weight_out,
    ) = weights
    pair_id = jnp.sum(
        jnp.arange(ctx_size, dtype=jnp.int32) * (pair_owner == my_index).astype(jnp.int32)
    )
    own_pos = jnp.stack([pair_id, ctx_size - 1 - pair_id])
    position = own_pos[:, None] * piece_len + jnp.arange(piece_len, dtype=jnp.int32)[None, :]
    valid = (position < lengths[0][:, None]).astype(jnp.float32)
    valid_rows = valid.reshape(row_count, 1)
    has_before = jnp.stack([pair_id > 0, pair_id < ctx_size - 1])
    has_after = jnp.stack([pair_id < ctx_size - 1, pair_id > 0])
    lower_owner = pair_owner[jnp.maximum(pair_id - 1, 0)]
    upper_owner = pair_owner[jnp.minimum(pair_id + 1, ctx_size - 1)]
    rows = tokens[0].astype(jnp.float32)
    inv_rms = lax.rsqrt(jnp.mean(rows * rows, axis=1, keepdims=True) + EPSILON)
    gain_values = gain_full.astype(jnp.float32)
    normed = (rows * inv_rms * gain_values).astype(jnp.bfloat16)
    mixed = jnp.dot(normed, weight_in, preferred_element_type=jnp.float32)
    x_in = mixed[:, :inner_width].astype(jnp.bfloat16).reshape(2, piece_len, inner_width)
    gate_vals = mixed[:, inner_width:].reshape(2, piece_len, inner_width)
    tails = x_in[:, piece_len - (tap_count - 1) :]
    all_tails = lax.all_gather(tails[None], "ctx", axis=0, tiled=True)
    before_rows = jnp.stack([all_tails[lower_owner, 0], all_tails[upper_owner, 1]])
    before_rows = jnp.where(has_before[:, None, None], before_rows, jnp.zeros_like(before_rows))
    padded = jnp.concatenate([before_rows, x_in], axis=1).astype(jnp.float32)
    tap_values = conv_taps.astype(jnp.float32)
    conv_out = padded[:, 0:piece_len] * tap_values[0]
    for offset in range(1, tap_count):
        conv_out = conv_out + padded[:, offset : offset + piece_len] * tap_values[offset]
    conv_out = conv_out + conv_shift.astype(jnp.float32)
    xs_low = jax.nn.silu(conv_out).astype(jnp.bfloat16)
    xs_rows = xs_low.reshape(row_count, inner_width)
    xs_vals = xs_low.astype(jnp.float32)
    proj = jnp.dot(xs_rows, weight_x, preferred_element_type=jnp.float32)
    delta = proj[:, :dt_rank].astype(jnp.bfloat16)
    input_map = proj[:, dt_rank : dt_rank + state_dim].reshape(2, piece_len, state_dim)
    output_map = proj[:, dt_rank + state_dim :].reshape(2, piece_len, state_dim)
    pre_step = jnp.dot(delta, weight_dt, preferred_element_type=jnp.float32) + bias_dt.astype(
        jnp.float32
    )
    step_size = jax.nn.softplus(pre_step).reshape(2, piece_len, inner_width) * valid[:, :, None]
    neg_rate = -jnp.exp(rate_log.astype(jnp.float32))
    drive = step_size * xs_vals
    cumul = jnp.cumsum(step_size, axis=1)
    total_log = cumul[:, -1]
    zero_state = jnp.zeros((2, state_dim, inner_width), jnp.float32)
    step_blocks = arrange(step_size, block_len)
    drive_blocks = arrange(drive, block_len)
    input_blocks = arrange(input_map, block_len)
    output_blocks = arrange(output_map, block_len)
    cumul_blocks = arrange(cumul, block_len)

    def end_term(running, block_in):
        cum_blk, drive_blk, input_blk = block_in
        weight_blk = jnp.exp(neg_rate * (total_log[None, :, None, :] - cum_blk[:, :, None, :]))
        return (
            running
            + jnp.sum(weight_blk * drive_blk[:, :, None, :] * input_blk[:, :, :, None], axis=0),
            None,
        )

    end_state, _ = lax.scan(end_term, zero_state, (cumul_blocks, drive_blocks, input_blocks))
    decay_total = jnp.exp(neg_rate[None] * total_log[:, None, :])
    states_all, decays_all = (
        lax.all_gather(end_state[None].astype(jnp.bfloat16), "ctx", axis=0, tiled=True).astype(
            jnp.float32
        ),
        lax.all_gather(decay_total[None].astype(jnp.bfloat16), "ctx", axis=0, tiled=True).astype(
            jnp.float32
        ),
    )
    seq_ends = sequence_order(states_all, pair_owner)
    seq_decays = sequence_order(decays_all, pair_owner)

    def carry_step(carry_now, item_in):
        end_piece, decay_piece = item_in
        return (end_piece + decay_piece * carry_now, carry_now)

    _, carries = lax.scan(carry_step, zero_state, (seq_ends, seq_decays))
    carry_in = pick_own(carries, own_pos)

    def forward_block(state_in, block_in):
        step_blk, drive_blk, input_blk, output_blk = block_in
        decays = jnp.exp(step_blk[:, :, None, :] * neg_rate)
        pushes = drive_blk[:, :, None, :] * input_blk[:, :, :, None]
        hidden = run_linear(decays, pushes, state_in, False)
        return (hidden[-1], (state_in, jnp.sum(output_blk[:, :, :, None] * hidden, axis=2)))

    _, (block_starts, read_blocks) = lax.scan(
        forward_block, carry_in, (step_blocks, drive_blocks, input_blocks, output_blocks)
    )
    skip_values = skip_full.astype(jnp.float32)
    ssm = restore(read_blocks) + skip_values * xs_vals
    silu_gate = jax.nn.silu(gate_vals)
    branch = (ssm * silu_gate).astype(jnp.bfloat16).reshape(row_count, inner_width)
    block_out = rows + jnp.dot(branch, weight_out, preferred_element_type=jnp.float32)
    error_rows = block_out - teacher[0].astype(jnp.float32)
    square_local = jnp.sum(valid_rows * error_rows * error_rows)
    count_local = jnp.sum(valid)
    square_total, count_total = lax.psum((square_local, count_local), ("ctx", "fsdp"))
    loss = square_total / (count_total * block_out.shape[1])
    weights = (
        lax.all_gather(norm_gain, "fsdp", axis=0, tiled=True),
        lax.all_gather(in_proj, "fsdp", axis=0, tiled=True),
        lax.all_gather(conv_weight, "fsdp", axis=1, tiled=True),
        lax.all_gather(conv_bias, "fsdp", axis=0, tiled=True),
        lax.all_gather(x_proj, "fsdp", axis=0, tiled=True),
        lax.all_gather(dt_proj, "fsdp", axis=1, tiled=True),
        lax.all_gather(dt_bias, "fsdp", axis=0, tiled=True),
        lax.all_gather(a_log, "fsdp", axis=1, tiled=True),
        lax.all_gather(skip_scale, "fsdp", axis=0, tiled=True),
        lax.all_gather(out_proj, "fsdp", axis=0, tiled=True),
    )
    (
        gain_full,
        weight_in,
        conv_taps,
        conv_shift,
        weight_x,
        weight_dt,
        bias_dt,
        rate_log,
        skip_full,
        weight_out,
    ) = weights
    total_slots = fsdp_size * 2 * piece_len * ctx_size
    g_out = 2.0 * valid_rows * error_rows * (total_slots / count_total)
    d_out = g_out.astype(jnp.bfloat16)
    grad_out_w = rows_product(branch, d_out)
    d_branch = back_product(d_out, weight_out).reshape(2, piece_len, inner_width)
    d_ssm = d_branch * silu_gate
    d_gate = d_branch * ssm * silu_slope(gate_vals)
    grad_skip = jnp.sum(d_ssm * xs_vals, axis=(0, 1))
    dssm_blocks = arrange(d_ssm, block_len)

    def start_term(running, block_in):
        cum_blk, dssm_blk, output_blk = block_in
        weight_blk = jnp.exp(neg_rate * cum_blk[:, :, None, :])
        return (
            running
            + jnp.sum(weight_blk * dssm_blk[:, :, None, :] * output_blk[:, :, :, None], axis=0),
            None,
        )

    start_grad, _ = lax.scan(start_term, zero_state, (cumul_blocks, dssm_blocks, output_blocks))
    grads_all = lax.all_gather(start_grad[None], "ctx", axis=0, tiled=True)
    seq_grads = sequence_order(grads_all, pair_owner)

    def back_step(carry_now, item_in):
        grad_piece, decay_piece = item_in
        return (grad_piece + decay_piece * carry_now, carry_now)

    _, after_all = lax.scan(back_step, zero_state, (seq_grads, seq_decays), reverse=True)
    incoming = pick_own(after_all, own_pos)

    def backward_block(carry_pair, block_in):
        later, rate_sum = carry_pair
        state_in, step_blk, drive_blk, xs_blk, input_blk, output_blk, dssm_blk = block_in
        decays = jnp.exp(step_blk[:, :, None, :] * neg_rate)
        pushes = drive_blk[:, :, None, :] * input_blk[:, :, :, None]
        hidden = run_linear(decays, pushes, state_in, False)
        hidden_prev = jnp.concatenate([state_in[None], hidden[:-1]], axis=0)
        sources = output_blk[:, :, :, None] * dssm_blk[:, :, None, :]
        next_decays = jnp.concatenate([decays[1:], jnp.ones_like(decays[:1])], axis=0)
        adjoint = run_linear(next_decays, sources, later, True)
        d_output = jnp.sum(dssm_blk[:, :, None, :] * hidden, axis=3)
        d_input = jnp.sum(adjoint * drive_blk[:, :, None, :], axis=3)
        adj_input = jnp.sum(adjoint * input_blk[:, :, :, None], axis=2)
        decay_terms = adjoint * hidden_prev * decays
        d_step = xs_blk * adj_input + jnp.sum(decay_terms * neg_rate, axis=2)
        d_xs_part = step_blk * adj_input
        rate_sum = rate_sum + jnp.sum(decay_terms * step_blk[:, :, None, :], axis=0)
        return ((decays[0] * adjoint[0], rate_sum), (d_output, d_input, d_step, d_xs_part))

    (_, rate_grad), (d_out_blocks, d_in_blocks, d_step_blocks, d_xs_blocks) = lax.scan(
        backward_block,
        (incoming, zero_state),
        (
            block_starts,
            step_blocks,
            drive_blocks,
            arrange(xs_vals, block_len),
            input_blocks,
            output_blocks,
            dssm_blocks,
        ),
        reverse=True,
    )
    grad_rate = jnp.sum(rate_grad, axis=0) * neg_rate
    d_step_all = (restore(d_step_blocks) * valid[:, :, None]).reshape(row_count, inner_width)
    d_pre = d_step_all * jax.nn.sigmoid(pre_step)
    grad_bias_dt = jnp.sum(d_pre, axis=0)
    d_pre_low = d_pre.astype(jnp.bfloat16)
    grad_dt_w = rows_product(delta, d_pre_low)
    d_delta = back_product(d_pre_low, weight_dt)
    d_proj = jnp.concatenate(
        [
            d_delta,
            restore(d_in_blocks).reshape(row_count, state_dim),
            restore(d_out_blocks).reshape(row_count, state_dim),
        ],
        axis=1,
    ).astype(jnp.bfloat16)
    grad_x_w = rows_product(xs_rows, d_proj)
    d_xs_all = (
        skip_values * d_ssm
        + restore(d_xs_blocks)
        + back_product(d_proj, weight_x).reshape(2, piece_len, inner_width)
    )
    d_conv = d_xs_all * silu_slope(conv_out)
    grad_conv_b = jnp.sum(d_conv, axis=(0, 1))
    grad_conv_w = jnp.stack(
        [
            jnp.sum(d_conv * padded[:, offset : offset + piece_len], axis=(0, 1))
            for offset in range(tap_count)
        ]
    )
    d_padded = jnp.zeros((2, piece_len + tap_count - 1, inner_width), jnp.float32)
    for offset in range(tap_count):
        d_padded = d_padded.at[:, offset : offset + piece_len].add(tap_values[offset] * d_conv)
    heads = d_padded[:, : tap_count - 1]
    all_heads = lax.all_gather(heads[None].astype(jnp.bfloat16), "ctx", axis=0, tiled=True).astype(
        jnp.float32
    )
    from_next = jnp.stack([all_heads[upper_owner, 0], all_heads[lower_owner, 1]])
    from_next = jnp.where(has_after[:, None, None], from_next, jnp.zeros_like(from_next))
    d_x_in = d_padded[:, tap_count - 1 :]
    d_x_in = d_x_in.at[:, piece_len - (tap_count - 1) :].add(from_next)
    d_mixed = jnp.concatenate(
        [d_x_in.reshape(row_count, inner_width), d_gate.reshape(row_count, inner_width)], axis=1
    ).astype(jnp.bfloat16)
    grad_in_w = rows_product(normed, d_mixed)
    d_normed = back_product(d_mixed, weight_in)
    grad_gain = jnp.sum(d_normed * rows * inv_rms, axis=0)
    scaled = d_normed * gain_values
    cubed = inv_rms * inv_rms * inv_rms
    d_rows = inv_rms * scaled - rows * cubed * jnp.mean(scaled * rows, axis=1, keepdims=True)
    grad_tokens = (d_rows + g_out)[None]
    (
        part_gain,
        part_in,
        part_conv_w,
        part_conv_b,
        part_x,
        part_dt,
        part_bias,
        part_rate,
        part_skip,
        part_out,
    ) = (
        lax.psum_scatter(
            grad_gain.astype(jnp.bfloat16), "fsdp", scatter_dimension=0, tiled=True
        ).astype(jnp.float32),
        lax.psum_scatter(
            grad_in_w.astype(jnp.bfloat16), "fsdp", scatter_dimension=0, tiled=True
        ).astype(jnp.float32),
        lax.psum_scatter(
            grad_conv_w.astype(jnp.bfloat16), "fsdp", scatter_dimension=1, tiled=True
        ).astype(jnp.float32),
        lax.psum_scatter(
            grad_conv_b.astype(jnp.bfloat16), "fsdp", scatter_dimension=0, tiled=True
        ).astype(jnp.float32),
        lax.psum_scatter(
            grad_x_w.astype(jnp.bfloat16), "fsdp", scatter_dimension=0, tiled=True
        ).astype(jnp.float32),
        lax.psum_scatter(
            grad_dt_w.astype(jnp.bfloat16), "fsdp", scatter_dimension=1, tiled=True
        ).astype(jnp.float32),
        lax.psum_scatter(
            grad_bias_dt.astype(jnp.bfloat16), "fsdp", scatter_dimension=0, tiled=True
        ).astype(jnp.float32),
        lax.psum_scatter(
            grad_rate.astype(jnp.bfloat16), "fsdp", scatter_dimension=1, tiled=True
        ).astype(jnp.float32),
        lax.psum_scatter(
            grad_skip.astype(jnp.bfloat16), "fsdp", scatter_dimension=0, tiled=True
        ).astype(jnp.float32),
        lax.psum_scatter(
            grad_out_w.astype(jnp.bfloat16), "fsdp", scatter_dimension=0, tiled=True
        ).astype(jnp.float32),
    )
    (
        sum_gain,
        sum_in,
        sum_conv_w,
        sum_conv_b,
        sum_x,
        sum_dt,
        sum_bias,
        sum_rate,
        sum_skip,
        sum_out,
    ) = (
        lax.psum(part_gain.astype(jnp.bfloat16), "ctx").astype(jnp.float32),
        lax.psum(part_in.astype(jnp.bfloat16), "ctx").astype(jnp.float32),
        lax.psum(part_conv_w.astype(jnp.bfloat16), "ctx").astype(jnp.float32),
        lax.psum(part_conv_b.astype(jnp.bfloat16), "ctx").astype(jnp.float32),
        lax.psum(part_x.astype(jnp.bfloat16), "ctx").astype(jnp.float32),
        lax.psum(part_dt.astype(jnp.bfloat16), "ctx").astype(jnp.float32),
        lax.psum(part_bias.astype(jnp.bfloat16), "ctx").astype(jnp.float32),
        lax.psum(part_rate.astype(jnp.bfloat16), "ctx").astype(jnp.float32),
        lax.psum(part_skip.astype(jnp.bfloat16), "ctx").astype(jnp.float32),
        lax.psum(part_out.astype(jnp.bfloat16), "ctx").astype(jnp.float32),
    )
    return (
        block_out.astype(jnp.bfloat16)[None],
        loss,
        grad_tokens,
        sum_gain,
        sum_in,
        sum_conv_w,
        sum_conv_b,
        sum_x,
        sum_dt,
        sum_bias,
        sum_rate,
        sum_skip,
        sum_out,
    )


def solution(mesh):
    in_specs = (
        P("fsdp", "ctx", None),
        P("fsdp", "ctx", None),
        P("fsdp", None),
        P(),
        P("fsdp"),
        P("fsdp", None),
        P(None, "fsdp"),
        P("fsdp"),
        P("fsdp", None),
        P(None, "fsdp"),
        P("fsdp"),
        P(None, "fsdp"),
        P("fsdp"),
        P("fsdp", None),
    )
    out_specs = (
        P("fsdp", "ctx", None),
        P(),
        P("fsdp", "ctx", None),
        P("fsdp"),
        P("fsdp", None),
        P(None, "fsdp"),
        P("fsdp"),
        P("fsdp", None),
        P(None, "fsdp"),
        P("fsdp"),
        P(None, "fsdp"),
        P("fsdp"),
        P("fsdp", None),
    )
    return jax.shard_map(local, mesh=mesh, in_specs=in_specs, out_specs=out_specs, check_vma=False)
```

profile of v0, /device:TPU:0, one launch (start us, length us, event | category | flops | bytes accessed | tf_op | source)
XLA Modules:
  0.0 2194.5 jit_solution(7914026505587972116)
XLA Ops:
  82.4 30.8 %all-gather = bf16[16,3,2048]{2,1,0:T(4,128)(2,1)S(1)} all-gather(bf16[2,3,2048]{2,1,0:T(4,128)(2,1)S(1)} %slice.1627), channel_id=2, replica_groups=mesh['ctx'=8,'fsdp'=4] {'ctx'}, dimensions={0}, use_global_device_ids=true | all-gather | bytes 221184 | tf_op jit(solution)/shard_map/all_gather | solution.py:127
  146.3 13.5 copy_bitcast_fusion.1
  159.8 64.8 %while.97 = (s32[]{:T(128)}, f32[2,16,2048]{2,1,0:T(8,128)S(1)}, f32[16,2048]{1,0:T(8,128)S(1)}, f32[2,1,2048]{2,0,1:T(2,128)}, f32[8,32,2,2048]{3,2,1,0:T(2,128...) while((s32[]{:T(128)}, f32[2,16,2048]{2,1,0:T(8,128)S(1)}, ...), condition=%wide.region_6.7_spmd.clone, body=%wide.region_4.6_spmd.clone.sunk | while | flops 8585219 | bytes 4362355 | solution.py:167
  242.9 16.0 copy_bitcast_fusion
  284.0 15.5 while.98
  306.3 388.8 %while.96 = (s32[]{:T(128)}, f32[2,16,2048]{2,1,0:T(8,128)S(1)}, f32[8,2,16,2048]{3,2,1,0:T(8,128)}, f32[8,32,2,2048]{3,2,1,0:T(2,128)}, f32[8,32,2,2048]{3,2,1,...) while((s32[]{:T(128)}, f32[2,16,2048]{2,1,0:T(8,128)S(1)}, ...), condition=%wide.region_11.12_spmd, body=%wide.region_9.11_spmd.sunk | while | flops 14548993 | bytes 143549600 | solution.py:194
  713.3 39.4 %all-reduce.7 = (f32[]{:T(128)}, f32[]{:T(128)}) all-reduce(f32[]{:T(128)} %get-tuple-element.1200, f32[]{:T(128)} %get-tuple-element.1191), channel_id=1, replica_groups=mesh['ctx'=8,'fsdp'=4] {'ctx','fsdp'}, use_global_device_ids=true, to_apply=%region_13.14 | all-reduce | flops 2 | bytes 16 | tf_op jit(solution)/shard_map/psum | solution.py:205
  768.6 26.9 %while.99 = (s32[]{:T(128)}, f32[2,16,2048]{2,1,0:T(8,128)S(1)}, f32[16,2048]{1,0:T(8,128)S(1)}, f32[8,32,2,2048]{3,2,1,0:T(2,128)}, f32[8,32,2,2048]{3,2,1,0:T(...) while((s32[]{:T(128)}, f32[2,16,2048]{2,1,0:T(8,128)S(1)}, ...), condition=%wide.region_18.19_spmd.clone, body=%wide.region_16.18_spmd.clone.sunk | while | flops 8454147 | bytes 4345959 | solution.py:250
  796.3 51.1 %all-gather.22.cloned.1.call-done = f32[16,16,2048]{2,1,0:T(8,128)} async-done(((f32[2,16,2048]{2,1,0:T(8,128)}), f32[16,16,2048]{2,1,0:T(8,128)}) %all-gather.22.cloned.1.call-update) | async-done | bytes 2097168 | tf_op jit(solution)/shard_map/all_gather | solution.py:251
  857.0 14.8 while.100
  882.5 907.5 %while.101 = (s32[]{:T(128)}, f32[2,16,2048]{2,1,0:T(8,128)S(1)}, f32[2,16,2048]{2,1,0:T(8,128)}, bf16[8,32,2,16]{3,2,1,0:T(2,128)(2,1)}, bf16[8,32,2,16]{3,2,1,...) while((s32[]{:T(128)}, f32[2,16,2048]{2,1,0:T(8,128)S(1)}, ...), condition=%wide.region_27.28_spmd.clone, body=%wide.region_21.27_spmd.clone.sunk | while | flops 44169216 | bytes 254087552 | solution.py:280
  1089.8 10.2 multiply_reduce_fusion.21
  1316.6 10.2 multiply_reduce_fusion.21
  1656.7 10.2 multiply_reduce_fusion.21
  1770.1 10.2 multiply_reduce_fusion.21
  1838.6 12.3 scatter-add.15
  1857.9 12.5 scatter-add.16
  1871.3 30.8 %all-gather.3 = bf16[16,3,2048]{2,1,0:T(4,128)(2,1)S(1)} all-gather(bf16[2,3,2048]{2,1,0:T(4,128)(2,1)S(1)} %slice.2368), channel_id=5, replica_groups=mesh['ctx'=8,'fsdp'=4] {'ctx'}, dimensions={0}, use_global_device_ids=true | all-gather | bytes 221184 | tf_op jit(solution)/shard_map/all_gather | solution.py:327
  1923.8 67.7 %reduce-scatter.9.cloned.1.call-done = bf16[256,4096]{1,0:T(8,128)(2,1)} async-done(((bf16[1024,4096]{1,0:T(8,128)(2,1)}), bf16[256,4096]{1,0:T(8,128)(2,1)}) %reduce-scatter.9.cloned.1.call-update) | async-done | bytes 2097168 | tf_op jit(solution)/shard_map/reduce_scatter | solution.py:359
  1994.8 10.9 fusion.119
  2005.8 10.6 all-reduce.10
  2022.1 16.2 reduce-scatter.15.cloned.1.call-done
  2038.3 38.9 %all-reduce.8 = (bf16[256]{0:T(256)(128)(2,1)S(1)}, bf16[4,512]{1,0:T(4,128)(2,1)S(1)}, bf16[512]{0:T(512)(128)(2,1)S(1)}, bf16[512]{0:T(512)(128)(2,1)S(1)}, bf...) all-reduce(bf16[256]{0:T(256)(128)(2,1)S(1)} %dynamic-slice.40, ...), channel_id=1, replica_groups=mesh['ctx'=8,'fsdp'=4] {'ctx'}, use_global_device_ids=true, to_apply=%region_31.32 | all-reduce | flops 12032 | bytes 48128 | tf_op jit(solution)/shard_map/psum | solution.py:399
  2080.8 97.3 %all-reduce.13.cloned.1.call-done = (bf16[256,4096]{1,0:T(8,128)(2,1)}, bf16[512,96]{0,1:T(8,128)(2,1)}, bf16[64,512]{1,0:T(8,128)(2,1)}, bf16[512,1024]{1,0:T(8,128)(2,1)}) async-done(((bf16[256,4096]{1,0:T(8,128)(2,1)}, bf16[512,96]{0,1:T(8,128)(2,1)}, bf16[64,512]{1,0:T(8,128)(2,1)}, bf16[512,1024]{1,0:T(8,128)(2,1)}), (bf16[256,4096]{1,0:T(8,128)(2,1)}, bf16[512,96]{0,1:T(8,128)(2,1)}, ...) | async-done | bytes 3309584 | tf_op jit(solution)/shard_map/psum | solution.py:400
  (1386 shorter events, 1672.7 us)
Async XLA Ops:
  7.2 67.5 %all-gather.14.cloned.1.call-start = ((), (), s32[]{:S(2)}) async-start(), calls=%async_computation.6 | async-start | bytes 10485760 | tf_op jit(solution)/shard_map/all_gather | solution.py:86
  7.9 250.9 %all-gather.16.cloned.1.call-start = ((), (), s32[]{:S(2)}) async-start(), calls=%async_computation.7 | async-start | bytes 1179648 | tf_op jit(solution)/shard_map/all_gather | solution.py:173
  23.6 58.4 %copy-start.63 = (f32[4,1,256]{2,1,0:T(1,128)}, f32[4,1,256]{2,1,0:T(1,128)S(1)}, u32[]{:S(2)}) copy-start(f32[4,1,256]{2,1,0:T(1,128)S(1)} %convert_element_type.242) | copy-start | bytes 12292
  35.6 84.2 %copy-start.60 = (f32[4,1,512]{2,1,0:T(1,128)}, f32[4,1,512]{2,1,0:T(1,128)S(1)}, u32[]{:S(2)}) copy-start(f32[4,1,512]{2,1,0:T(1,128)S(1)} %convert_element_type.244) | copy-start | bytes 24580
  56.0 63.8 %copy-start.33 = (bf16[64,2048]{1,0:T(8,128)(2,1)}, bf16[64,2048]{1,0:T(8,128)(2,1)S(1)}, u32[]{:S(2)}) copy-start(bf16[64,2048]{1,0:T(8,128)(2,1)S(1)} %all_gather.56) | copy-start | bytes 786436
  66.1 52.2 %copy-start.29 = (bf16[2048,96]{0,1:T(8,128)(2,1)}, bf16[2048,96]{0,1:T(8,128)(2,1)S(1)}, u32[]{:S(2)}) copy-start(bf16[2048,96]{0,1:T(8,128)(2,1)S(1)} %all_gather.55) | copy-start | bytes 1179652
  69.7 44.3 %copy-start.49 = (f32[1,2048]{1,0:T(1,128)}, f32[1,2048]{1,0:T(1,128)S(1)}, u32[]{:S(2)}) copy-start(f32[1,2048]{1,0:T(1,128)S(1)} %get-tuple-element.1184) | copy-start | bytes 24580
  118.3 581.4 %copy-start.6 = (bf16[2,256,2048]{2,1,0:T(8,128)(2,1)}, bf16[2,256,2048]{2,1,0:T(8,128)(2,1)S(1)}, u32[]{:S(2)}) copy-start(bf16[2,256,2048]{2,1,0:T(8,128)(2,1)S(1)} %get-tuple-element.1104) | copy-start | bytes 6291460
  143.1 125.0 %all-gather.20.cloned.1.call-start = ((), (), s32[]{:S(2)}) async-start(), calls=%async_computation.14 | async-start | bytes 1179648 | tf_op jit(solution)/shard_map/all_gather | solution.py:170
  225.3 481.4 %all-gather.18.cloned.1.call-start = ((), (), s32[]{:S(2)}) async-start(), calls=%async_computation.8 | async-start | bytes 5242880 | tf_op jit(solution)/shard_map/all_gather | solution.py:94
  225.9 621.5 %all-gather.22.cloned.1.call-start = ((), (), s32[]{:S(2)}) async-start(), calls=%async_computation.15 | async-start | bytes 2359296 | tf_op jit(solution)/shard_map/all_gather | solution.py:251
  237.0 462.7 %copy-start.57 = (f32[4,1,512]{2,1,0:T(1,128)}, f32[4,1,512]{2,1,0:T(1,128)S(1)}, u32[]{:S(2)}) copy-start(f32[4,1,512]{2,1,0:T(1,128)S(1)} %convert_element_type.245) | copy-start | bytes 24580
  237.7 469.1 %copy-start.69 = (f32[1,2,2,128]{3,1,2,0:T(2,128)}, f32[1,2,2,128]{3,1,2,0:T(2,128)S(1)}, u32[]{:S(2)}) copy-start(f32[1,2,2,128]{3,1,2,0:T(2,128)S(1)} %copy.134) | copy-start | bytes 6148
  237.7 515.8 %copy-start.61 = (f32[1,2,2,128]{3,1,2,0:T(2,128)}, f32[1,2,2,128]{3,1,2,0:T(2,128)S(1)}, u32[]{:S(2)}) copy-start(f32[1,2,2,128]{3,1,2,0:T(2,128)S(1)} %copy.135) | copy-start | bytes 6148
  713.3 46.8 %copy-start.24 = (f32[512,1024]{1,0:T(8,128)}, f32[512,1024]{1,0:T(8,128)S(1)}, u32[]{:S(2)}) copy-start(f32[512,1024]{1,0:T(8,128)S(1)} %get-tuple-element.1201) | copy-start | bytes 6291460
  796.2 1127.5 %reduce-scatter.13.cloned.1.call-start = ((), (), s32[]{:S(2)}) async-start(), calls=%async_computation.11 | async-start | bytes 327680 | tf_op jit(solution)/shard_map/reduce_scatter | solution.py:371
  1806.1 117.7 %reduce-scatter.11.cloned.1.call-start = ((), (), s32[]{:S(2)}) async-start(), calls=%async_computation.10 | async-start | bytes 491520 | tf_op jit(solution)/shard_map/reduce_scatter | solution.py:368
  1810.4 113.4 %reduce-scatter.17.cloned.1.call-start = ((), (), s32[]{:S(2)}) async-start(), calls=%async_computation.13 | async-start | bytes 5242880 | tf_op jit(solution)/shard_map/reduce_scatter | solution.py:383
  1816.5 175.1 %reduce-scatter.9.cloned.1.call-start = ((), (), s32[]{:S(2)}) async-start(), calls=%async_computation.9 | async-start | bytes 10485760 | tf_op jit(solution)/shard_map/reduce_scatter | solution.py:359
  1850.9 51.3 %copy-start.52 = (f32[1,2048]{1,0:T(1,128)S(1)}, f32[1,2048]{1,0:T(1,128)}, u32[]{:S(2)}) copy-start(f32[1,2048]{1,0:T(1,128)} %copy-done.51) | copy-start | bytes 24580
  1921.5 70.1 %copy-start.71 = (u32[32]{0:T(128)S(1)}, u32[32]{0:T(128)}, u32[]{:S(2)}) copy-start(u32[32]{0:T(128)} %constant.433) | copy-start | bytes 388
  1921.5 99.6 %reduce-scatter.19.cloned.1.call-start = ((), (), s32[]{:S(2)}) async-start(), calls=%async_computation.16 | async-start | bytes 655360
  1922.7 115.6 %reduce-scatter.15.cloned.1.call-start = ((), (), s32[]{:S(2)}) async-start(), calls=%async_computation.12 | async-start | bytes 81920 | tf_op jit(solution)/shard_map/reduce_scatter | solution.py:377
  1923.5 254.5 %all-reduce.13.cloned.1.call-start = ((), (), s32[]{:S(2)}) async-start(), calls=%async_computation.17 | async-start | bytes 6619136 | tf_op jit(solution)/shard_map/psum | solution.py:400
  (128 other events, 1098.9 us)
Sparse Core Ops, SparseCore 0:
  9.6 65.0 all-gather.13
  143.2 40.0 all-gather.15
  225.4 40.0 all-gather.19
  267.0 33.2 all-gather.17
  796.3 50.9 all-gather.21
  1806.2 18.5 reduce-scatter.12
  1828.0 20.8 reduce-scatter.10
  1851.5 44.5 reduce-scatter.16
  1921.6 69.9 reduce-scatter.8
  1994.0 21.7 reduce-scatter.18
  2018.8 19.4 reduce-scatter.14
  2042.6 135.3 all-reduce.12
where the time goes:
time: 2220 us; the launch traced here: 2190 us
  other arithmetic  1320 us (59%)
  local copies, waits for them, and re-layouts  344 us (15%)
  waiting for transfers between devices  239 us (11%)
  blocking collectives  201 us (9%)
  matrix products  54.4 us (2%)
  between operations  29.6 us (1%)
    while x504, other arithmetic  826 us
    while x264, local copies, waits for them, and re-layouts  112 us
    psum x1, waiting for transfers between devices, local(): lax.psum(part_in.astype(jnp.bfloat16), 'ctx').astype(jnp.float32)  97.3 us
    reduce_sum x8, other arithmetic, backward_block(): d_step = xs_blk * adj_input + jnp.sum(decay_terms * neg_rate, axis=2)  81.5 us
    reduce_scatter x1, waiting for transfers between devices, local(): lax.psum_scatter(grad_in_w.astype(jnp.bfloat16), 'fsdp', scatter_dimensio...  67.7 us
    all_gather x1, waiting for transfers between devices, local(): grads_all = lax.all_gather(start_grad[None], 'ctx', axis=0, tiled=True)  51.1 us
  transfers between devices with their start and end apart: 12, of which 5 were waited for; matrix products, arithmetic and copies ran while one was open for 29% of the time, Pallas kernels for 0%

commit v1 on v0

v1 whole, which is shorter than its diff:
```python
import functools

import jax
import jax.numpy as jnp
from jax import lax
from jax.experimental import pallas as pl
from jax.experimental.pallas import tpu as pltpu
from jax.sharding import PartitionSpec as P

EPSILON = 1e-05
LOG2E = 1.4426950408889634
F32 = jnp.float32
BF16 = jnp.bfloat16
LANES = 128
HALO = 16
HEAD = 16
VMEM_LIMIT = 60 * 1024 * 1024


def swap(values, axis, bit):
    size = lax.axis_size(axis)
    return lax.ppermute(values, axis, [(i, i ^ bit) for i in range(size)])


def after(values, earlier):
    return lax.optimization_barrier((values, earlier))[0]


def bits_of(size):
    return [1 << k for k in range(size.bit_length() - 1)]


def gather_fsdp(values):
    blocks = {0: values}
    for bit in reversed(bits_of(lax.axis_size("fsdp"))):
        for r in sorted(blocks):
            blocks[r | bit] = swap(blocks[r], "fsdp", bit)
    return [blocks[r] for r in range(len(blocks))]


def gather_ctx(values):
    size = lax.axis_size("ctx")
    blocks = {0: values}
    for j in range(2, size, 2):
        blocks[j] = swap(values, "ctx", j)
    for j in range(0, size, 2):
        blocks[j | 1] = swap(blocks[j], "ctx", 1)
    return [blocks[j] for j in range(size)]


def total(values, axes):
    for axis in axes:
        for bit in bits_of(lax.axis_size(axis)):
            values = values + swap(values, axis, bit)
    return values


def joined(kept, received):
    return (kept.astype(F32) + received.astype(F32)).astype(BF16)


def reduce_shard(keep, send, ctx_first):
    fsdp_steps = [("fsdp", bit) for bit in bits_of(lax.axis_size("fsdp"))[1:]]
    ctx_steps = [("ctx", bit) for bit in bits_of(lax.axis_size("ctx"))]
    steps = ctx_steps + fsdp_steps if ctx_first else fsdp_steps + ctx_steps
    values = joined(keep, swap(send, "fsdp", 1))
    me = lax.axis_index("ctx")
    for axis, bit in steps:
        if axis == "fsdp":
            values = joined(values[0::2], swap(values[1::2], axis, bit))
        else:
            half = values.shape[1] // 2
            up = (me & bit) != 0
            low, high = values[:, :half], values[:, half:]
            values = joined(
                jnp.where(up, high, low), swap(jnp.where(up, low, high), axis, bit)
            )
    for axis, bit in reversed(ctx_steps):
        other = swap(values, axis, bit)
        up = (me & bit) != 0
        values = jnp.concatenate(
            [jnp.where(up, other, values), jnp.where(up, values, other)], axis=1
        )
    return values[0]


def dot(left, right):
    return jnp.dot(left, right, preferred_element_type=F32)


def rows_dot(left, right):
    return lax.dot_general(left, right, (((0,), (0,)), ((), ())), preferred_element_type=F32)


def back_dot(left, right):
    return lax.dot_general(left, right, (((1,), (1,)), ((), ())), preferred_element_type=F32)


def sigmoid(values):
    return 1.0 / (1.0 + jnp.exp(-values))


def softplus(values):
    small = jnp.exp(-jnp.abs(values))
    grown = 1.0 + small
    part = jnp.where(grown == 1.0, small, jnp.log(grown) * (small / jnp.maximum(grown - 1.0, 1e-30)))
    return jnp.maximum(values, 0.0) + part


def tile_cols(j):
    return slice(j * LANES, (j + 1) * LANES)


def input_kernel(scal, normed_ref, *refs, count, piece):
    weights, (s_ref, x_ref, conv_ref, xs_ref, proj_ref) = refs[:count], refs[count:]
    depth = weights[0].shape[0]
    width = weights[0].shape[1]
    mixed = dot(normed_ref[:, 0:depth], weights[0][...])
    for r in range(1, count):
        mixed = mixed + dot(normed_ref[:, r * depth : (r + 1) * depth], weights[r][...])
    x_low = mixed.astype(BF16).reshape(2, HALO + piece, width)
    x_ref[...] = x_low
    x = x_low.astype(F32)
    head = s_ref[0:HEAD, :].astype(F32)
    conv = head[4:5] + x[:, HALO - 3 : HALO - 3 + piece] * head[0:1]
    for k in range(1, 4):
        conv = conv + x[:, HALO - 3 + k : HALO - 3 + k + piece] * head[k : k + 1]
    conv_ref[...] = conv
    xs = (conv * sigmoid(conv)).astype(BF16)
    xs_ref[...] = xs
    part = back_dot(xs.reshape(2 * piece, width), s_ref[96:192, :])

    @pl.when(pl.program_id(0) == 0)
    def first():
        proj_ref[...] = part

    @pl.when(pl.program_id(0) > 0)
    def later():
        proj_ref[...] += part


def gate_kernel(scal, normed_ref, *refs, count, piece):
    weights, (gate_ref,) = refs[:count], refs[count:]
    depth = weights[0].shape[0]
    width = weights[0].shape[1]
    own = jnp.concatenate(
        [normed_ref[HALO : HALO + piece], normed_ref[2 * HALO + piece : 2 * HALO + 2 * piece]], axis=0
    )
    gate = dot(own[:, 0:depth], weights[0][...])
    for r in range(1, count):
        gate = gate + dot(own[:, r * depth : (r + 1) * depth], weights[r][...])
    gate_ref[...] = gate.reshape(2, piece, width)


def end_kernel(
    scal, proj_ref, s_ref, xs_ref, b_ref, step_ref, end_ref, log_ref, drive_ref, *, tiles, groups, rank
):
    piece = groups * 8
    width = tiles * LANES
    states = b_ref.shape[2]
    head = s_ref[0:HEAD, :].astype(F32)
    delta = proj_ref[:, 0:rank].astype(BF16)
    pre = dot(delta, s_ref[HEAD : HEAD + rank, :]) + head[5:6]
    row = lax.broadcasted_iota(jnp.int32, (piece, width), 0)
    for h in range(2):
        step = softplus(pre[h * piece : (h + 1) * piece])
        step = jnp.where(row < scal[1 + h], step, 0.0)
        log_ref[h : h + 1, :] = jnp.sum(step, axis=0, keepdims=True)
        step_ref[h] = step.reshape(groups, 8, width)
        drive_ref[h] = (step * xs_ref[h].astype(F32)).reshape(groups, 8, width)
    rate2 = -jnp.exp(s_ref[80 : 80 + states, :].astype(F32)) * LOG2E
    rates = [rate2[:, tile_cols(j)] for j in range(tiles)]

    def body(t, held):
        held = list(held)
        for s in range(8):
            for h in range(2):
                b = b_ref[h, t * 8 + s]
                for j in range(tiles):
                    step = step_ref[h, t, s : s + 1, tile_cols(j)]
                    drive = drive_ref[h, t, s : s + 1, tile_cols(j)]
                    k = h * tiles + j
                    held[k] = jnp.exp2(step * rates[j]) * held[k] + drive * b
        return tuple(held)

    zero = jnp.zeros((states, LANES), F32)
    held = lax.fori_loop(0, groups, body, (zero,) * (2 * tiles))
    for h in range(2):
        for j in range(tiles):
            end_ref[h * states : (h + 1) * states, tile_cols(j)] = held[h * tiles + j].astype(BF16)


def carried(ends, log_ref, rate2, h, ctx, states, cols):
    value = jnp.zeros((states, LANES), F32)
    for j in range(1, ctx):
        decay = jnp.exp2(rate2 * log_ref[h * ctx + j : h * ctx + j + 1, cols])
        value = value + decay * ends[j - 1][h * states : (h + 1) * states, cols].astype(F32)
    return value


def forward_kernel(scal, *refs, tiles, groups, ctx, features):
    ends = refs[: ctx - 1]
    (
        log_ref, scale_ref, s_ref, step_ref, xs_ref, gate_ref, b_ref, c_ref, weight_ref, tokens_ref, teacher_ref,
        ssm_ref, branch_ref, hidden_ref, start_ref, out_ref, gout_ref, dout_ref, square_ref,
        drive_ref, read_ref, acc_ref,
    ) = refs[ctx - 1 :]
    piece = groups * 8
    width = tiles * LANES
    states = b_ref.shape[2]
    i = pl.program_id(0)
    head = s_ref[0:HEAD, :].astype(F32)
    for h in range(2):
        drive_ref[h] = step_ref[h] * xs_ref[h].astype(F32).reshape(groups, 8, width)
    rate2 = -jnp.exp(s_ref[80 : 80 + states, :].astype(F32)) * LOG2E
    rates = [rate2[:, tile_cols(j)] for j in range(tiles)]
    held = []
    for h in range(2):
        for j in range(tiles):
            held.append(carried(ends, log_ref, rates[j], h, ctx, states, tile_cols(j)))
            start_ref[h, :, tile_cols(j)] = held[-1]

    def body(t, held):
        held = list(held)
        for s in range(8):
            p = t * 8 + s
            for h in range(2):
                b = b_ref[h, p]
                c = c_ref[h, p]
                for j in range(tiles):
                    step = step_ref[h, t, s : s + 1, tile_cols(j)]
                    drive = drive_ref[h, t, s : s + 1, tile_cols(j)]
                    k = h * tiles + j
                    now = jnp.exp2(step * rates[j]) * held[k] + drive * b
                    held[k] = now
                    hidden_ref[j, h, p] = now.astype(BF16)
                    read_ref[h, t, s : s + 1, tile_cols(j)] = jnp.sum(now * c, axis=0, keepdims=True)
        return tuple(held)

    lax.fori_loop(0, groups, body, tuple(held))
    branches = []
    for h in range(2):
        ssm = read_ref[h].reshape(piece, width) + head[6:7] * xs_ref[h].astype(F32)
        ssm_ref[h] = ssm
        gate = gate_ref[h]
        branches.append((ssm * (gate * sigmoid(gate))).astype(BF16))
        branch_ref[h] = branches[-1]
    part = dot(jnp.concatenate(branches, axis=0), weight_ref[...])

    @pl.when(i == 0)
    def first():
        acc_ref[...] = part

    @pl.when(i > 0)
    def later():
        acc_ref[...] += part

    @pl.when(i == pl.num_programs(0) - 1)
    def last():
        row = lax.broadcasted_iota(jnp.int32, (piece, features), 0)
        square = jnp.zeros((8, features), F32)
        for h in range(2):
            rows = slice(h * piece, (h + 1) * piece)
            block_out = tokens_ref[rows, :].astype(F32) + acc_ref[rows, :]
            out_ref[rows, :] = block_out.astype(BF16)
            error = jnp.where(row < scal[1 + h], block_out - teacher_ref[rows, :].astype(F32), 0.0)
            square = square + jnp.sum((error * error).reshape(groups, 8, features), axis=0)
            g_out = error * (2.0 * scale_ref[0, 0])
            gout_ref[rows, :] = g_out
            dout_ref[rows, :] = g_out.astype(BF16)
        square_ref[...] = square


def first_grad_kernel(
    scal, dout_ref, weight_ref, s_ref, step_ref, xs_ref, gate_ref, ssm_ref, c_ref,
    dssm_ref, dgate_ref, skip_ref, grad_ref, *, tiles, groups
):
    piece = groups * 8
    width = tiles * LANES
    states = c_ref.shape[2]
    d_branch = back_dot(dout_ref[...], weight_ref[...])
    skip = jnp.zeros((1, width), F32)
    for h in range(2):
        grad = d_branch[h * piece : (h + 1) * piece]
        gate = gate_ref[h]
        sig = sigmoid(gate)
        d_ssm = grad * (gate * sig)
        dgate_ref[h] = (grad * ssm_ref[h] * (sig * (1.0 + gate * (1.0 - sig)))).astype(BF16)
        skip = skip + jnp.sum(d_ssm * xs_ref[h].astype(F32), axis=0, keepdims=True)
        dssm_ref[h] = d_ssm.reshape(groups, 8, width)
    skip_ref[...] = skip
    rate2 = -jnp.exp(s_ref[80 : 80 + states, :].astype(F32)) * LOG2E
    rates = [rate2[:, tile_cols(j)] for j in range(tiles)]

    def body(i, held):
        held = list(held)
        t = groups - 1 - i
        for s in range(7, -1, -1):
            for h in range(2):
                c = c_ref[h, t * 8 + s]
                for j in range(tiles):
                    step = step_ref[h, t, s : s + 1, tile_cols(j)]
                    dssm = dssm_ref[h, t, s : s + 1, tile_cols(j)]
                    k = h * tiles + j
                    held[k] = jnp.exp2(step * rates[j]) * (held[k] + dssm * c)
        return tuple(held)

    zero = jnp.zeros((states, LANES), F32)
    held = lax.fori_loop(0, groups, body, (zero,) * (2 * tiles))
    for h in range(2):
        for j in range(tiles):
            grad_ref[h * states : (h + 1) * states, tile_cols(j)] = held[h * tiles + j].astype(BF16)


def out_grad_kernel(even_ref, odd_ref, dout_ref, keep_ref, send_ref):
    keep_ref[0] = rows_dot(even_ref[...], dout_ref[...]).astype(BF16)
    send_ref[0] = rows_dot(odd_ref[...], dout_ref[...]).astype(BF16)


def gate_grad_kernel(scal, normed_ref, dgate_ref, *refs, count, piece):
    weights, (keep_ref, send_ref, dnormed_ref) = refs[:count], refs[count:]
    depth = weights[0].shape[0]
    width = weights[0].shape[1]
    own = jnp.concatenate(
        [normed_ref[HALO : HALO + piece], normed_ref[2 * HALO + piece : 2 * HALO + 2 * piece]], axis=0
    )
    d_gate = dgate_ref[...].reshape(2 * piece, width)

    @pl.when(pl.program_id(0) == 0)
    def clear():
        dnormed_ref[...] = jnp.zeros_like(dnormed_ref)

    for r in range(count):
        cols = slice(r * depth, (r + 1) * depth)
        target = send_ref if r % 2 else keep_ref
        target[r // 2] = rows_dot(own[:, cols], d_gate).astype(BF16)
        dnormed_ref[:, cols] += back_dot(d_gate, weights[r][...])


def backward_kernel(scal, *refs, tiles, groups, ctx, rank):
    grads = refs[: ctx - 1]
    (
        log_ref, proj_ref, s_ref, step_ref, xs_ref, b_ref, c_ref, start_ref, dssm_ref, hidden_ref,
        dxs_ref, small_ref, ddelta_ref, db_ref, dc_ref,
        drive_ref, adj_ref, dstep_ref,
    ) = refs[ctx - 1 :]
    piece = groups * 8
    width = tiles * LANES
    states = b_ref.shape[2]
    i = pl.program_id(0)
    head = s_ref[0:HEAD, :].astype(F32)
    for h in range(2):
        drive_ref[h] = step_ref[h] * xs_ref[h].astype(F32).reshape(groups, 8, width)

    @pl.when(i == 0)
    def clear():
        db_ref[...] = jnp.zeros_like(db_ref)
        dc_ref[...] = jnp.zeros_like(dc_ref)
        ddelta_ref[...] = jnp.zeros_like(ddelta_ref)

    rate = -jnp.exp(s_ref[80 : 80 + states, :].astype(F32))
    rates = [rate[:, tile_cols(j)] for j in range(tiles)]
    rates2 = [values * LOG2E for values in rates]

    def one(t, s, p, first, later, sums):
        for h in range(2):
            b = b_ref[h, p]
            c = c_ref[h, p]
            db = dc = None
            for j in range(tiles):
                cols = tile_cols(j)
                step = step_ref[h, t, s : s + 1, cols]
                drive = drive_ref[h, t, s : s + 1, cols]
                dssm = dssm_ref[h, t, s : s + 1, cols]
                k = h * tiles + j
                hidden = hidden_ref[j, h, p].astype(F32)
                before = start_ref[h, :, cols] if first else hidden_ref[j, h, p - 1].astype(F32)
                adjoint = dssm * c + later[k]
                later[k] = jnp.exp2(step * rates2[j]) * adjoint
                term = later[k] * before
                sums[j] = sums[j] + term * step
                dstep_ref[h, t, s : s + 1, cols] = jnp.sum(term * rates[j], axis=0, keepdims=True)
                adj_ref[h, t, s : s + 1, cols] = jnp.sum(adjoint * b, axis=0, keepdims=True)
                db = adjoint * drive if db is None else db + adjoint * drive
                dc = dssm * hidden if dc is None else dc + dssm * hidden
            db_ref[h, p] += db
            dc_ref[h, p] += dc

    def body(k, both):
        later, sums = list(both[: 2 * tiles]), list(both[2 * tiles :])
        t = groups - 1 - k
        for s in range(7, -1, -1):
            one(t, s, t * 8 + s, False, later, sums)
        return tuple(later + sums)

    later = tuple(
        carried(grads, log_ref, rates2[j], h, ctx, states, tile_cols(j))
        for h in range(2)
        for j in range(tiles)
    )
    zero = jnp.zeros((states, LANES), F32)
    both = lax.fori_loop(0, groups - 1, body, later + (zero,) * tiles)
    later, sums = list(both[: 2 * tiles]), list(both[2 * tiles :])
    for s in range(7, -1, -1):
        one(0, s, s, s == 0, later, sums)
    for j in range(tiles):
        small_ref[rank : rank + states, tile_cols(j)] = sums[j] * rates[j]
    delta = proj_ref[:, 0:rank].astype(BF16)
    pre = dot(delta, s_ref[HEAD : HEAD + rank, :]) + head[5:6]
    row = lax.broadcasted_iota(jnp.int32, (piece, width), 0)
    lows = []
    bias = jnp.zeros((1, width), F32)
    for h in range(2):
        xs = xs_ref[h].astype(F32)
        adj = adj_ref[h].reshape(piece, width)
        d_step = xs * adj + dstep_ref[h].reshape(piece, width)
        d_pre = jnp.where(row < scal[1 + h], d_step * sigmoid(pre[h * piece : (h + 1) * piece]), 0.0)
        bias = bias + jnp.sum(d_pre, axis=0, keepdims=True)
        lows.append(d_pre.astype(BF16))
        dxs_ref[h] = head[6:7] * dssm_ref[h].reshape(piece, width) + step_ref[h].reshape(piece, width) * adj
    small_ref[rank + states : rank + states + 8, :] = jnp.broadcast_to(bias, (8, width))
    low = jnp.concatenate(lows, axis=0)
    small_ref[0:rank, :] = rows_dot(delta, low)
    ddelta_ref[...] += back_dot(low, s_ref[HEAD : HEAD + rank, :])


def tail_kernel(
    scal, dproj_ref, s_ref, dxs_ref, conv_ref, x_ref, xs_ref, normed_ref, *refs, count, piece
):
    weights, (small_ref, keep_ref, send_ref, dnormed_ref, pad_ref) = refs[:count], refs[count:]
    depth = weights[0].shape[0]
    width = weights[0].shape[1]
    ext = HALO + piece

    @pl.when(pl.program_id(0) == 0)
    def clear():
        dnormed_ref[...] = jnp.zeros_like(dnormed_ref)
        for h in range(2):
            pad_ref[h, 0:HALO, :] = jnp.zeros((HALO, width), F32)
            pad_ref[h, ext : ext + 8, :] = jnp.zeros((8, width), F32)

    head = s_ref[0:HEAD, :].astype(F32)
    small_ref[8:104, :] = rows_dot(dproj_ref[...], xs_ref[...].reshape(2 * piece, width))
    d_xs = dot(dproj_ref[...], s_ref[96:192, :])
    taps = [jnp.zeros((1, width), F32) for _ in range(5)]
    lows = []
    for h in range(2):
        conv = conv_ref[h]
        sig = sigmoid(conv)
        d_conv = (dxs_ref[h] + d_xs[h * piece : (h + 1) * piece]) * (sig * (1.0 + conv * (1.0 - sig)))
        pad_ref[h, HALO:ext, :] = d_conv
        x = x_ref[h].astype(F32)
        for k in range(4):
            rows = slice(HALO - 3 + k, HALO - 3 + k + piece)
            taps[k] = taps[k] + jnp.sum(d_conv * x[rows], axis=0, keepdims=True)
        taps[4] = taps[4] + jnp.sum(d_conv, axis=0, keepdims=True)
        d_x = head[3:4] * pad_ref[h, 0:ext, :]
        for k in range(3):
            d_x = d_x + head[k : k + 1] * pad_ref[h, 3 - k : 3 - k + ext, :]
        lows.append(d_x.astype(BF16))
    small_ref[0:8, :] = jnp.concatenate(taps + [jnp.zeros((3, width), F32)], axis=0)
    low = jnp.concatenate(lows, axis=0)
    for r in range(count):
        cols = slice(r * depth, (r + 1) * depth)
        target = send_ref if r % 2 else keep_ref
        target[r // 2] = rows_dot(normed_ref[:, cols], low).astype(BF16)
        dnormed_ref[:, cols] += back_dot(low, weights[r][...])


def shape(dims, dtype=F32):
    return jax.ShapeDtypeStruct(dims, dtype)


def call(kernel, name, grid, scal, args, in_specs, out_specs, out_shape, scratch, flops, exps=0):
    size = sum(a.size * a.dtype.itemsize for a in args) + sum(
        s.size * s.dtype.itemsize for s in out_shape
    )
    return pl.pallas_call(
        kernel,
        grid_spec=pltpu.PrefetchScalarGridSpec(
            num_scalar_prefetch=1,
            grid=(grid,),
            in_specs=in_specs,
            out_specs=out_specs,
            scratch_shapes=scratch,
        ),
        out_shape=out_shape,
        name=name,
        compiler_params=pltpu.CompilerParams(vmem_limit_bytes=VMEM_LIMIT),
        cost_estimate=pl.CostEstimate(flops=flops, bytes_accessed=size, transcendentals=exps),
    )(scal, *args)


def whole_spec(dims):
    return pl.BlockSpec(dims, lambda i, scal: (0,) * len(dims))


def local(
    tokens,
    teacher,
    lengths,
    pair_owner,
    norm_gain,
    in_proj,
    conv_weight,
    conv_bias,
    x_proj,
    dt_proj,
    dt_bias,
    a_log,
    skip_scale,
    out_proj,
):
    ctx = lax.axis_size("ctx")
    fsdp = lax.axis_size("fsdp")
    me_ctx = lax.axis_index("ctx")
    me_fsdp = lax.axis_index("fsdp")
    piece = tokens.shape[1] // 2
    features = tokens.shape[2]
    width = in_proj.shape[1] // 2
    rank = dt_proj.shape[0]
    states = a_log.shape[0]
    groups = piece // 8
    ext = HALO + piece
    depth = features // fsdp
    part = width // fsdp
    rows_all = 2 * piece
    elements = rows_all * states * width

    relative = jnp.arange(ctx, dtype=jnp.int32) ^ me_ctx
    pair_of = jnp.sum(
        jnp.arange(ctx, dtype=jnp.int32)[None, :]
        * (pair_owner[None, :] == relative[:, None]).astype(jnp.int32),
        axis=1,
    )
    places = jnp.stack([pair_of, ctx - 1 - pair_of])
    pair_id = pair_of[0]
    own = places[:, 0]
    limits = jnp.clip(lengths[0] - own * piece, 0, piece)
    scal = jnp.concatenate([me_fsdp[None], limits]).astype(jnp.int32)
    between = (places[:, :, None] < places[:, None, :]) & (
        places[:, None, :] < own[:, None, None]
    )
    between_back = (places[:, :, None] > places[:, None, :]) & (
        places[:, None, :] > own[:, None, None]
    )
    before = places < own[:, None]
    behind = places > own[:, None]
    has_before = jnp.stack([pair_id > 0, pair_id < ctx - 1])
    has_after = jnp.stack([pair_id < ctx - 1, pair_id > 0])
    lower = pair_owner[jnp.maximum(pair_id - 1, 0)] ^ me_ctx
    upper = pair_owner[jnp.minimum(pair_id + 1, ctx - 1)] ^ me_ctx

    rows_head = jnp.concatenate(
        [
            conv_weight,
            conv_bias[None],
            dt_bias[None],
            skip_scale[None],
            jnp.pad(norm_gain, (0, part - depth))[None],
            jnp.zeros((HEAD - 8, part), BF16),
            dt_proj,
            a_log,
            x_proj.T,
        ],
        axis=0,
    )
    small_blocks = gather_fsdp(rows_head)
    small = jnp.concatenate(small_blocks, axis=1)
    gain = jnp.concatenate([block[7, :depth] for block in small_blocks]).astype(F32)
    x_blocks = gather_fsdp(in_proj[:, :width])
    gate_blocks = gather_fsdp(after(in_proj[:, width:], x_blocks[-2]))
    out_blocks = gather_fsdp(after(out_proj, gate_blocks[-2]))

    def to_blocks(values, size):
        axis = values.ndim - 1
        return jnp.concatenate(
            [
                lax.dynamic_slice_in_dim(values, (me_fsdp ^ r) * size, size, axis=axis)
                for r in range(fsdp)
            ],
            axis=axis,
        )

    own_rows = tokens[0]
    token_rel = to_blocks(own_rows, depth).reshape(2, piece, features)
    tails = jnp.stack(gather_ctx(to_blocks(own_rows.reshape(2, piece, features)[:, piece - 3 :], depth)))
    before_rows = jnp.stack([tails[lower, 0], tails[upper, 1]])
    before_rows = jnp.where(has_before[:, None, None], before_rows, jnp.zeros_like(before_rows))
    rows_ext = jnp.concatenate(
        [jnp.zeros((2, HALO - 3, features), BF16), before_rows, token_rel], axis=1
    ).astype(F32)
    inv_rms = lax.rsqrt(jnp.mean(rows_ext * rows_ext, axis=2, keepdims=True) + EPSILON)
    normed = (rows_ext * inv_rms * gain).astype(BF16).reshape(2 * ext, features)

    count = total(jnp.sum(jnp.minimum(lengths, 2 * ctx * piece)).astype(F32)[None], ("fsdp",))
    scale = ((fsdp * rows_all * ctx) / count).reshape(1, 1)

    def cols_at(block):
        per = part // block
        return lambda i, scal: (0, (scal[0] ^ (i // per)) * per + i % per)

    def spec_small(block, offset=0):
        return pl.BlockSpec((small.shape[0], block), lambda i, scal: (0, i + offset))

    def spec_rows(block, offset=0):
        return pl.BlockSpec((2, piece, block), lambda i, scal: (0, 0, i + offset))

    def spec_groups(block):
        return pl.BlockSpec((2, groups, 8, block), lambda i, scal: (0, 0, 0, i))

    cb = min(256, part)
    steps = width // cb
    weight_specs = [pl.BlockSpec((depth, cb), cols_at(cb)) for _ in range(fsdp)]
    x_ext, conv, xs, proj = call(
        functools.partial(input_kernel, count=fsdp, piece=piece),
        "inputs", steps, scal, (normed, *x_blocks, small),
        [whole_spec((2 * ext, features)), *weight_specs, spec_small(cb)],
        [
            pl.BlockSpec((2, ext, cb), lambda i, scal: (0, 0, i)),
            spec_rows(cb),
            spec_rows(cb),
            whole_spec((rows_all, rank + 2 * states)),
        ],
        [
            shape((2, ext, width), BF16),
            shape((2, piece, width)),
            shape((2, piece, width), BF16),
            shape((rows_all, rank + 2 * states)),
        ],
        [], 2 * rows_all * features * width,
    )
    wide_dims = (2, piece, states, LANES)
    maps = proj[:, rank:].reshape(2, piece, 2 * states, 1)
    b_wide = jnp.broadcast_to(maps[:, :, :states], wide_dims)

    tiles = 4
    block = tiles * LANES
    step, ends, logs = call(
        functools.partial(end_kernel, tiles=tiles, groups=groups, rank=rank),
        "end_states", width // block, scal, (proj, small, xs, b_wide),
        [whole_spec(proj.shape), spec_small(block), spec_rows(block), whole_spec(wide_dims)],
        [
            spec_groups(block),
            pl.BlockSpec((2 * states, block), lambda i, scal: (0, i)),
            pl.BlockSpec((2, block), lambda i, scal: (0, i)),
        ],
        [shape((2, groups, 8, width)), shape((2 * states, width), BF16), shape((2, width))],
        [pltpu.VMEM((2, groups, 8, block), F32)], 5 * elements, elements,
    )
    log_hi = logs.astype(BF16)
    log_mid = (logs - log_hi.astype(F32)).astype(BF16)
    log_lo = (logs - log_hi.astype(F32) - log_mid.astype(F32)).astype(BF16)
    sent = jnp.concatenate([ends, log_hi, log_mid, log_lo, jnp.zeros((2, width), BF16)], axis=0)
    end_blocks = gather_ctx(sent)
    log_parts = jnp.stack([b[2 * states : 2 * states + 6] for b in end_blocks]).astype(F32)
    log_all = log_parts[:, 0:2] + log_parts[:, 2:4] + log_parts[:, 4:6]

    def spans(inside, wanted):
        summed = jnp.sum(
            jnp.where(inside[..., None], log_all.transpose(1, 0, 2)[:, None], 0.0), axis=2
        )
        return jnp.where(wanted[..., None], summed, 1e30).reshape(2 * ctx, width)

    log_before = spans(between, before)
    log_behind = spans(between_back, behind)

    c_wide = jnp.broadcast_to(maps[:, :, states:], wide_dims)
    (gate,) = call(
        functools.partial(gate_kernel, count=fsdp, piece=piece),
        "gates", steps, scal, (normed, *gate_blocks),
        [whole_spec((2 * ext, features)), *weight_specs], [spec_rows(cb)],
        [shape((2, piece, width))], [], 2 * rows_all * features * width,
    )
    weight_out = jnp.concatenate(out_blocks, axis=0)

    tiles = 2
    block = tiles * LANES
    end_spec = pl.BlockSpec((2 * states, block), lambda i, scal: (0, i))
    log_spec = pl.BlockSpec((2 * ctx, block), lambda i, scal: (0, i))
    hidden_spec = pl.BlockSpec((tiles, 2, piece, states, LANES), lambda i, scal: (i, 0, 0, 0, 0))
    start_spec = pl.BlockSpec((2, states, block), lambda i, scal: (0, 0, i))
    out_spec = pl.BlockSpec((block, features), lambda i, scal: (i, 0))
    row_spec = whole_spec((rows_all, features))
    ssm, branch, hidden, starts, out_low, g_out, d_out, squares = call(
        functools.partial(forward_kernel, tiles=tiles, groups=groups, ctx=ctx, features=features),
        "forward_states", width // block, scal,
        (*end_blocks[1:], log_before, scale, small, step, xs, gate, b_wide, c_wide, weight_out,
         own_rows, teacher[0]),
        [
            *([end_spec] * (ctx - 1)), log_spec, pl.BlockSpec(memory_space=pltpu.SMEM),
            spec_small(block), spec_groups(block), spec_rows(block), spec_rows(block),
            whole_spec(wide_dims), whole_spec(wide_dims), out_spec, row_spec, row_spec,
        ],
        [
            spec_rows(block), spec_rows(block), hidden_spec, start_spec, row_spec, row_spec, row_spec,
            whole_spec((8, features)),
        ],
        [
            shape((2, piece, width)),
            shape((2, piece, width), BF16),
            shape((width // LANES, 2, piece, states, LANES), BF16),
            shape((2, states, width)),
            shape((rows_all, features), BF16),
            shape((rows_all, features)),
            shape((rows_all, features), BF16),
            shape((8, features)),
        ],
        [
            pltpu.VMEM((2, groups, 8, block), F32),
            pltpu.VMEM((2, groups, 8, block), F32),
            pltpu.VMEM((rows_all, features), F32),
        ],
        10 * elements, elements,
    )
    tiles = 4
    block = tiles * LANES
    d_ssm, d_gate, grad_skip, first_grads = call(
        functools.partial(first_grad_kernel, tiles=tiles, groups=groups),
        "first_grads", width // block, scal,
        (d_out, weight_out, small, step, xs, gate, ssm, c_wide),
        [
            row_spec, pl.BlockSpec((block, features), lambda i, scal: (i, 0)), spec_small(block),
            spec_groups(block), spec_rows(block), spec_rows(block), spec_rows(block), whole_spec(wide_dims),
        ],
        [
            spec_groups(block), spec_rows(block), pl.BlockSpec((1, block), lambda i, scal: (0, i)),
            pl.BlockSpec((2 * states, block), lambda i, scal: (0, i)),
        ],
        [
            shape((2, groups, 8, width)),
            shape((2, piece, width), BF16),
            shape((1, width)),
            shape((2 * states, width), BF16),
        ],
        [], 6 * elements, elements,
    )
    grad_blocks = gather_ctx(first_grads)

    pairs = fsdp // 2
    subs = part // cb
    branch_rows = branch.reshape(rows_all, width)
    keep_out, send_out = pl.pallas_call(
        out_grad_kernel,
        grid=(pairs, subs),
        in_specs=[
            pl.BlockSpec((rows_all, cb), lambda k, s: (0, 2 * k * subs + s)),
            pl.BlockSpec((rows_all, cb), lambda k, s: (0, (2 * k + 1) * subs + s)),
            pl.BlockSpec((rows_all, features), lambda k, s: (0, 0)),
        ],
        out_specs=[pl.BlockSpec((1, cb, features), lambda k, s: (k, s, 0))] * 2,
        out_shape=[shape((pairs, part, features), BF16)] * 2,
        name="out_grads",
        compiler_params=pltpu.CompilerParams(vmem_limit_bytes=VMEM_LIMIT),
        cost_estimate=pl.CostEstimate(
            flops=2 * rows_all * width * features, bytes_accessed=9 * 2**20, transcendentals=0
        ),
    )(branch_rows, branch_rows, d_out)
    pair_spec = pl.BlockSpec((pairs, depth, cb), lambda i, scal: (0, 0, i))
    pair_at = pl.BlockSpec(
        (pairs, depth, cb), lambda i, scal: (0, 0, cols_at(cb)(i, scal)[1])
    )
    keep_gate, send_gate, d_normed_gate = call(
        functools.partial(gate_grad_kernel, count=fsdp, piece=piece),
        "gate_grads", steps, scal, (normed, d_gate, *gate_blocks),
        [whole_spec((2 * ext, features)), spec_rows(cb), *weight_specs],
        [pair_at, pair_at, row_spec],
        [shape((pairs, depth, width), BF16)] * 2 + [shape((rows_all, features))],
        [], 4 * rows_all * features * width,
    )
    sum_out = reduce_shard(keep_out, send_out, False)
    sum_gate = reduce_shard(keep_gate, send_gate, True)

    tiles = 2
    block = tiles * LANES
    d_xs, small_back, d_delta, db_wide, dc_wide = call(
        functools.partial(backward_kernel, tiles=tiles, groups=groups, ctx=ctx, rank=rank),
        "backward_states", width // block, scal,
        (*grad_blocks[1:], log_behind, proj, small, step, xs, b_wide, c_wide, starts, d_ssm, hidden),
        [
            *([end_spec] * (ctx - 1)), log_spec, whole_spec(proj.shape), spec_small(block),
            spec_groups(block), spec_rows(block), whole_spec(wide_dims), whole_spec(wide_dims),
            start_spec, spec_groups(block), hidden_spec,
        ],
        [
            spec_rows(block), pl.BlockSpec((rank + states + 8, block), lambda i, scal: (0, i)),
            whole_spec((rows_all, rank)), whole_spec(wide_dims), whole_spec(wide_dims),
        ],
        [
            shape((2, piece, width)),
            shape((rank + states + 8, width)),
            shape((rows_all, rank)),
            shape(wide_dims),
            shape(wide_dims),
        ],
        [pltpu.VMEM((2, groups, 8, block), F32)] * 3,
        24 * elements, elements,
    )
    d_proj = jnp.concatenate(
        [
            d_delta,
            jnp.sum(db_wide, axis=3).reshape(rows_all, states),
            jnp.sum(dc_wide, axis=3).reshape(rows_all, states),
        ],
        axis=1,
    ).astype(BF16)
    half_steps = steps // 2
    halves = []
    for side in range(2):
        base = side * half_steps

        def place(i, scal, base=base):
            return cols_at(cb)(i + base, scal)[1]

        def at_rows(dims):
            return pl.BlockSpec((2, dims, cb), lambda i, scal, place=place: (0, 0, place(i, scal)))

        def at_cols(i, scal, base=base):
            return 0, i + base

        halves.append(
            call(
                functools.partial(tail_kernel, count=fsdp, piece=piece),
                "tail_grads", half_steps, scal,
                (d_proj, small, d_xs, conv, x_ext, xs, normed, *x_blocks),
                [
                    whole_spec(d_proj.shape),
                    pl.BlockSpec((small.shape[0], cb), lambda i, scal, place=place: (0, place(i, scal))),
                    at_rows(piece), at_rows(piece), at_rows(ext), at_rows(piece),
                    whole_spec((2 * ext, features)),
                    *([pl.BlockSpec((depth, cb), at_cols)] * fsdp),
                ],
                [
                    pl.BlockSpec((104, cb), lambda i, scal: (0, i)),
                    pair_spec, pair_spec, whole_spec((2 * ext, features)),
                ],
                [
                    shape((104, width // 2)),
                    shape((pairs, depth, width // 2), BF16),
                    shape((pairs, depth, width // 2), BF16),
                    shape((2 * ext, features)),
                ],
                [pltpu.VMEM((2, ext + 8, cb), F32)],
                4 * rows_all * features * width // 2,
            )
        )
    sum_x = [
        reduce_shard(side[1], side[2], ctx_first) for side, ctx_first in zip(halves, (False, True))
    ]
    tail_small = to_blocks(jnp.concatenate([halves[0][0], halves[1][0]], axis=1), part)
    d_normed = (halves[0][3] + halves[1][3]).reshape(2, ext, features)
    halo_grad = d_normed[:, HALO - 3 : HALO]
    halo_all = jnp.stack(gather_ctx(halo_grad.astype(BF16))).astype(F32)
    from_next = jnp.stack([halo_all[upper, 0], halo_all[lower, 1]])
    from_next = jnp.where(has_after[:, None, None], from_next, 0.0)
    unit = rows_ext * inv_rms
    own_normed = d_normed[:, HALO:] + d_normed_gate.reshape(2, piece, features)
    grad_gain = jnp.sum(halo_grad * unit[:, HALO - 3 : HALO], axis=(0, 1)) + jnp.sum(
        own_normed * unit[:, HALO:], axis=(0, 1)
    )
    grad_gain = jnp.pad(grad_gain.reshape(fsdp, 1, depth), ((0, 0), (0, 0), (0, part - depth)))
    small_rows = jnp.concatenate(
        [
            tail_small[0:5],
            small_back[rank + states : rank + states + 1],
            grad_skip,
            grad_gain.transpose(1, 0, 2).reshape(1, width),
            jnp.zeros((HEAD - 8, width), F32),
            small_back[0 : rank + states],
            tail_small[8:104],
        ],
        axis=0,
    ).astype(BF16)
    small_pairs = small_rows.reshape(small_rows.shape[0], pairs, 2, part).transpose(2, 1, 0, 3)
    sum_small = reduce_shard(small_pairs[0], small_pairs[1], False).astype(F32)

    own_normed = own_normed + jnp.pad(from_next, ((0, 0), (piece - 3, 0), (0, 0)))
    own_inv = inv_rms[:, HALO:]
    own_u = rows_ext[:, HALO:]
    scaled = own_normed * gain
    d_rows = own_inv * scaled - own_u * (own_inv * own_inv * own_inv) * jnp.mean(
        scaled * own_u, axis=2, keepdims=True
    )
    d_rows = d_rows.reshape(rows_all, features)

    grad_tokens = (to_blocks(d_rows, depth) + g_out)[None]
    square_total = total(jnp.sum(squares)[None], ("fsdp", "ctx"))[0]
    loss = square_total / (count[0] * features)
    grad_in = jnp.concatenate([*sum_x, sum_gate], axis=1).astype(F32)
    return (
        out_low[None],
        loss,
        grad_tokens,
        sum_small[7, :depth],
        grad_in,
        sum_small[0:4],
        sum_small[4],
        sum_small[96:192].T,
        sum_small[HEAD : HEAD + rank],
        sum_small[5],
        sum_small[80 : 80 + states],
        sum_small[6],
        sum_out.astype(F32),
    )


def solution(mesh):
    in_specs = (
        P("fsdp", "ctx", None),
        P("fsdp", "ctx", None),
        P("fsdp", None),
        P(),
        P("fsdp"),
        P("fsdp", None),
        P(None, "fsdp"),
        P("fsdp"),
        P("fsdp", None),
        P(None, "fsdp"),
        P("fsdp"),
        P(None, "fsdp"),
        P("fsdp"),
        P("fsdp", None),
    )
    out_specs = (
        P("fsdp", "ctx", None),
        P(),
        P("fsdp", "ctx", None),
        P("fsdp"),
        P("fsdp", None),
        P(None, "fsdp"),
        P("fsdp"),
        P("fsdp", None),
        P(None, "fsdp"),
        P("fsdp"),
        P(None, "fsdp"),
        P("fsdp"),
        P("fsdp", None),
    )
    return jax.shard_map(local, mesh=mesh, in_specs=in_specs, out_specs=out_specs, check_vma=False)
```

time: 2220 us -> 602 us (0.27)
  other arithmetic: 1320 us -> 55.3 us
  local copies, waits for them, and re-layouts: 344 us -> 47.2 us
  Pallas kernels: 0 us -> 220 us
  blocking collectives: 201 us -> 0 us
  starting transfers between devices: 1.19 us -> 91.8 us
  waiting for transfers between devices: 239 us -> 168 us
  matrix products: 54.4 us -> 0 us
    while x504 -> x0, other arithmetic: 826 us -> none
    pallas_call x0 -> x10, Pallas kernels: none -> 220 us  [the longest x9 214 us: call(): pl.pallas_call(kernel, grid_spec=pltpu.PrefetchScalarGridSpec(num_scalar_...]
    reduce_sum x44 -> x9, other arithmetic: 190 us -> 14.2 us  [the longest x1 3.51 us: local(): jnp.sum(own_normed * unit[:, HALO:], axis=(0, 1))]
    ppermute x0 -> x87, waiting for transfers between devices: none -> 168 us  [swap(): return lax.ppermute(values, axis, [(i, i ^ bit) for i in range(size)])]
    while x264 -> x0, local copies, waits for them, and re-layouts: 112 us -> none
    all_gather x10 -> x0, blocking collectives: 112 us -> none  [the longest x1 30.8 us: local(): all_tails = lax.all_gather(tails[None], 'ctx', axis=0, tiled=True)]
    psum x1 -> x0, waiting for transfers between devices: 97.3 us -> none  [local(): lax.psum(part_in.astype(jnp.bfloat16), 'ctx').astype(jnp.float32)]
    ppermute x0 -> x87, starting transfers between devices: none -> 91.8 us  [swap(): return lax.ppermute(values, axis, [(i, i ^ bit) for i in range(size)])]
  transfers between devices with their start and end apart: 12 -> 87, of which waited for: 5 -> 48; matrix products, arithmetic and copies ran while one was open for 29% -> 12% of each run, Pallas kernels for 0% -> 10%
where the time goes in v1:
time: 602 us; the launch traced here: 594 us
  Pallas kernels  220 us (37%)
  waiting for transfers between devices  168 us (28%)
  starting transfers between devices  91.8 us (15%)
  other arithmetic  55.3 us (9%)
  local copies, waits for them, and re-layouts  47.2 us (8%)
  between operations  12.4 us (2%)
    pallas_call x9, Pallas kernels, call(): pl.pallas_call(kernel, grid_spec=pltpu.PrefetchScalarGridSpec(num_scalar_...  214 us
    ppermute x87, waiting for transfers between devices, swap(): return lax.ppermute(values, axis, [(i, i ^ bit) for i in range(size)])  168 us
    ppermute x87, starting transfers between devices, swap(): return lax.ppermute(values, axis, [(i, i ^ bit) for i in range(size)])  91.8 us
  transfers between devices with their start and end apart: 87, of which 48 were waited for; matrix products, arithmetic and copies ran while one was open for 12% of the time, Pallas kernels for 10%

profile of v1, /device:TPU:0, one launch (start us, length us, event | category | flops | bytes accessed | tf_op | source)
XLA Modules:
  0.0 594.4 jit_solution(10731931946607549875)
XLA Ops:
  58.8 11.3 %collective-permute-done.11.refs_2_ = bf16[256,2048]{1,0:T(8,128)(2,1)S(1)} collective-permute-done((bf16[256,2048]{1,0:T(8,128)(2,1)S(1)}, bf16[256,2048]{1,0:T(8,128)(2,1)S(1)}, u32[]{:S(2)}, u32[]{:S(2)}) %collective-permute-start.11) | collective-permute-done | bytes 1048608 | tf_op jit(solution)/shard_map/ppermute | solution.py:22
  77.7 14.1 %inputs.1 = (bf16[2,272,2048]{2,1,0:T(8,128)(2,1)}, f32[2,256,2048]{2,1,0:T(8,128)}, bf16[2,256,2048]{2,1,0:T(8,128)(2,1)}, f32[512,96]{1,0:T(8,128)}) custom-call(s32[3]{0:T(128)} %pad_add_fusion.3.scal, bf16[544,1024]{1,0:T(8,128)(2,1)} %fusion.1.normed_ref, bf16[256,2048]{1,0:T(8,128)(2,1)} %copy-done.2, ...), custom_call_target="tpu_custom_call" | custom-call | flops 2147483648 | bytes 14811136 | tf_op jit(solution)/shard_map/inputs/pallas_call | solution.py:478
  95.5 19.7 %end_states.1 = (f32[2,32,8,2048]{3,2,1,0:T(8,128)}, bf16[32,2048]{1,0:T(8,128)(2,1)}, f32[2,2048]{1,0:T(2,128)}) custom-call(s32[3]{0:T(128)} %pad_add_fusion.3.scal, f32[512,96]{1,0:T(8,128)} %get-tuple-element.52.proj_ref.refs_8_, bf16[192,2048]{1,0:T(8,128)(2,1)} %pad_maximum_fusion.3.refs_4_.s_ref.refs_9_, ...), custom_call_target="tpu_custom_call" | custom-call | flops 83886080 | bytes 11616256 | tf_op jit(solution)/shard_map/end_states/pallas_call | solution.py:478
  128.5 6.6 %collective-permute-done.16.refs_3_ = bf16[40,2048]{1,0:T(8,128)(2,1)S(1)} collective-permute-done((bf16[40,2048]{1,0:T(8,128)(2,1)S(1)}, bf16[40,2048]{1,0:T(8,128)(2,1)S(1)}, u32[]{:S(2)}, u32[]{:S(2)}) %collective-permute-start.16) | collective-permute-done | bytes 163872 | tf_op jit(solution)/shard_map/ppermute | solution.py:22
  137.3 6.2 %collective-permute-done.17.refs_4_ = bf16[40,2048]{1,0:T(8,128)(2,1)S(1)} collective-permute-done((bf16[40,2048]{1,0:T(8,128)(2,1)S(1)}, bf16[40,2048]{1,0:T(8,128)(2,1)S(1)}, u32[]{:S(2)}, u32[]{:S(2)}) %collective-permute-start.17) | collective-permute-done | bytes 163872 | tf_op jit(solution)/shard_map/ppermute | solution.py:22
  158.8 9.4 %gates.1.refs_12_.gate_ref = f32[2,256,2048]{2,1,0:T(8,128)} custom-call(s32[3]{0:T(128)} %pad_add_fusion.3.scal, bf16[544,1024]{1,0:T(8,128)(2,1)} %fusion.1.normed_ref, bf16[256,2048]{1,0:T(8,128)(2,1)} %get-tuple-element.57.refs_0_, bf16[256,2048]{1,0:T(8,128)(2,1)} %collective-permute-done.22.refs_1_, bf16[256,2048]{1,0:T(8,128)(2,1)} %copy-done.11, ...), custom_call_target="tpu_custom_call" | custom-call | flops 2147483648 | bytes 9502720 | tf_op jit(solution)/shard_map/gates/pallas_call | solution.py:478
  173.2 41.9 %forward_states.1 = (f32[2,256,2048]{2,1,0:T(8,128)}, bf16[2,256,2048]{2,1,0:T(8,128)(2,1)}, bf16[16,2,256,16,128]{4,3,2,1,0:T(8,128)(2,1)}, f32[2,16,2048]{2,1,...) custom-call(s32[3]{0:T(128)} %pad_add_fusion.3.scal, ...), custom_call_target="tpu_custom_call" | custom-call | flops 167772160 | bytes 71565312 | tf_op jit(solution)/shard_map/forward_states/pallas_call | solution.py:478
  215.2 22.7 %first_grads.1 = (f32[2,32,8,2048]{3,2,1,0:T(8,128)}, bf16[2,256,2048]{2,1,0:T(8,128)(2,1)}, f32[1,2048]{1,0:T(1,128)}, bf16[32,2048]{1,0:T(8,128)(2,1)}) custom-call(s32[3]{0:T(128)} %pad_add_fusion.3.scal, bf16[512,1024]{1,0:T(8,128)(2,1)} %get-tuple-element.61.dout_ref, bf16[2048,1024]{1,0:T(8,128)(2,1)} %constant_dynamic-update-slice_fusion.16.refs_15_.weight_ref, ...), custom_call_target="tpu_custom_call" | custom-call | flops 100663296 | bytes 31334400 | tf_op jit(solution)/shard_map/first_grads/pallas_call | solution.py:478
  237.8 5.8 collective-permute-start.34
  249.8 7.4 %collective-permute-done.36.refs_3_ = bf16[32,2048]{1,0:T(8,128)(2,1)S(1)} collective-permute-done((bf16[32,2048]{1,0:T(8,128)(2,1)}, bf16[32,2048]{1,0:T(8,128)(2,1)S(1)}, u32[]{:S(2)}, u32[]{:S(2)}) %collective-permute-start.36) | collective-permute-done | bytes 131104 | tf_op jit(solution)/shard_map/ppermute | solution.py:22
  259.2 12.0 %gate_grads.1 = (bf16[2,256,2048]{2,1,0:T(8,128)(2,1)}, bf16[2,256,2048]{2,1,0:T(8,128)(2,1)}, f32[512,1024]{1,0:T(8,128)}) custom-call(s32[3]{0:T(128)} %pad_add_fusion.3.scal, bf16[544,1024]{1,0:T(8,128)(2,1)} %fusion.1.normed_ref, bf16[2,256,2048]{2,1,0:T(8,128)(2,1)} %get-tuple-element.75.dgate_ref, bf16[256,2048]{1,0:T(8,128)(2,1)} %get-tuple-element.57.refs_0_, ...), custom_call_target="tpu_custom_call" | custom-call | flops 4294967296 | bytes 13697024 | tf_op jit(solution)/shard_map/gate_grads/pallas_call | solution.py:478
  272.1 70.5 %backward_states.1 = (f32[2,256,2048]{2,1,0:T(8,128)}, f32[88,2048]{1,0:T(8,128)}, f32[512,64]{1,0:T(8,128)}, f32[2,256,16,128]{3,2,1,0:T(8,128)}, f32[2,256,16,128]{3,2,1,0:T(8,128)}) custom-call(s32[3]{0:T(128)} %pad_add_fusion.3.scal, bf16[32,2048]{1,0:T(8,128)(2,1)} %copy-done.22, bf16[32,2048]{1,0:T(8,128)(2,1)} %copy-done.19, ...), custom_call_target="tpu_custom_call" | custom-call | flops 402653184 | bytes 68157440 | tf_op jit(solution)/shard_map/backward_states/pallas_call | solution.py:478
  350.3 11.7 %tail_grads.3 = (f32[104,1024]{1,0:T(8,128)}, bf16[2,256,1024]{2,1,0:T(8,128)(2,1)}, bf16[2,256,1024]{2,1,0:T(8,128)(2,1)}, f32[544,1024]{1,0:T(8,128)}) custom-call(s32[3]{0:T(128)} %pad_add_fusion.3.scal, bf16[512,96]{1,0:T(8,128)(2,1)} %pad_maximum_fusion.10.dproj_ref, bf16[192,2048]{1,0:T(8,128)(2,1)} %pad_maximum_fusion.3.refs_4_.s_ref.refs_9_, ...), custom_call_target="tpu_custom_call" | custom-call | flops 2147483648 | bytes 23658496 | tf_op jit(solution)/shard_map/tail_grads/pallas_call | solution.py:478
  362.0 11.7 %tail_grads.2 = (f32[104,1024]{1,0:T(8,128)}, bf16[2,256,1024]{2,1,0:T(8,128)(2,1)}, bf16[2,256,1024]{2,1,0:T(8,128)(2,1)}, f32[544,1024]{1,0:T(8,128)}) custom-call(s32[3]{0:T(128)} %pad_add_fusion.3.scal, bf16[512,96]{1,0:T(8,128)(2,1)} %pad_maximum_fusion.10.dproj_ref, bf16[192,2048]{1,0:T(8,128)(2,1)} %pad_maximum_fusion.3.refs_4_.s_ref.refs_9_, ...), custom_call_target="tpu_custom_call" | custom-call | flops 2147483648 | bytes 23658496 | tf_op jit(solution)/shard_map/tail_grads/pallas_call | solution.py:478
  412.4 6.0 %out_grads.1 = (bf16[2,512,1024]{2,1,0:T(8,128)(2,1)}, bf16[2,512,1024]{2,1,0:T(8,128)(2,1)}) custom-call(bf16[512,2048]{1,0:T(8,128)(2,1)} %bitcast.199, bf16[512,2048]{1,0:T(8,128)(2,1)} %bitcast.200, bf16[512,1024]{1,0:T(8,128)(2,1)} %get-tuple-element.61.dout_ref), custom_call_target="tpu_custom_call" | custom-call | flops 2147483648 | bytes 9437184 | tf_op jit(solution)/shard_map/out_grads/pallas_call | solution.py:743
  419.7 6.3 %collective-permute-done.28 = f32[1]{0:T(128)} collective-permute-done((f32[1]{0:T(128)}, f32[1]{0:T(128)}, u32[]{:S(2)}, u32[]{:S(2)}) %collective-permute-start.28) | collective-permute-done | bytes 36 | tf_op jit(solution)/shard_map/ppermute | solution.py:22
  471.5 6.3 %collective-permute-done.64 = bf16[2,128,1024]{2,1,0:T(8,128)(2,1)S(1)} collective-permute-done((bf16[2,128,1024]{2,1,0:T(8,128)(2,1)S(1)}, bf16[2,128,1024]{2,1,0:T(8,128)(2,1)S(1)}, u32[]{:S(2)}, u32[]{:S(2)}) %collective-permute-start.64) | collective-permute-done | bytes 524320 | tf_op jit(solution)/shard_map/ppermute | solution.py:22
  491.7 5.6 collective-permute-done.66
  498.5 5.6 collective-permute-done.67
  518.6 5.7 collective-permute-done.70
  529.5 5.5 collective-permute-done.81
  536.3 6.3 %collective-permute-done.73 = bf16[2,64,2048]{2,1,0:T(8,128)(2,1)S(1)} collective-permute-done((bf16[2,64,2048]{2,1,0:T(8,128)(2,1)S(1)}, bf16[2,64,2048]{2,1,0:T(8,128)(2,1)S(1)}, u32[]{:S(2)}, u32[]{:S(2)}) %collective-permute-start.73) | collective-permute-done | bytes 524320 | tf_op jit(solution)/shard_map/ppermute | solution.py:22
  547.1 12.0 %collective-permute-done.74 = bf16[2,32,2048]{2,1,0:T(8,128)(2,1)S(1)} collective-permute-done((bf16[2,32,2048]{2,1,0:T(8,128)(2,1)S(1)}, bf16[2,32,2048]{2,1,0:T(8,128)(2,1)S(1)}, u32[]{:S(2)}, u32[]{:S(2)}) %collective-permute-start.74) | collective-permute-done | bytes 262176 | tf_op jit(solution)/shard_map/ppermute | solution.py:22
  578.1 6.3 %collective-permute-done.86 = bf16[1,256,1024]{2,1,0:T(8,128)(2,1)S(1)} collective-permute-done((bf16[1,256,1024]{2,1,0:T(8,128)(2,1)S(1)}, bf16[1,256,1024]{2,1,0:T(8,128)(2,1)S(1)}, u32[]{:S(2)}, u32[]{:S(2)}) %collective-permute-start.86) | collective-permute-done | bytes 524320 | tf_op jit(solution)/shard_map/ppermute | solution.py:22
  (472 shorter events, 265.3 us)
Async XLA Ops:
  1.7 40.6 %collective-permute-start = (bf16[2,3,1024]{2,1,0:T(4,128)(2,1)S(1)}, bf16[2,3,1024]{2,1,0:T(4,128)(2,1)}, u32[]{:S(2)}, u32[]{:S(2)}) collective-permute-start(bf16[2,3,1024]{2,1,0:T(4,128)(2,1)S(1)} %pad_maximum_fusion.15), channel_id=1, source_target_pairs={{0,4},{4,0},{8,12},{12,8},{16,20},{20,16},{24,28},{28,24},{1,5},{5... | collective-permute-start | bytes 36872 | tf_op jit(solution)/shard_map/ppermute | solution.py:22
  4.7 37.7 %collective-permute-start.1 = (bf16[2,3,1024]{2,1,0:T(4,128)(2,1)S(1)}, bf16[2,3,1024]{2,1,0:T(4,128)(2,1)S(1)}, u32[]{:S(2)}, u32[]{:S(2)}) collective-permute-start(bf16[2,3,1024]{2,1,0:T(4,128)(2,1)S(1)} %pad_maximum_fusion.15), channel_id=1, source_target_pairs={{0,8},{4,12},{8,0},{12,4},{16,24},{20,28},{24,16},{28,20},{1,9},{5... | collective-permute-start | bytes 36872 | tf_op jit(solution)/shard_map/ppermute | solution.py:22
  6.3 38.6 %collective-permute-start.3 = (bf16[2,3,1024]{2,1,0:T(4,128)(2,1)S(1)}, bf16[2,3,1024]{2,1,0:T(4,128)(2,1)S(1)}, u32[]{:S(2)}, u32[]{:S(2)}) collective-permute-start(bf16[2,3,1024]{2,1,0:T(4,128)(2,1)S(1)} %pad_maximum_fusion.15), channel_id=1, source_target_pairs={{0,16},{4,20},{8,24},{12,28},{16,0},{20,4},{24,8},{28,12},{1,17},{... | collective-permute-start | bytes 36872 | tf_op jit(solution)/shard_map/ppermute | solution.py:22
  8.9 39.3 %collective-permute-start.5 = (bf16[2,3,1024]{2,1,0:T(4,128)(2,1)S(1)}, bf16[2,3,1024]{2,1,0:T(4,128)(2,1)S(1)}, u32[]{:S(2)}, u32[]{:S(2)}) collective-permute-start(bf16[2,3,1024]{2,1,0:T(4,128)(2,1)S(1)} %pad_maximum_fusion.15), channel_id=1, source_target_pairs={{0,24},{4,28},{8,16},{12,20},{16,8},{20,12},{24,0},{28,4},{1,25},{... | collective-permute-start | bytes 36872 | tf_op jit(solution)/shard_map/ppermute | solution.py:22
  11.0 24.8 %collective-permute-start.20 = (f32[1]{0:T(128)}, f32[1]{0:T(128)}, u32[]{:S(2)}, u32[]{:S(2)}) collective-permute-start(f32[1]{0:T(128)} %bitcast.37), channel_id=1, source_target_pairs={{0,1},{1,0},{2,3},{3,2},{4,5},{5,4},{6,7},{7,6},{8,9},{9,8},{10,11... | collective-permute-start | bytes 20 | tf_op jit(solution)/shard_map/ppermute | solution.py:22
  40.0 31.9 %collective-permute-start.8 = (bf16[192,512]{1,0:T(8,128)(2,1)}, bf16[192,512]{1,0:T(8,128)(2,1)}, u32[]{:S(2)}, u32[]{:S(2)}) collective-permute-start(bf16[192,512]{1,0:T(8,128)(2,1)} %concatenate.152), channel_id=1, source_target_pairs={{0,2},{1,3},{2,0},{3,1},{4,6},{5,7},{6,4},{7,5},{8,10},{9,11},{10,... | collective-permute-start | bytes 589832 | tf_op jit(solution)/shard_map/ppermute | solution.py:22
  42.3 30.8 %collective-permute-start.7 = (bf16[192,512]{1,0:T(8,128)(2,1)}, bf16[192,512]{1,0:T(8,128)(2,1)}, u32[]{:S(2)}, u32[]{:S(2)}) collective-permute-start(bf16[192,512]{1,0:T(8,128)(2,1)} %concatenate.152), channel_id=1, source_target_pairs={{0,1},{1,0},{2,3},{3,2},{4,5},{5,4},{6,7},{7,6},{8,9},{9,8},{10,11... | collective-permute-start | bytes 589832 | tf_op jit(solution)/shard_map/ppermute | solution.py:22
  44.9 25.2 %collective-permute-start.11 = (bf16[256,2048]{1,0:T(8,128)(2,1)S(1)}, bf16[256,2048]{1,0:T(8,128)(2,1)S(1)}, u32[]{:S(2)}, u32[]{:S(2)}) collective-permute-start(bf16[256,2048]{1,0:T(8,128)(2,1)S(1)} %get-tuple-element.104.refs_0_), channel_id=1, source_target_pairs={{0,2},{1,3},{2,0},{3,1},{4,6},{5,7},{6,4},{7,5},{8,10},{9,11},{10,... | collective-permute-start | bytes 3145736 | tf_op jit(solution)/shard_map/ppermute | solution.py:22
  48.2 29.5 %collective-permute-start.10 = (bf16[256,2048]{1,0:T(8,128)(2,1)S(1)}, bf16[256,2048]{1,0:T(8,128)(2,1)}, u32[]{:S(2)}, u32[]{:S(2)}) collective-permute-start(bf16[256,2048]{1,0:T(8,128)(2,1)S(1)} %get-tuple-element.104.refs_0_), channel_id=1, source_target_pairs={{0,1},{1,0},{2,3},{3,2},{4,5},{5,4},{6,7},{7,6},{8,9},{9,8},{10,11... | collective-permute-start | bytes 3145736 | tf_op jit(solution)/shard_map/ppermute | solution.py:22
  77.3 45.8 %collective-permute-start.23 = (bf16[256,2048]{1,0:T(8,128)(2,1)}, bf16[256,2048]{1,0:T(8,128)(2,1)S(1)}, u32[]{:S(2)}, u32[]{:S(2)}) collective-permute-start(bf16[256,2048]{1,0:T(8,128)(2,1)} %get-tuple-element.57.refs_0_), channel_id=1, source_target_pairs={{0,2},{1,3},{2,0},{3,1},{4,6},{5,7},{6,4},{7,5},{8,10},{9,11},{10,... | collective-permute-start | bytes 3145736 | tf_op jit(solution)/shard_map/ppermute | solution.py:22
  77.7 80.1 %collective-permute-start.22 = (bf16[256,2048]{1,0:T(8,128)(2,1)}, bf16[256,2048]{1,0:T(8,128)(2,1)}, u32[]{:S(2)}, u32[]{:S(2)}) collective-permute-start(bf16[256,2048]{1,0:T(8,128)(2,1)} %get-tuple-element.57.refs_0_), channel_id=1, source_target_pairs={{0,1},{1,0},{2,3},{3,2},{4,5},{5,4},{6,7},{7,6},{8,9},{9,8},{10,11... | collective-permute-start | bytes 3145736 | tf_op jit(solution)/shard_map/ppermute | solution.py:22
  123.8 30.5 %collective-permute-start.25 = (bf16[512,1024]{1,0:T(8,128)(2,1)S(1)}, bf16[512,1024]{1,0:T(8,128)(2,1)S(1)}, u32[]{:S(2)}, u32[]{:S(2)}) collective-permute-start(bf16[512,1024]{1,0:T(8,128)(2,1)S(1)} %copy-done.13), channel_id=1, source_target_pairs={{0,1},{1,0},{2,3},{3,2},{4,5},{5,4},{6,7},{7,6},{8,9},{9,8},{10,11... | collective-permute-start | bytes 3145736 | tf_op jit(solution)/shard_map/ppermute | solution.py:22
  135.1 17.6 %collective-permute-start.26 = (bf16[512,1024]{1,0:T(8,128)(2,1)S(1)}, bf16[512,1024]{1,0:T(8,128)(2,1)}, u32[]{:S(2)}, u32[]{:S(2)}) collective-permute-start(bf16[512,1024]{1,0:T(8,128)(2,1)S(1)} %copy-done.13), channel_id=1, source_target_pairs={{0,2},{1,3},{2,0},{3,1},{4,6},{5,7},{6,4},{7,5},{8,10},{9,11},{10,... | collective-permute-start | bytes 3145736 | tf_op jit(solution)/shard_map/ppermute | solution.py:22
  137.2 20.5 %collective-permute-start.24 = (bf16[256,2048]{1,0:T(8,128)(2,1)S(1)}, bf16[256,2048]{1,0:T(8,128)(2,1)S(1)}, u32[]{:S(2)}, u32[]{:S(2)}) collective-permute-start(bf16[256,2048]{1,0:T(8,128)(2,1)S(1)} %collective-permute-done.23.refs_2_), channel_id=1, source_target_pairs={{0,1},{1,0},{2,3},{3,2},{4,5},{5,4},{6,7},{7,6},{8,9},{9,8},{10,11... | collective-permute-start | bytes 3145736 | tf_op jit(solution)/shard_map/ppermute | solution.py:22
  247.7 23.6 %collective-permute-start.33 = (bf16[32,2048]{1,0:T(8,128)(2,1)}, bf16[32,2048]{1,0:T(8,128)(2,1)S(1)}, u32[]{:S(2)}, u32[]{:S(2)}) collective-permute-start(bf16[32,2048]{1,0:T(8,128)(2,1)} %get-tuple-element.63), channel_id=1, source_target_pairs={{0,4},{4,0},{8,12},{12,8},{16,20},{20,16},{24,28},{28,24},{1,5},{5... | collective-permute-start | bytes 393224 | tf_op jit(solution)/shard_map/ppermute | solution.py:22
  248.3 23.0 %collective-permute-start.35 = (bf16[32,2048]{1,0:T(8,128)(2,1)S(1)}, bf16[32,2048]{1,0:T(8,128)(2,1)S(1)}, u32[]{:S(2)}, u32[]{:S(2)}) collective-permute-start(bf16[32,2048]{1,0:T(8,128)(2,1)S(1)} %collective-permute-done.34.refs_1_), channel_id=1, source_target_pairs={{0,4},{4,0},{8,12},{12,8},{16,20},{20,16},{24,28},{28,24},{1,5},{5... | collective-permute-start | bytes 393224 | tf_op jit(solution)/shard_map/ppermute | solution.py:22
  411.3 34.3 %collective-permute-start.50 = (bf16[1,48,512]{2,1,0:T(8,128)(2,1)S(1)}, bf16[1,48,512]{2,1,0:T(8,128)(2,1)S(1)}, u32[]{:S(2)}, u32[]{:S(2)}) collective-permute-start(bf16[1,48,512]{2,1,0:T(8,128)(2,1)S(1)} %broadcast_select_fusion.41), channel_id=1, source_target_pairs={{0,8},{4,12},{8,0},{12,4},{16,24},{20,28},{24,16},{28,20},{1,9},{5... | collective-permute-start | bytes 147464 | tf_op jit(solution)/shard_map/ppermute | solution.py:22
  418.4 61.6 %collective-permute-start.79 = (bf16[2,512,1024]{2,1,0:T(8,128)(2,1)}, bf16[2,512,1024]{2,1,0:T(8,128)(2,1)}, u32[]{:S(2)}, u32[]{:S(2)}) collective-permute-start(bf16[2,512,1024]{2,1,0:T(8,128)(2,1)} %get-tuple-element.90), channel_id=1, source_target_pairs={{0,1},{1,0},{2,3},{3,2},{4,5},{5,4},{6,7},{7,6},{8,9},{9,8},{10,11... | collective-permute-start | bytes 6291464 | tf_op jit(solution)/shard_map/ppermute | solution.py:22
  418.5 65.9 %collective-permute-start.71 = (bf16[2,256,2048]{2,1,0:T(8,128)(2,1)}, bf16[2,256,2048]{2,1,0:T(8,128)(2,1)}, u32[]{:S(2)}, u32[]{:S(2)}) collective-permute-start(bf16[2,256,2048]{2,1,0:T(8,128)(2,1)} %get-tuple-element.87), channel_id=1, source_target_pairs={{0,1},{1,0},{2,3},{3,2},{4,5},{5,4},{6,7},{7,6},{8,9},{9,8},{10,11... | collective-permute-start | bytes 6291464 | tf_op jit(solution)/shard_map/ppermute | solution.py:22
  445.0 21.8 %collective-permute-start.63 = (bf16[2,256,1024]{2,1,0:T(8,128)(2,1)}, bf16[2,256,1024]{2,1,0:T(8,128)(2,1)S(1)}, u32[]{:S(2)}, u32[]{:S(2)}) collective-permute-start(bf16[2,256,1024]{2,1,0:T(8,128)(2,1)} %get-tuple-element.85), channel_id=1, source_target_pairs={{0,1},{1,0},{2,3},{3,2},{4,5},{5,4},{6,7},{7,6},{8,9},{9,8},{10,11... | collective-permute-start | bytes 3145736 | tf_op jit(solution)/shard_map/ppermute | solution.py:22
  445.1 23.2 %collective-permute-start.55 = (bf16[2,256,1024]{2,1,0:T(8,128)(2,1)S(1)}, bf16[2,256,1024]{2,1,0:T(8,128)(2,1)S(1)}, u32[]{:S(2)}, u32[]{:S(2)}) collective-permute-start(bf16[2,256,1024]{2,1,0:T(8,128)(2,1)S(1)} %copy-done.48), channel_id=1, source_target_pairs={{0,1},{1,0},{2,3},{3,2},{4,5},{5,4},{6,7},{7,6},{8,9},{9,8},{10,11... | collective-permute-start | bytes 3145736 | tf_op jit(solution)/shard_map/ppermute | solution.py:22
  482.7 41.8 %collective-permute-start.80 = (bf16[1,512,1024]{2,1,0:T(8,128)(2,1)S(1)}, bf16[1,512,1024]{2,1,0:T(8,128)(2,1)S(1)}, u32[]{:S(2)}, u32[]{:S(2)}) collective-permute-start(bf16[1,512,1024]{2,1,0:T(8,128)(2,1)S(1)} %slice.431), channel_id=1, source_target_pairs={{0,2},{1,3},{2,0},{3,1},{4,6},{5,7},{6,4},{7,5},{8,10},{9,11},{10,... | collective-permute-start | bytes 3145736 | tf_op jit(solution)/shard_map/ppermute | solution.py:22
  486.9 40.2 %collective-permute-start.72 = (bf16[2,128,2048]{2,1,0:T(8,128)(2,1)S(1)}, bf16[2,128,2048]{2,1,0:T(8,128)(2,1)S(1)}, u32[]{:S(2)}, u32[]{:S(2)}) collective-permute-start(bf16[2,128,2048]{2,1,0:T(8,128)(2,1)S(1)} %broadcast_select_fusion), channel_id=1, source_target_pairs={{0,4},{4,0},{8,12},{12,8},{16,20},{20,16},{24,28},{28,24},{1,5},{5... | collective-permute-start | bytes 3145736 | tf_op jit(solution)/shard_map/ppermute | solution.py:22
  542.9 16.2 %collective-permute-start.74 = (bf16[2,32,2048]{2,1,0:T(8,128)(2,1)S(1)}, bf16[2,32,2048]{2,1,0:T(8,128)(2,1)S(1)}, u32[]{:S(2)}, u32[]{:S(2)}) collective-permute-start(bf16[2,32,2048]{2,1,0:T(8,128)(2,1)S(1)} %broadcast_select_fusion.11), channel_id=1, source_target_pairs={{0,16},{4,20},{8,24},{12,28},{16,0},{20,4},{24,8},{28,12},{1,17},{... | collective-permute-start | bytes 786440 | tf_op jit(solution)/shard_map/ppermute | solution.py:22
  (113 other events, 1118.3 us)

commit v2 on v1

--- a/solution.py
+++ b/solution.py
@@ -38,14 +38,31 @@
     return [blocks[r] for r in range(len(blocks))]
 
 
-def gather_ctx(values):
+def gather_far(values):
     size = lax.axis_size("ctx")
-    blocks = {0: values}
-    for j in range(2, size, 2):
-        blocks[j] = swap(values, "ctx", j)
-    for j in range(0, size, 2):
-        blocks[j | 1] = swap(blocks[j], "ctx", 1)
-    return [blocks[j] for j in range(size)]
+    return [values] + [swap(values, "ctx", j) for j in range(2, size, 2)]
+
+
+def gather_near(far):
+    return [block for own in far for block in (own, swap(own, "ctx", 1))]
+
+
+def together(*trees):
+    return lax.optimization_barrier(trees)
+
+
+def gather_small_ctx(values):
+    stacked = values[None]
+    for bit in bits_of(lax.axis_size("ctx")):
+        stacked = jnp.concatenate([stacked, swap(stacked, "ctx", bit)], axis=0)
+    return stacked
+
+
+def three_parts(values):
+    high = values.astype(BF16)
+    rest = values - high.astype(F32)
+    middle = rest.astype(BF16)
+    return high, middle, (rest - middle.astype(F32)).astype(BF16)
 
 
 def total(values, axes):
@@ -59,29 +76,73 @@
     return (kept.astype(F32) + received.astype(F32)).astype(BF16)
 
 
-def reduce_shard(keep, send, ctx_first):
-    fsdp_steps = [("fsdp", bit) for bit in bits_of(lax.axis_size("fsdp"))[1:]]
-    ctx_steps = [("ctx", bit) for bit in bits_of(lax.axis_size("ctx"))]
-    steps = ctx_steps + fsdp_steps if ctx_first else fsdp_steps + ctx_steps
-    values = joined(keep, swap(send, "fsdp", 1))
-    me = lax.axis_index("ctx")
-    for axis, bit in steps:
-        if axis == "fsdp":
-            values = joined(values[0::2], swap(values[1::2], axis, bit))
-        else:
-            half = values.shape[1] // 2
-            up = (me & bit) != 0
-            low, high = values[:, :half], values[:, half:]
-            values = joined(
-                jnp.where(up, high, low), swap(jnp.where(up, low, high), axis, bit)
-            )
-    for axis, bit in reversed(ctx_steps):
-        other = swap(values, axis, bit)
-        up = (me & bit) != 0
-        values = jnp.concatenate(
-            [jnp.where(up, other, values), jnp.where(up, values, other)], axis=1
-        )
-    return values[0]
+def halves_of(values, bit):
+    half = values.shape[1] // 2
+    up = (lax.axis_index("ctx") & bit) != 0
+    return values[:, :half], values[:, half:], up
+
+
+def fsdp_step(bit):
+    return lambda values: (values[0::2], swap(values[1::2], "fsdp", bit), joined)
+
+
+def scatter_step(bit):
+    def run(values):
+        low, high, up = halves_of(values, bit)
+        return jnp.where(up, high, low), swap(jnp.where(up, low, high), "ctx", bit), joined
+
+    return run
+
+
+def spread_step(bit):
+    def finish(own, other):
+        up = (lax.axis_index("ctx") & bit) != 0
+        return jnp.concatenate([jnp.where(up, other, own), jnp.where(up, own, other)], axis=1)
+
+    return lambda values: (values, swap(values, "ctx", bit), finish)
+
+
+def reduce_steps(ctx_first, turn=0):
+    fsdp_steps = [fsdp_step(bit) for bit in bits_of(lax.axis_size("fsdp"))[1:]]
+    bits = bits_of(lax.axis_size("ctx"))
+    bits = bits[turn:] + bits[:turn]
+    scatter = [scatter_step(bit) for bit in bits]
+    spread = [spread_step(bit) for bit in reversed(bits)]
+    return (scatter + fsdp_steps if ctx_first else fsdp_steps + scatter) + spread
+
+
+def advance(chains, beside=()):
+    begun = [(steps.pop(0)(values) if steps else None, steps, values) for steps, values in chains]
+    received = [step[1] for step, _, _ in begun if step]
+    received, beside = together(received, beside)
+    after = []
+    for step, steps, values in begun:
+        if step:
+            values = step[2](step[0], received.pop(0))
+        after.append((steps, values))
+    return after, beside
+
+
+def fsdp_blocks(blocks):
+    for bit in bits_of(lax.axis_size("fsdp")):
+        blocks = [joined(k, swap(v, "fsdp", bit)) for k, v in zip(blocks[0::2], blocks[1::2])]
+        yield blocks
+
+
+def fsdp_selected(blocks, bit):
+    up = (lax.axis_index("fsdp") & bit) != 0
+    return [
+        joined(jnp.where(up, high, low), swap(jnp.where(up, low, high), "fsdp", bit))
+        for low, high in zip(blocks[0::2], blocks[1::2])
+    ]
+
+
+def side_by_side(values, rows):
+    return jnp.concatenate([values[:rows], values[rows:]], axis=1)
+
+
+def one_above(values, columns):
+    return jnp.concatenate([values[:, :columns], values[:, columns:]], axis=0)
 
 
 def dot(left, right):
@@ -200,11 +261,11 @@
 
 def forward_kernel(scal, *refs, tiles, groups, ctx, features):
     ends = refs[: ctx - 1]
-    (
-        log_ref, scale_ref, s_ref, step_ref, xs_ref, gate_ref, b_ref, c_ref, weight_ref, tokens_ref, teacher_ref,
-        ssm_ref, branch_ref, hidden_ref, start_ref, out_ref, gout_ref, dout_ref, square_ref,
-        drive_ref, read_ref, acc_ref,
-    ) = refs[ctx - 1 :]
+    log_ref, s_ref, step_ref, xs_ref, gate_ref, b_ref, cdiag_ref, weight_ref = refs[ctx - 1 : ctx + 7]
+    rest = refs[ctx + 7 :]
+    scale_ref, tokens_ref, teacher_ref = rest[:3]
+    ssm_ref, branch_ref, hidden_ref, start_ref, out_ref, gout_ref, dout_ref, square_ref = rest[3:11]
+    drive_ref, read_ref, odd_ref, even_ref, acc_ref = rest[11:]
     piece = groups * 8
     width = tiles * LANES
     states = b_ref.shape[2]
@@ -220,24 +281,43 @@
             held.append(carried(ends, log_ref, rates[j], h, ctx, states, tile_cols(j)))
             start_ref[h, :, tile_cols(j)] = held[-1]
 
-    def body(t, held):
+    def scan(t, held, keep_ref):
         held = list(held)
-        for s in range(8):
-            p = t * 8 + s
+        for s in range(16):
+            p = t * 16 + s
             for h in range(2):
                 b = b_ref[h, p]
-                c = c_ref[h, p]
                 for j in range(tiles):
-                    step = step_ref[h, t, s : s + 1, tile_cols(j)]
-                    drive = drive_ref[h, t, s : s + 1, tile_cols(j)]
+                    cols = tile_cols(j)
+                    step = step_ref[h, t * 2 + s // 8, s % 8 : s % 8 + 1, cols]
+                    drive = drive_ref[h, t * 2 + s // 8, s % 8 : s % 8 + 1, cols]
                     k = h * tiles + j
-                    now = jnp.exp2(step * rates[j]) * held[k] + drive * b
-                    held[k] = now
-                    hidden_ref[j, h, p] = now.astype(BF16)
-                    read_ref[h, t, s : s + 1, tile_cols(j)] = jnp.sum(now * c, axis=0, keepdims=True)
+                    held[k] = jnp.exp2(step * rates[j]) * held[k] + drive * b
+                    low = held[k].astype(BF16)
+                    hidden_ref[j, h, p] = low
+                    keep_ref[h, j, s * states : (s + 1) * states, :] = low
         return tuple(held)
 
-    lax.fori_loop(0, groups, body, tuple(held))
+    def read(t, keep_ref):
+        for h in range(2):
+            for j in range(tiles):
+                out = dot(cdiag_ref[h, t], keep_ref[h, j])
+                read_ref[h, t * 2, :, tile_cols(j)] = out[0:8]
+                read_ref[h, t * 2 + 1, :, tile_cols(j)] = out[8:16]
+
+    def body(k, held):
+        t = 2 * k + 1
+        read(t - 1, even_ref)
+        held = scan(t, held, odd_ref)
+        read(t, odd_ref)
+        return scan(t + 1, held, even_ref)
+
+    blocks = groups // 2
+    held = scan(0, held, even_ref)
+    held = lax.fori_loop(0, blocks // 2 - 1, body, held)
+    read(blocks - 2, even_ref)
+    scan(blocks - 1, held, odd_ref)
+    read(blocks - 1, odd_ref)
     branches = []
     for h in range(2):
         ssm = read_ref[h].reshape(piece, width) + head[6:7] * xs_ref[h].astype(F32)
@@ -340,69 +420,97 @@
 def backward_kernel(scal, *refs, tiles, groups, ctx, rank):
     grads = refs[: ctx - 1]
     (
-        log_ref, proj_ref, s_ref, step_ref, xs_ref, b_ref, c_ref, start_ref, dssm_ref, hidden_ref,
+        log_ref, proj_ref, s_ref, step_ref, xs_ref, c_ref, bdiag_ref, start_ref, dssm_ref, hidden_ref,
         dxs_ref, small_ref, ddelta_ref, db_ref, dc_ref,
-        drive_ref, adj_ref, dstep_ref,
+        adj_ref, dstep_ref, dbs_ref, dcs_ref, adj_odd, adj_even, term_odd, term_even,
     ) = refs[ctx - 1 :]
     piece = groups * 8
     width = tiles * LANES
-    states = b_ref.shape[2]
+    states = c_ref.shape[2]
+    blocks = groups // 2
     i = pl.program_id(0)
     head = s_ref[0:HEAD, :].astype(F32)
-    for h in range(2):
-        drive_ref[h] = step_ref[h] * xs_ref[h].astype(F32).reshape(groups, 8, width)
 
     @pl.when(i == 0)
     def clear():
-        db_ref[...] = jnp.zeros_like(db_ref)
-        dc_ref[...] = jnp.zeros_like(dc_ref)
+        dbs_ref[...] = jnp.zeros_like(dbs_ref)
+        dcs_ref[...] = jnp.zeros_like(dcs_ref)
         ddelta_ref[...] = jnp.zeros_like(ddelta_ref)
 
     rate = -jnp.exp(s_ref[80 : 80 + states, :].astype(F32))
     rates = [rate[:, tile_cols(j)] for j in range(tiles)]
     rates2 = [values * LOG2E for values in rates]
-
-    def one(t, s, p, first, later, sums):
+    row16 = lax.broadcasted_iota(jnp.int32, (16, 16 * states), 0)
+    col16 = lax.broadcasted_iota(jnp.int32, (16, 16 * states), 1)
+    same = (col16 // states == row16).astype(F32)
+    same_low = same.astype(BF16)
+
+    def scan(t, first, later, sums, adj_keep, term_keep):
         for h in range(2):
-            b = b_ref[h, p]
-            c = c_ref[h, p]
+            for s in range(15, -1, -1):
+                p = t * 16 + s
+                c = c_ref[h, p]
+                for j in range(tiles):
+                    cols = tile_cols(j)
+                    step = step_ref[h, t * 2 + s // 8, s % 8 : s % 8 + 1, cols]
+                    dssm = dssm_ref[h, t * 2 + s // 8, s % 8 : s % 8 + 1, cols]
+                    k = h * tiles + j
+                    if first and s == 0:
+                        before = start_ref[h, :, cols]
+                    else:
+                        before = hidden_ref[j, h, p - 1].astype(F32)
+                    adjoint = dssm * c + later[k]
+                    later[k] = jnp.exp2(step * rates2[j]) * adjoint
+                    term = later[k] * before
+                    sums[j] = sums[j] + term * step
+                    place = slice(s * states, (s + 1) * states)
+                    adj_keep[h, j, place, :] = adjoint.astype(BF16)
+                    term_keep[h, j, place, :] = (term * rates[j]).astype(BF16)
+
+    def products(t, adj_keep, term_keep):
+        for h in range(2):
             db = dc = None
             for j in range(tiles):
                 cols = tile_cols(j)
-                step = step_ref[h, t, s : s + 1, cols]
-                drive = drive_ref[h, t, s : s + 1, cols]
-                dssm = dssm_ref[h, t, s : s + 1, cols]
-                k = h * tiles + j
-                hidden = hidden_ref[j, h, p].astype(F32)
-                before = start_ref[h, :, cols] if first else hidden_ref[j, h, p - 1].astype(F32)
-                adjoint = dssm * c + later[k]
-                later[k] = jnp.exp2(step * rates2[j]) * adjoint
-                term = later[k] * before
-                sums[j] = sums[j] + term * step
-                dstep_ref[h, t, s : s + 1, cols] = jnp.sum(term * rates[j], axis=0, keepdims=True)
-                adj_ref[h, t, s : s + 1, cols] = jnp.sum(adjoint * b, axis=0, keepdims=True)
-                db = adjoint * drive if db is None else db + adjoint * drive
-                dc = dssm * hidden if dc is None else dc + dssm * hidden
-            db_ref[h, p] += db
-            dc_ref[h, p] += dc
+                adjoint = adj_keep[h, j]
+                out = dot(bdiag_ref[h, t], adjoint)
+                adj_ref[h, t * 2, :, cols] = out[0:8]
+                adj_ref[h, t * 2 + 1, :, cols] = out[8:16]
+                out = dot(same_low, term_keep[h, j])
+                dstep_ref[h, t * 2, :, cols] = out[0:8]
+                dstep_ref[h, t * 2 + 1, :, cols] = out[8:16]
+                step = step_ref[h, pl.ds(t * 2, 2), :, cols].reshape(16, LANES)
+                dssm = dssm_ref[h, pl.ds(t * 2, 2), :, cols].reshape(16, LANES)
+                drive = (step * xs_ref[h, pl.ds(t * 16, 16), cols].astype(F32)).astype(BF16)
+                hidden = hidden_ref[j, h, pl.ds(t * 16, 16)].reshape(16 * states, LANES)
+                db_now = back_dot(drive, adjoint)
+                dc_now = back_dot(dssm.astype(BF16), hidden)
+                db = db_now if db is None else db + db_now
+                dc = dc_now if dc is None else dc + dc_now
+            dbs_ref[h, t] += db
+            dcs_ref[h, t] += dc
 
     def body(k, both):
         later, sums = list(both[: 2 * tiles]), list(both[2 * tiles :])
-        t = groups - 1 - k
-        for s in range(7, -1, -1):
-            one(t, s, t * 8 + s, False, later, sums)
+        t = blocks - 2 - 2 * k
+        products(t + 1, adj_odd, term_odd)
+        scan(t, False, later, sums, adj_even, term_even)
+        products(t, adj_even, term_even)
+        scan(t - 1, False, later, sums, adj_odd, term_odd)
         return tuple(later + sums)
 
-    later = tuple(
+    later = [
         carried(grads, log_ref, rates2[j], h, ctx, states, tile_cols(j))
         for h in range(2)
         for j in range(tiles)
-    )
-    zero = jnp.zeros((states, LANES), F32)
-    both = lax.fori_loop(0, groups - 1, body, later + (zero,) * tiles)
+    ]
+    sums = [jnp.zeros((states, LANES), F32)] * tiles
+    scan(blocks - 1, False, later, sums, adj_odd, term_odd)
+    both = lax.fori_loop(0, blocks // 2 - 1, body, tuple(later + sums))
     later, sums = list(both[: 2 * tiles]), list(both[2 * tiles :])
-    for s in range(7, -1, -1):
-        one(0, s, s, s == 0, later, sums)
+    products(1, adj_odd, term_odd)
+    scan(0, True, later, sums, adj_even, term_even)
+    products(0, adj_even, term_even)
     for j in range(tiles):
         small_ref[rank : rank + states, tile_cols(j)] = sums[j] * rates[j]
     delta = proj_ref[:, 0:rank].astype(BF16)
@@ -423,22 +531,32 @@
     small_ref[0:rank, :] = rows_dot(delta, low)
     ddelta_ref[...] += back_dot(low, s_ref[HEAD : HEAD + rank, :])
 
+    @pl.when(i == pl.num_programs(0) - 1)
+    def last():
+        for h in range(2):
+            for t in range(blocks):
+                db_ref[h, t : t + 1, :] = jnp.sum(dbs_ref[h, t] * same, axis=0, keepdims=True)
+                dc_ref[h, t : t + 1, :] = jnp.sum(dcs_ref[h, t] * same, axis=0, keepdims=True)
+
 
 def tail_kernel(
-    scal, dproj_ref, s_ref, dxs_ref, conv_ref, x_ref, xs_ref, normed_ref, *refs, count, piece
+    scal, dproj_ref, s_ref, dlow_ref, dhigh_ref, conv_ref, x_ref, xs_ref, normed_ref, before_ref, *refs,
+    count, piece, is_upper
 ):
-    weights, (small_ref, keep_ref, send_ref, dnormed_ref, pad_ref) = refs[:count], refs[count:]
-    depth = weights[0].shape[0]
+    weights, (small_ref, keep_ref, send_ref, dnormed_ref, pad_ref) = refs[: 2 * count], refs[2 * count :]
+    half = weights[0].shape[0]
+    depth = 2 * half
     width = weights[0].shape[1]
     ext = HALO + piece
 
     @pl.when(pl.program_id(0) == 0)
     def clear():
-        dnormed_ref[...] = jnp.zeros_like(dnormed_ref)
+        dnormed_ref[...] = before_ref[...]
         for h in range(2):
             pad_ref[h, 0:HALO, :] = jnp.zeros((HALO, width), F32)
             pad_ref[h, ext : ext + 8, :] = jnp.zeros((8, width), F32)
 
+    upper = is_upper(pl.program_id(0), scal)
     head = s_ref[0:HEAD, :].astype(F32)
     small_ref[8:104, :] = rows_dot(dproj_ref[...], xs_ref[...].reshape(2 * piece, width))
     d_xs = dot(dproj_ref[...], s_ref[96:192, :])
@@ -447,7 +565,8 @@
     for h in range(2):
         conv = conv_ref[h]
         sig = sigmoid(conv)
-        d_conv = (dxs_ref[h] + d_xs[h * piece : (h + 1) * piece]) * (sig * (1.0 + conv * (1.0 - sig)))
+        dxs = jnp.where(upper, dhigh_ref[h], dlow_ref[h])
+        d_conv = (dxs + d_xs[h * piece : (h + 1) * piece]) * (sig * (1.0 + conv * (1.0 - sig)))
         pad_ref[h, HALO:ext, :] = d_conv
         x = x_ref[h].astype(F32)
         for k in range(4):
@@ -464,7 +583,8 @@
         cols = slice(r * depth, (r + 1) * depth)
         target = send_ref if r % 2 else keep_ref
         target[r // 2] = rows_dot(normed_ref[:, cols], low).astype(BF16)
-        dnormed_ref[:, cols] += back_dot(low, weights[r][...])
+    for r in range(2 * count):
+        dnormed_ref[:, r * half : (r + 1) * half] += back_dot(low, weights[r][...])
 
 
 def shape(dims, dtype=F32):
@@ -551,6 +671,14 @@
     lower = pair_owner[jnp.maximum(pair_id - 1, 0)] ^ me_ctx
     upper = pair_owner[jnp.minimum(pair_id + 1, ctx - 1)] ^ me_ctx
 
+    own_rows = tokens[0]
+    valid_slots = jnp.minimum(lengths[0], 2 * ctx * piece)
+    coded = jnp.concatenate([valid_slots // 128, valid_slots % 128]).astype(BF16)[None]
+    first, second = jnp.split(in_proj[:, :width], 2, axis=0)
+    x_first = gather_fsdp(first)
+    second, coded, last_rows, _ = lax.optimization_barrier(
+        (second, coded, own_rows.reshape(2, piece, features)[:, piece - 3 :], x_first[fsdp // 2])
+    )
     rows_head = jnp.concatenate(
         [
             conv_weight,
@@ -558,7 +686,8 @@
             dt_bias[None],
             skip_scale[None],
             jnp.pad(norm_gain, (0, part - depth))[None],
-            jnp.zeros((HEAD - 8, part), BF16),
+            jnp.pad(coded, ((0, 0), (0, part - 4))),
+            jnp.zeros((HEAD - 9, part), BF16),
             dt_proj,
             a_log,
             x_proj.T,
@@ -568,9 +697,10 @@
     small_blocks = gather_fsdp(rows_head)
     small = jnp.concatenate(small_blocks, axis=1)
     gain = jnp.concatenate([block[7, :depth] for block in small_blocks]).astype(F32)
-    x_blocks = gather_fsdp(in_proj[:, :width])
-    gate_blocks = gather_fsdp(after(in_proj[:, width:], x_blocks[-2]))
-    out_blocks = gather_fsdp(after(out_proj, gate_blocks[-2]))
+    x_second = gather_fsdp(second)
+    x_blocks = [piece_now for pair in zip(x_first, x_second) for piece_now in pair]
+    gate_blocks = gather_fsdp(after(in_proj[:, width:], x_second[fsdp // 2]))
+    out_blocks = gather_fsdp(after(out_proj, gate_blocks[fsdp // 2]))
 
     def to_blocks(values, size):
         axis = values.ndim - 1
@@ -582,9 +712,8 @@
             axis=axis,
         )
 
-    own_rows = tokens[0]
     token_rel = to_blocks(own_rows, depth).reshape(2, piece, features)
-    tails = jnp.stack(gather_ctx(to_blocks(own_rows.reshape(2, piece, features)[:, piece - 3 :], depth)))
+    tails = gather_small_ctx(to_blocks(last_rows, depth))
     before_rows = jnp.stack([tails[lower, 0], tails[upper, 1]])
     before_rows = jnp.where(has_before[:, None, None], before_rows, jnp.zeros_like(before_rows))
     rows_ext = jnp.concatenate(
@@ -593,7 +722,8 @@
     inv_rms = lax.rsqrt(jnp.mean(rows_ext * rows_ext, axis=2, keepdims=True) + EPSILON)
     normed = (rows_ext * inv_rms * gain).astype(BF16).reshape(2 * ext, features)
 
-    count = total(jnp.sum(jnp.minimum(lengths, 2 * ctx * piece)).astype(F32)[None], ("fsdp",))
+    codes = jnp.stack([block[8, :4] for block in small_blocks]).astype(F32)
+    count = jnp.sum(codes[:, 0:2] * 128.0 + codes[:, 2:4])
     scale = ((fsdp * rows_all * ctx) / count).reshape(1, 1)
 
     def cols_at(block):
@@ -612,10 +742,11 @@
     cb = min(256, part)
     steps = width // cb
     weight_specs = [pl.BlockSpec((depth, cb), cols_at(cb)) for _ in range(fsdp)]
+    half_specs = [pl.BlockSpec((depth // 2, cb), cols_at(cb)) for _ in range(2 * fsdp)]
     x_ext, conv, xs, proj = call(
-        functools.partial(input_kernel, count=fsdp, piece=piece),
+        functools.partial(input_kernel, count=2 * fsdp, piece=piece),
         "inputs", steps, scal, (normed, *x_blocks, small),
-        [whole_spec((2 * ext, features)), *weight_specs, spec_small(cb)],
+        [whole_spec((2 * ext, features)), *half_specs, spec_small(cb)],
         [
             pl.BlockSpec((2, ext, cb), lambda i, scal: (0, 0, i)),
             spec_rows(cb),
@@ -636,61 +767,65 @@
 
     tiles = 4
     block = tiles * LANES
+    half = width // 2
+    per_half = half // block
+    group_spec = spec_groups(block)
+    state_row = pl.BlockSpec((2 * states, block), lambda i, scal: (0, i))
+    log_spec = pl.BlockSpec((2 * ctx, block), lambda i, scal: (0, i))
+    row_spec = whole_spec((rows_all, features))
+    wide_spec = whole_spec(wide_dims)
+    diag_spec = whole_spec((2, piece // 16, 16, 16 * states))
+    hidden_spec = pl.BlockSpec((tiles, 2, piece, states, LANES), lambda i, scal: (i, 0, 0, 0, 0))
+    start_spec = pl.BlockSpec((2, states, block), lambda i, scal: (0, 0, i))
+    keep_spaces = [pltpu.VMEM((2, tiles, 16 * states, LANES), BF16)]
+    group_space = pltpu.VMEM((2, groups, 8, block), F32)
+
     step, ends, logs = call(
         functools.partial(end_kernel, tiles=tiles, groups=groups, rank=rank),
         "end_states", width // block, scal, (proj, small, xs, b_wide),
-        [whole_spec(proj.shape), spec_small(block), spec_rows(block), whole_spec(wide_dims)],
-        [
-            spec_groups(block),
-            pl.BlockSpec((2 * states, block), lambda i, scal: (0, i)),
-            pl.BlockSpec((2, block), lambda i, scal: (0, i)),
-        ],
+        [whole_spec(proj.shape), spec_small(block), spec_rows(block), wide_spec],
+        [group_spec, state_row, pl.BlockSpec((2, block), lambda i, scal: (0, i))],
         [shape((2, groups, 8, width)), shape((2 * states, width), BF16), shape((2, width))],
-        [pltpu.VMEM((2, groups, 8, block), F32)], 5 * elements, elements,
-    )
-    log_hi = logs.astype(BF16)
-    log_mid = (logs - log_hi.astype(F32)).astype(BF16)
-    log_lo = (logs - log_hi.astype(F32) - log_mid.astype(F32)).astype(BF16)
-    sent = jnp.concatenate([ends, log_hi, log_mid, log_lo, jnp.zeros((2, width), BF16)], axis=0)
-    end_blocks = gather_ctx(sent)
-    log_parts = jnp.stack([b[2 * states : 2 * states + 6] for b in end_blocks]).astype(F32)
-    log_all = log_parts[:, 0:2] + log_parts[:, 2:4] + log_parts[:, 4:6]
-
-    def spans(inside, wanted):
-        summed = jnp.sum(
-            jnp.where(inside[..., None], log_all.transpose(1, 0, 2)[:, None], 0.0), axis=2
-        )
-        return jnp.where(wanted[..., None], summed, 1e30).reshape(2 * ctx, width)
-
-    log_before = spans(between, before)
-    log_behind = spans(between_back, behind)
-
-    c_wide = jnp.broadcast_to(maps[:, :, states:], wide_dims)
+        [group_space], 5 * elements, elements,
+    )
+    sent = jnp.concatenate([ends, *three_parts(logs), jnp.zeros((2, width), BF16)], axis=0)
+
+    def diagonal(values):
+        values = values.reshape(2, piece // 16, 1, 16, states).astype(BF16)
+        same = jnp.eye(16, dtype=BF16)[None, None, :, :, None]
+        return (values * same).reshape(2, piece // 16, 16, 16 * states)
+
+    far = gather_far(sent)
     (gate,) = call(
         functools.partial(gate_kernel, count=fsdp, piece=piece),
         "gates", steps, scal, (normed, *gate_blocks),
         [whole_spec((2 * ext, features)), *weight_specs], [spec_rows(cb)],
         [shape((2, piece, width))], [], 2 * rows_all * features * width,
     )
+    far, gate = together(far, gate)
+    near = gather_near(far)
+    c_wide = jnp.broadcast_to(maps[:, :, states:], wide_dims)
+    b_diag = diagonal(maps[:, :, :states])
+    c_diag = diagonal(maps[:, :, states:])
     weight_out = jnp.concatenate(out_blocks, axis=0)
-
-    tiles = 2
-    block = tiles * LANES
-    end_spec = pl.BlockSpec((2 * states, block), lambda i, scal: (0, i))
-    log_spec = pl.BlockSpec((2 * ctx, block), lambda i, scal: (0, i))
-    hidden_spec = pl.BlockSpec((tiles, 2, piece, states, LANES), lambda i, scal: (i, 0, 0, 0, 0))
-    start_spec = pl.BlockSpec((2, states, block), lambda i, scal: (0, 0, i))
-    out_spec = pl.BlockSpec((block, features), lambda i, scal: (i, 0))
-    row_spec = whole_spec((rows_all, features))
+    near, c_wide, b_diag, c_diag, weight_out = together(near, c_wide, b_diag, c_diag, weight_out)
+    parts = jnp.stack([b[2 * states : 2 * states + 6] for b in near]).astype(F32)
+    logs = (parts[:, 0:2] + parts[:, 2:4] + parts[:, 4:6]).transpose(1, 0, 2)
+
+    def spans(inside, wanted):
+        summed = jnp.sum(jnp.where(inside[..., None], logs[:, None], 0.0), axis=2)
+        return jnp.where(wanted[..., None], summed, 1e30).reshape(2 * ctx, width)
+
     ssm, branch, hidden, starts, out_low, g_out, d_out, squares = call(
         functools.partial(forward_kernel, tiles=tiles, groups=groups, ctx=ctx, features=features),
         "forward_states", width // block, scal,
-        (*end_blocks[1:], log_before, scale, small, step, xs, gate, b_wide, c_wide, weight_out,
-         own_rows, teacher[0]),
+        (*near[1:], spans(between, before), small, step, xs, gate, b_wide, c_diag, weight_out,
+         scale, own_rows, teacher[0]),
         [
-            *([end_spec] * (ctx - 1)), log_spec, pl.BlockSpec(memory_space=pltpu.SMEM),
-            spec_small(block), spec_groups(block), spec_rows(block), spec_rows(block),
-            whole_spec(wide_dims), whole_spec(wide_dims), out_spec, row_spec, row_spec,
+            *([state_row] * (ctx - 1)), log_spec, spec_small(block), group_spec, spec_rows(block),
+            spec_rows(block), wide_spec, diag_spec,
+            pl.BlockSpec((block, features), lambda i, scal: (i, 0)),
+            pl.BlockSpec(memory_space=pltpu.SMEM), row_spec, row_spec,
         ],
         [
             spec_rows(block), spec_rows(block), hidden_spec, start_spec, row_spec, row_spec, row_spec,
@@ -706,27 +841,18 @@
             shape((rows_all, features), BF16),
             shape((8, features)),
         ],
-        [
-            pltpu.VMEM((2, groups, 8, block), F32),
-            pltpu.VMEM((2, groups, 8, block), F32),
-            pltpu.VMEM((rows_all, features), F32),
-        ],
+        [group_space] * 2 + keep_spaces * 2 + [pltpu.VMEM((rows_all, features), F32)],
         10 * elements, elements,
     )
-    tiles = 4
-    block = tiles * LANES
-    d_ssm, d_gate, grad_skip, first_grads = call(
+    d_ssm, d_gate, grad_skip, grads_first = call(
         functools.partial(first_grad_kernel, tiles=tiles, groups=groups),
         "first_grads", width // block, scal,
         (d_out, weight_out, small, step, xs, gate, ssm, c_wide),
         [
             row_spec, pl.BlockSpec((block, features), lambda i, scal: (i, 0)), spec_small(block),
-            spec_groups(block), spec_rows(block), spec_rows(block), spec_rows(block), whole_spec(wide_dims),
+            group_spec, spec_rows(block), spec_rows(block), spec_rows(block), wide_spec,
         ],
-        [
-            spec_groups(block), spec_rows(block), pl.BlockSpec((1, block), lambda i, scal: (0, i)),
-            pl.BlockSpec((2 * states, block), lambda i, scal: (0, i)),
-        ],
+        [group_spec, spec_rows(block), pl.BlockSpec((1, block), lambda i, scal: (0, i)), state_row],
         [
             shape((2, groups, 8, width)),
             shape((2, piece, width), BF16),
@@ -735,9 +861,23 @@
         ],
         [], 6 * elements, elements,
     )
-    grad_blocks = gather_ctx(first_grads)
+    back_far = gather_far(grads_first)
 
     pairs = fsdp // 2
+    half_blocks = half // cb
+    pair_spec = pl.BlockSpec((pairs, depth, cb), lambda i, scal: (0, 0, i))
+    pair_at = pl.BlockSpec((pairs, depth, cb), lambda i, scal: (0, 0, cols_at(cb)(i, scal)[1]))
+    keep_gate, send_gate, d_normed_gate = call(
+        functools.partial(gate_grad_kernel, count=fsdp, piece=piece),
+        "gate_grads", steps, scal, (normed, d_gate, *gate_blocks),
+        [whole_spec((2 * ext, features)), spec_rows(cb), *weight_specs],
+        [pair_at, pair_at, row_spec],
+        [shape((pairs, depth, width), BF16)] * 2 + [shape((rows_all, features))],
+        [], 4 * rows_all * features * width,
+    )
+    back_far, keep_gate, send_gate = together(back_far, keep_gate, send_gate)
+    back_near = gather_near(back_far)
+    got_gate = swap(send_gate, "fsdp", 1)
     subs = part // cb
     branch_rows = branch.reshape(rows_all, width)
     keep_out, send_out = pl.pallas_call(
@@ -756,151 +896,207 @@
             flops=2 * rows_all * width * features, bytes_accessed=9 * 2**20, transcendentals=0
         ),
     )(branch_rows, branch_rows, d_out)
-    pair_spec = pl.BlockSpec((pairs, depth, cb), lambda i, scal: (0, 0, i))
-    pair_at = pl.BlockSpec(
-        (pairs, depth, cb), lambda i, scal: (0, 0, cols_at(cb)(i, scal)[1])
-    )
-    keep_gate, send_gate, d_normed_gate = call(
-        functools.partial(gate_grad_kernel, count=fsdp, piece=piece),
-        "gate_grads", steps, scal, (normed, d_gate, *gate_blocks),
-        [whole_spec((2 * ext, features)), spec_rows(cb), *weight_specs],
-        [pair_at, pair_at, row_spec],
-        [shape((pairs, depth, width), BF16)] * 2 + [shape((rows_all, features))],
-        [], 4 * rows_all * features * width,
-    )
-    sum_out = reduce_shard(keep_out, send_out, False)
-    sum_gate = reduce_shard(keep_gate, send_gate, True)
-
-    tiles = 2
-    block = tiles * LANES
-    d_xs, small_back, d_delta, db_wide, dc_wide = call(
-        functools.partial(backward_kernel, tiles=tiles, groups=groups, ctx=ctx, rank=rank),
-        "backward_states", width // block, scal,
-        (*grad_blocks[1:], log_behind, proj, small, step, xs, b_wide, c_wide, starts, d_ssm, hidden),
-        [
-            *([end_spec] * (ctx - 1)), log_spec, whole_spec(proj.shape), spec_small(block),
-            spec_groups(block), spec_rows(block), whole_spec(wide_dims), whole_spec(wide_dims),
-            start_spec, spec_groups(block), hidden_spec,
-        ],
-        [
-            spec_rows(block), pl.BlockSpec((rank + states + 8, block), lambda i, scal: (0, i)),
-            whole_spec((rows_all, rank)), whole_spec(wide_dims), whole_spec(wide_dims),
-        ],
-        [
-            shape((2, piece, width)),
-            shape((rank + states + 8, width)),
-            shape((rows_all, rank)),
-            shape(wide_dims),
-            shape(wide_dims),
-        ],
-        [pltpu.VMEM((2, groups, 8, block), F32)] * 3,
-        24 * elements, elements,
-    )
+    got_gate, keep_out, send_out = together(got_gate, keep_out, send_out)
+    got_out = swap(send_out, "fsdp", 1)
+    core_gate = joined(keep_gate, got_gate)
+    back_near, got_out, core_gate = together(back_near, got_out, core_gate)
+    chains = [(reduce_steps(False), joined(keep_out, got_out)), (reduce_steps(True, 1), core_gate)]
+    log_behind = spans(between_back, behind)
+
+    def backward(c):
+        def at(i):
+            return i + c * per_half
+
+        return call(
+            functools.partial(backward_kernel, tiles=tiles, groups=groups, ctx=ctx, rank=rank),
+            "backward_states", per_half, scal,
+            (*back_near[1:], log_behind, proj, small, step, xs, c_wide, b_diag, starts, d_ssm, hidden),
+            [
+                *([pl.BlockSpec((2 * states, block), lambda i, scal: (0, at(i)))] * (ctx - 1)),
+                pl.BlockSpec((2 * ctx, block), lambda i, scal: (0, at(i))),
+                whole_spec(proj.shape), spec_small(block, c * per_half),
+                pl.BlockSpec((2, groups, 8, block), lambda i, scal: (0, 0, 0, at(i))),
+                spec_rows(block, c * per_half), wide_spec, diag_spec,
+                pl.BlockSpec((2, states, block), lambda i, scal: (0, 0, at(i))),
+                pl.BlockSpec((2, groups, 8, block), lambda i, scal: (0, 0, 0, at(i))),
+                pl.BlockSpec((tiles, 2, piece, states, LANES), lambda i, scal: (at(i), 0, 0, 0, 0)),
+            ],
+            [
+                spec_rows(block), pl.BlockSpec((rank + states + 8, block), lambda i, scal: (0, i)),
+                whole_spec((rows_all, rank)),
+                whole_spec((2, piece // 16, 16 * states)), whole_spec((2, piece // 16, 16 * states)),
+            ],
+            [
+                shape((2, piece, half)),
+                shape((rank + states + 8, half)),
+                shape((rows_all, rank)),
+                shape((2, piece // 16, 16 * states)),
+                shape((2, piece // 16, 16 * states)),
+            ],
+            [group_space] * 2 + [pltpu.VMEM((2, piece // 16, 16, 16 * states), F32)] * 2 + keep_spaces * 4,
+            16 * elements // 2, elements // 2,
+        )
+
+    chains, back_first = advance(chains, backward(0))
+    step, _ = together(step, [values for _, values in chains])
+    chains, back_second = advance(chains, backward(1))
+
+    def small_part(c, back):
+        rows = jnp.concatenate(
+            [back[1], grad_skip[:, c * half : (c + 1) * half], jnp.zeros((7, half), F32)], axis=0
+        ).astype(BF16)
+        return [rows[:, k * part : (k + 1) * part] for k in range(fsdp // 2)]
+
     d_proj = jnp.concatenate(
         [
-            d_delta,
-            jnp.sum(db_wide, axis=3).reshape(rows_all, states),
-            jnp.sum(dc_wide, axis=3).reshape(rows_all, states),
+            back_first[2] + back_second[2],
+            (back_first[3] + back_second[3]).reshape(rows_all, states),
+            (back_first[4] + back_second[4]).reshape(rows_all, states),
         ],
         axis=1,
     ).astype(BF16)
     half_steps = steps // 2
-    halves = []
-    for side in range(2):
-        base = side * half_steps
-
-        def place(i, scal, base=base):
+
+    def tail(c, d_proj, d_before):
+        base = c * half_steps
+
+        def place(i, scal):
             return cols_at(cb)(i + base, scal)[1]
 
         def at_rows(dims):
-            return pl.BlockSpec((2, dims, cb), lambda i, scal, place=place: (0, 0, place(i, scal)))
-
-        def at_cols(i, scal, base=base):
-            return 0, i + base
-
-        halves.append(
-            call(
-                functools.partial(tail_kernel, count=fsdp, piece=piece),
-                "tail_grads", half_steps, scal,
-                (d_proj, small, d_xs, conv, x_ext, xs, normed, *x_blocks),
+            return pl.BlockSpec((2, dims, cb), lambda i, scal: (0, 0, place(i, scal)))
+
+        return call(
+            functools.partial(
+                tail_kernel, count=fsdp, piece=piece,
+                is_upper=lambda i, scal: place(i, scal) >= half_blocks,
+            ),
+            "tail_grads", half_steps, scal,
+            (d_proj, small, back_first[0], back_second[0], conv, x_ext, xs, normed, d_before, *x_blocks),
+            [
+                whole_spec(d_proj.shape),
+                pl.BlockSpec((small.shape[0], cb), lambda i, scal: (0, place(i, scal))),
+                pl.BlockSpec(
+                    (2, piece, cb), lambda i, scal: (0, 0, jnp.minimum(place(i, scal), half_blocks - 1))
+                ),
+                pl.BlockSpec(
+                    (2, piece, cb), lambda i, scal: (0, 0, jnp.maximum(place(i, scal) - half_blocks, 0))
+                ),
+                at_rows(piece), at_rows(ext), at_rows(piece),
+                whole_spec((2 * ext, features)), whole_spec((2 * ext, features)),
+                *([pl.BlockSpec((depth // 2, cb), lambda i, scal: (0, i + base))] * (2 * fsdp)),
+            ],
+            [
+                pl.BlockSpec((104, cb), lambda i, scal: (0, i)),
+                pair_spec, pair_spec, whole_spec((2 * ext, features)),
+            ],
+            [
+                shape((104, half)),
+                shape((pairs, depth, half), BF16),
+                shape((pairs, depth, half), BF16),
+                shape((2 * ext, features)),
+            ],
+            [pltpu.VMEM((2, ext + 8, cb), F32)],
+            4 * rows_all * features * half,
+        )
+
+    d_before = jnp.pad(
+        d_normed_gate.reshape(2, piece, features), ((0, 0), (HALO, 0), (0, 0))
+    ).reshape(2 * ext, features)
+    d_proj, d_before, _ = together(d_proj, d_before, [values for _, values in chains])
+    chains, tail_first = advance(chains, tail(0, d_proj, d_before))
+    got_ahead = swap(tail_first[2], "fsdp", 1)
+    small_now = small_part(0, back_first) + small_part(1, back_second)
+    for small_now in fsdp_blocks(small_now):
+        pass
+    d_proj, _ = together(d_proj, [values for _, values in chains])
+    chains, (tail_second, got_ahead, small_now) = advance(
+        chains, (tail(1, d_proj, tail_first[3]), got_ahead, small_now)
+    )
+    ahead = joined(tail_first[1], got_ahead)
+    tail_rows = [
+        values[:, k * part : (k + 1) * part].astype(BF16)
+        for values in (tail_first[0], tail_second[0])
+        for k in range(fsdp // 2)
+    ]
+    lines = small_now[0].shape[0] // 2
+    lines_tail = tail_rows[0].shape[0] // 2
+    got_last = swap(tail_second[2], "fsdp", 1)
+    chains, (got_last, d_ext, squares) = advance(
+        [*chains, (reduce_steps(True), ahead)], (got_last, tail_second[3], squares)
+    )
+    last = joined(tail_second[1], got_last)
+    last_steps = reduce_steps(False)
+    n_fsdp = len(bits_of(fsdp)) - 1
+    for bit in bits_of(fsdp):
+        tail_rows = fsdp_selected(tail_rows, bit)
+    while last_steps:
+        for_last = [([last_steps.pop(0)], last)]
+        chains, tail_rows = advance([*for_last, *chains], tail_rows)
+        last = chains.pop(0)[1]
+        n_fsdp -= 1
+        if n_fsdp == 0:
+            extra = jnp.concatenate(
                 [
-                    whole_spec(d_proj.shape),
-                    pl.BlockSpec((small.shape[0], cb), lambda i, scal, place=place: (0, place(i, scal))),
-                    at_rows(piece), at_rows(piece), at_rows(ext), at_rows(piece),
-                    whole_spec((2 * ext, features)),
-                    *([pl.BlockSpec((depth, cb), at_cols)] * fsdp),
+                    side_by_side(small_now[0], lines),
+                    side_by_side(tail_rows[0], lines_tail),
+                    jnp.zeros((128 - lines - lines_tail, 2 * part), BF16),
                 ],
-                [
-                    pl.BlockSpec((104, cb), lambda i, scal: (0, i)),
-                    pair_spec, pair_spec, whole_spec((2 * ext, features)),
-                ],
-                [
-                    shape((104, width // 2)),
-                    shape((pairs, depth, width // 2), BF16),
-                    shape((pairs, depth, width // 2), BF16),
-                    shape((2 * ext, features)),
-                ],
-                [pltpu.VMEM((2, ext + 8, cb), F32)],
-                4 * rows_all * features * width // 2,
-            )
-        )
-    sum_x = [
-        reduce_shard(side[1], side[2], ctx_first) for side, ctx_first in zip(halves, (False, True))
-    ]
-    tail_small = to_blocks(jnp.concatenate([halves[0][0], halves[1][0]], axis=1), part)
-    d_normed = (halves[0][3] + halves[1][3]).reshape(2, ext, features)
+                axis=0,
+            ).reshape(1, -1, half)
+            last = jnp.concatenate([last, extra], axis=1)
+    while any(steps_left for steps_left, _ in chains):
+        chains, _ = advance(chains)
+    out_now, gate_now, ahead = [values for _, values in chains]
+    sum_x = [ahead[0], last[0, :depth]]
+    extra = last[0, depth:].reshape(128, 2 * part)
+    sum_back = one_above(extra[:lines], part).astype(F32)
+    sum_tail = one_above(extra[lines : lines + lines_tail], part).astype(F32)
+
+    d_normed = d_ext.reshape(2, ext, features)
     halo_grad = d_normed[:, HALO - 3 : HALO]
-    halo_all = jnp.stack(gather_ctx(halo_grad.astype(BF16))).astype(F32)
+    unit = rows_ext * inv_rms
+    grad_gain = jnp.sum(d_normed[:, HALO - 3 :] * unit[:, HALO - 3 :], axis=(0, 1))
+    square = jnp.pad(jnp.stack(three_parts(jnp.sum(squares))), (0, features - 3))
+    halo_sent = jnp.concatenate(
+        [halo_grad.reshape(6, features).astype(BF16), square[None], grad_gain.astype(BF16)[None]]
+    )
+    halo_got = gather_small_ctx(halo_sent).astype(F32)
+    vector = jnp.concatenate(
+        [
+            to_blocks(jnp.sum(halo_got[:, 7], axis=0)[None], depth)[0],
+            jnp.pad(jnp.sum(halo_got[:, 6, 0:3])[None], (0, LANES - 1)),
+        ]
+    )
+    vector = total(vector, ("fsdp",))
+    sum_gain = lax.dynamic_slice_in_dim(vector, me_fsdp * depth, depth)
+    loss = vector[features] / (count * features)
+    halo_all = halo_got[:, 0:6].reshape(ctx, 2, 3, features)
     from_next = jnp.stack([halo_all[upper, 0], halo_all[lower, 1]])
     from_next = jnp.where(has_after[:, None, None], from_next, 0.0)
-    unit = rows_ext * inv_rms
-    own_normed = d_normed[:, HALO:] + d_normed_gate.reshape(2, piece, features)
-    grad_gain = jnp.sum(halo_grad * unit[:, HALO - 3 : HALO], axis=(0, 1)) + jnp.sum(
-        own_normed * unit[:, HALO:], axis=(0, 1)
-    )
-    grad_gain = jnp.pad(grad_gain.reshape(fsdp, 1, depth), ((0, 0), (0, 0), (0, part - depth)))
-    small_rows = jnp.concatenate(
-        [
-            tail_small[0:5],
-            small_back[rank + states : rank + states + 1],
-            grad_skip,
-            grad_gain.transpose(1, 0, 2).reshape(1, width),
-            jnp.zeros((HEAD - 8, width), F32),
-            small_back[0 : rank + states],
-            tail_small[8:104],
-        ],
-        axis=0,
-    ).astype(BF16)
-    small_pairs = small_rows.reshape(small_rows.shape[0], pairs, 2, part).transpose(2, 1, 0, 3)
-    sum_small = reduce_shard(small_pairs[0], small_pairs[1], False).astype(F32)
-
-    own_normed = own_normed + jnp.pad(from_next, ((0, 0), (piece - 3, 0), (0, 0)))
+    own_normed = d_normed[:, HALO:] + jnp.pad(from_next, ((0, 0), (piece - 3, 0), (0, 0)))
     own_inv = inv_rms[:, HALO:]
     own_u = rows_ext[:, HALO:]
     scaled = own_normed * gain
     d_rows = own_inv * scaled - own_u * (own_inv * own_inv * own_inv) * jnp.mean(
         scaled * own_u, axis=2, keepdims=True
     )
-    d_rows = d_rows.reshape(rows_all, features)
-
-    grad_tokens = (to_blocks(d_rows, depth) + g_out)[None]
-    square_total = total(jnp.sum(squares)[None], ("fsdp", "ctx"))[0]
-    loss = square_total / (count[0] * features)
-    grad_in = jnp.concatenate([*sum_x, sum_gate], axis=1).astype(F32)
+    grad_tokens = (to_blocks(d_rows.reshape(rows_all, features), depth) + g_out)[None]
+    grad_in = jnp.concatenate([*sum_x, gate_now[0]], axis=1).astype(F32)
     return (
         out_low[None],
         loss,
         grad_tokens,
-        sum_small[7, :depth],
+        sum_gain,
         grad_in,
-        sum_small[0:4],
-        sum_small[4],
-        sum_small[96:192].T,
-        sum_small[HEAD : HEAD + rank],
-        sum_small[5],
-        sum_small[80 : 80 + states],
-        sum_small[6],
-        sum_out.astype(F32),
+        sum_tail[0:4],
+        sum_tail[4],
+        sum_tail[8:104].T,
+        sum_back[0:rank],
+        sum_back[rank + states],
+        sum_back[rank : rank + states],
+        sum_back[rank + states + 8],
+        out_now[0].astype(F32),
     )
 
 

time: 602 us -> 514 us (0.85)
  waiting for transfers between devices: 168 us -> 105 us
  starting transfers between devices: 91.8 us -> 78.7 us
  other arithmetic: 55.3 us -> 63.4 us
  local copies, waits for them, and re-layouts: 47.2 us -> 39.8 us
  Pallas kernels: 220 us -> 213 us
    ppermute x87 -> x75, waiting for transfers between devices: 168 us -> 105 us  [swap(): return lax.ppermute(values, axis, [(i, i ^ bit) for i in range(size)])]
    ppermute x87 -> x75, starting transfers between devices: 91.8 us -> 78.7 us  [swap(): return lax.ppermute(values, axis, [(i, i ^ bit) for i in range(size)])]
    convert_element_type x25 -> x23, other arithmetic: 8.56 us -> 18.9 us  [joined(): return (kept.astype(F32) + received.astype(F32)).astype(BF16)]
    reduce_sum x7, other arithmetic: 13.8 us -> 3.62 us  [the longest x1 0.71 us: spans(): summed = jnp.sum(jnp.where(inside[..., None], logs[:, None], 0.0), axis=2)]
    unnamed x123 -> x155, local copies, waits for them, and re-layouts: 11.2 us -> 4.48 us
    pallas_call x9 -> x10, Pallas kernels: 214 us -> 207 us  [call(): pl.pallas_call(kernel, grid_spec=pltpu.PrefetchScalarGridSpec(num_scalar_...]
  transfers between devices with their start and end apart: 87 -> 75, of which waited for: 48 -> 25; matrix products, arithmetic and copies ran while one was open for 12% -> 15% of each run, Pallas kernels for 10% -> 30%
where the time goes in v2:
time: 514 us; the launch traced here: 509 us
  Pallas kernels  213 us (41%)
  waiting for transfers between devices  105 us (20%)
  starting transfers between devices  78.7 us (15%)
  other arithmetic  63.4 us (12%)
  local copies, waits for them, and re-layouts  39.8 us (8%)
  between operations  8.71 us (2%)
    pallas_call x10, Pallas kernels, call(): pl.pallas_call(kernel, grid_spec=pltpu.PrefetchScalarGridSpec(num_scalar_...  207 us
    ppermute x75, waiting for transfers between devices, swap(): return lax.ppermute(values, axis, [(i, i ^ bit) for i in range(size)])  105 us
    ppermute x75, starting transfers between devices, swap(): return lax.ppermute(values, axis, [(i, i ^ bit) for i in range(size)])  78.7 us
    convert_element_type x23, other arithmetic, joined(): return (kept.astype(F32) + received.astype(F32)).astype(BF16)  18.9 us
  transfers between devices with their start and end apart: 75, of which 25 were waited for; matrix products, arithmetic and copies ran while one was open for 15% of the time, Pallas kernels for 30%

profile of v2, /device:TPU:0, one launch (start us, length us, event | category | flops | bytes accessed | tf_op | source)
XLA Modules:
  0.0 508.9 jit_solution(5628531582966438194)
XLA Ops:
  8.7 8.4 %collective-permute-done.refs_4_ = bf16[128,2048]{1,0:T(8,128)(2,1)S(1)} collective-permute-done((bf16[128,2048]{1,0:T(8,128)(2,1)S(1)}, bf16[128,2048]{1,0:T(8,128)(2,1)S(1)}, u32[]{:S(2)}, u32[]{:S(2)}) %collective-permute-start) | collective-permute-done | bytes 524320 | tf_op jit(solution)/shard_map/ppermute | solution.py:22
  47.4 17.1 %collective-permute-done.16.refs_2_ = bf16[256,2048]{1,0:T(8,128)(2,1)} collective-permute-done((bf16[256,2048]{1,0:T(8,128)(2,1)}, bf16[256,2048]{1,0:T(8,128)(2,1)}, u32[]{:S(2)}, u32[]{:S(2)}) %collective-permute-start.16) | collective-permute-done | bytes 1048608 | tf_op jit(solution)/shard_map/ppermute | solution.py:22
  72.1 16.3 %inputs.1 = (bf16[2,272,2048]{2,1,0:T(8,128)(2,1)}, f32[2,256,2048]{2,1,0:T(8,128)}, bf16[2,256,2048]{2,1,0:T(8,128)(2,1)}, f32[512,96]{1,0:T(8,128)}) custom-call(s32[3]{0:T(128)} %pad_add_fusion.3.scal, bf16[544,1024]{1,0:T(8,128)(2,1)} %fusion.1.normed_ref, bf16[128,2048]{1,0:T(8,128)(2,1)} %copy-done.7, bf16[128,2048]{1,0:T(8,128)(2,1)} %copy-done.8, ...), custom_call_target="tpu_custom_call" | custom-call | flops 2147483648 | bytes 14811136 | tf_op jit(solution)/shard_map/inputs/pallas_call | solution.py:598
  93.1 19.6 %end_states.1 = (f32[2,32,8,2048]{3,2,1,0:T(8,128)}, bf16[32,2048]{1,0:T(8,128)(2,1)}, f32[2,2048]{1,0:T(2,128)}) custom-call(s32[3]{0:T(128)} %pad_add_fusion.3.scal, f32[512,96]{1,0:T(8,128)} %get-tuple-element.153.proj_ref.refs_8_, bf16[192,2048]{1,0:T(8,128)(2,1)} %pad_maximum_fusion.1.refs_8_.s_ref.refs_9_, ...), custom_call_target="tpu_custom_call" | custom-call | flops 83886080 | bytes 11616256 | tf_op jit(solution)/shard_map/end_states/pallas_call | solution.py:598
  126.5 9.4 %gates.1.refs_11_.gate_ref = f32[2,256,2048]{2,1,0:T(8,128)} custom-call(s32[3]{0:T(128)} %pad_add_fusion.3.scal, bf16[544,1024]{1,0:T(8,128)(2,1)} %fusion.1.normed_ref, bf16[256,2048]{1,0:T(8,128)(2,1)} %slice.330.refs_0_, bf16[256,2048]{1,0:T(8,128)(2,1)} %collective-permute-done.15.refs_1_, bf16[256,2048]{1,0:T(8,128)(2,1)} %collective-permute-done.16.refs_2_, ...), custom_call_target="tpu_custom_call" | custom-call | flops 2147483648 | bytes 9502720 | tf_op jit(solution)/shard_map/gates/pallas_call | solution.py:598
  142.2 3.7 pad_maximum_fusion.refs_14_.weight_ref
  148.8 3.5 collective-permute-done.20.refs_4_
  159.7 35.4 %forward_states.1 = (f32[2,256,2048]{2,1,0:T(8,128)}, bf16[2,256,2048]{2,1,0:T(8,128)(2,1)}, bf16[16,2,256,16,128]{4,3,2,1,0:T(8,128)(2,1)}, f32[2,16,2048]{2,1,...) custom-call(s32[3]{0:T(128)} %pad_add_fusion.3.scal, ...), custom_call_target="tpu_custom_call" | custom-call | flops 167772160 | bytes 67633152 | tf_op jit(solution)/shard_map/forward_states/pallas_call | solution.py:598
  195.1 22.6 %first_grads.1 = (f32[2,32,8,2048]{3,2,1,0:T(8,128)}, bf16[2,256,2048]{2,1,0:T(8,128)(2,1)}, f32[1,2048]{1,0:T(1,128)}, bf16[32,2048]{1,0:T(8,128)(2,1)}) custom-call(s32[3]{0:T(128)} %pad_add_fusion.3.scal, bf16[512,1024]{1,0:T(8,128)(2,1)} %get-tuple-element.176.dout_ref, bf16[2048,1024]{1,0:T(8,128)(2,1)} %pad_maximum_fusion.refs_14_.weight_ref, ...), custom_call_target="tpu_custom_call" | custom-call | flops 100663296 | bytes 31334400 | tf_op jit(solution)/shard_map/first_grads/pallas_call | solution.py:598
  217.7 4.1 collective-permute-start.25
  224.2 12.0 %gate_grads.1 = (bf16[2,256,2048]{2,1,0:T(8,128)(2,1)}, bf16[2,256,2048]{2,1,0:T(8,128)(2,1)}, f32[512,1024]{1,0:T(8,128)}) custom-call(s32[3]{0:T(128)} %pad_add_fusion.3.scal, bf16[544,1024]{1,0:T(8,128)(2,1)} %fusion.1.normed_ref, bf16[2,256,2048]{2,1,0:T(8,128)(2,1)} %get-tuple-element.180.dgate_ref, bf16[256,2048]{1,0:T(8,128)(2,1)} %slice.330.refs_0_, ...), custom_call_target="tpu_custom_call" | custom-call | flops 4294967296 | bytes 13697024 | tf_op jit(solution)/shard_map/gate_grads/pallas_call | solution.py:598
  236.4 5.8 %out_grads.1 = (bf16[2,512,1024]{2,1,0:T(8,128)(2,1)}, bf16[2,512,1024]{2,1,0:T(8,128)(2,1)}) custom-call(bf16[512,2048]{1,0:T(8,128)(2,1)} %bitcast.157, bf16[512,2048]{1,0:T(8,128)(2,1)} %bitcast.158, bf16[512,1024]{1,0:T(8,128)(2,1)} %get-tuple-element.176.dout_ref), custom_call_target="tpu_custom_call" | custom-call | flops 2147483648 | bytes 9437184 | tf_op jit(solution)/shard_map/out_grads/pallas_call | solution.py:883
  264.3 32.2 %backward_states.2 = (f32[2,256,1024]{2,1,0:T(8,128)}, f32[88,1024]{1,0:T(8,128)}, f32[512,64]{1,0:T(8,128)}, f32[2,16,256]{2,1,0:T(8,128)}, f32[2,16,256]{2,1,0:T(8,128)}) custom-call(s32[3]{0:T(128)} %pad_add_fusion.3.scal, bf16[32,2048]{1,0:T(8,128)(2,1)} %copy-done.25, bf16[32,2048]{1,0:T(8,128)(2,1)} %copy-done.22, bf16[32,2048]{1,0:T(8,128)(2,1)} %copy-done.26, ...), custom_call_target="tpu_custom_call" | custom-call | flops 134217728 | bytes 53444608 | tf_op jit(solution)/shard_map/backward_states/pallas_call | solution.py:598
  307.8 3.3 pad.26
  311.2 32.3 %backward_states.3 = (f32[2,256,1024]{2,1,0:T(8,128)}, f32[88,1024]{1,0:T(8,128)}, f32[512,64]{1,0:T(8,128)}, f32[2,16,256]{2,1,0:T(8,128)}, f32[2,16,256]{2,1,0:T(8,128)}) custom-call(s32[3]{0:T(128)} %pad_add_fusion.3.scal, bf16[32,2048]{1,0:T(8,128)(2,1)} %copy-done.25, bf16[32,2048]{1,0:T(8,128)(2,1)} %copy-done.22, bf16[32,2048]{1,0:T(8,128)(2,1)} %copy-done.26, ...), custom_call_target="tpu_custom_call" | custom-call | flops 134217728 | bytes 53444608 | tf_op jit(solution)/shard_map/backward_states/pallas_call | solution.py:598
  355.1 13.6 %tail_grads.2 = (f32[104,1024]{1,0:T(8,128)}, bf16[2,256,1024]{2,1,0:T(8,128)(2,1)}, bf16[2,256,1024]{2,1,0:T(8,128)(2,1)}, f32[544,1024]{1,0:T(8,128)}) custom-call(s32[3]{0:T(128)} %pad_add_fusion.3.scal, bf16[512,96]{1,0:T(8,128)(2,1)} %pad_maximum_fusion.15.dproj_ref, bf16[192,2048]{1,0:T(8,128)(2,1)} %pad_maximum_fusion.1.refs_8_.s_ref.refs_9_, ...), custom_call_target="tpu_custom_call" | custom-call | flops 2147483648 | bytes 25886720 | tf_op jit(solution)/shard_map/tail_grads/pallas_call | solution.py:598
  374.8 13.8 %tail_grads.3 = (f32[104,1024]{1,0:T(8,128)}, bf16[2,256,1024]{2,1,0:T(8,128)(2,1)}, bf16[2,256,1024]{2,1,0:T(8,128)(2,1)}, f32[544,1024]{1,0:T(8,128)}) custom-call(s32[3]{0:T(128)} %pad_add_fusion.3.scal, bf16[512,96]{1,0:T(8,128)(2,1)} %pad_maximum_fusion.15.dproj_ref, bf16[192,2048]{1,0:T(8,128)(2,1)} %pad_maximum_fusion.1.refs_8_.s_ref.refs_9_, ...), custom_call_target="tpu_custom_call" | custom-call | flops 2147483648 | bytes 25886720 | tf_op jit(solution)/shard_map/tail_grads/pallas_call | solution.py:598
  400.8 7.4 %collective-permute-done.48 = bf16[2,128,1024]{2,1,0:T(8,128)(2,1)} collective-permute-done((bf16[2,128,1024]{2,1,0:T(8,128)(2,1)S(1)}, bf16[2,128,1024]{2,1,0:T(8,128)(2,1)}, u32[]{:S(2)}, u32[]{:S(2)}) %collective-permute-start.48) | collective-permute-done | bytes 524320 | tf_op jit(solution)/shard_map/ppermute | solution.py:22
  421.4 7.1 %collective-permute-done.51 = bf16[2,8,1024]{2,1,0:T(8,128)(2,1)S(1)} collective-permute-done((bf16[2,8,1024]{2,1,0:T(8,128)(2,1)S(1)}, bf16[2,8,1024]{2,1,0:T(8,128)(2,1)S(1)}, u32[]{:S(2)}, u32[]{:S(2)}) %collective-permute-start.51) | collective-permute-done | bytes 32800 | tf_op jit(solution)/shard_map/ppermute | solution.py:22
  444.7 11.4 %collective-permute-done.65 = bf16[2,32,1024]{2,1,0:T(8,128)(2,1)S(1)} collective-permute-done((bf16[2,32,1024]{2,1,0:T(8,128)(2,1)S(1)}, bf16[2,32,1024]{2,1,0:T(8,128)(2,1)S(1)}, u32[]{:S(2)}, u32[]{:S(2)}) %collective-permute-start.65) | collective-permute-done | bytes 131104 | tf_op jit(solution)/shard_map/ppermute | solution.py:22
  456.0 4.5 collective-permute-done.63
  470.7 6.2 %collective-permute-done.69 = bf16[1,32,1024]{2,1,0:T(8,128)(2,1)S(1)} collective-permute-done((bf16[1,32,1024]{2,1,0:T(8,128)(2,1)S(1)}, bf16[1,32,1024]{2,1,0:T(8,128)(2,1)S(1)}, u32[]{:S(2)}, u32[]{:S(2)}) %collective-permute-start.69) | collective-permute-done | bytes 65568 | tf_op jit(solution)/shard_map/ppermute | solution.py:22
  487.2 5.2 %collective-permute-done.72 = bf16[1,96,1024]{2,1,0:T(8,128)(2,1)S(1)} collective-permute-done((bf16[1,96,1024]{2,1,0:T(8,128)(2,1)S(1)}, bf16[1,96,1024]{2,1,0:T(8,128)(2,1)S(1)}, u32[]{:S(2)}, u32[]{:S(2)}) %collective-permute-start.72) | collective-permute-done | bytes 196640 | tf_op jit(solution)/shard_map/ppermute | solution.py:22
  495.3 5.7 %collective-permute-done.74 = bf16[1,192,1024]{2,1,0:T(8,128)(2,1)S(1)} collective-permute-done((bf16[1,192,1024]{2,1,0:T(8,128)(2,1)S(1)}, bf16[1,192,1024]{2,1,0:T(8,128)(2,1)S(1)}, u32[]{:S(2)}, u32[]{:S(2)}) %collective-permute-start.74) | collective-permute-done | bytes 393248 | tf_op jit(solution)/shard_map/ppermute | solution.py:22
  (503 shorter events, 199.7 us)
Async XLA Ops:
  5.1 65.7 %collective-permute-start.7 = (bf16[128,2048]{1,0:T(8,128)(2,1)S(1)}, bf16[128,2048]{1,0:T(8,128)(2,1)}, u32[]{:S(2)}, u32[]{:S(2)}) collective-permute-start(bf16[128,2048]{1,0:T(8,128)(2,1)S(1)} %get-tuple-element.300.refs_0_), channel_id=1, source_target_pairs={{0,1},{1,0},{2,3},{3,2},{4,5},{5,4},{6,7},{7,6},{8,9},{9,8},{10,11... | collective-permute-start | bytes 1572872 | tf_op jit(solution)/shard_map/ppermute | solution.py:22
  37.5 33.8 %collective-permute-start.8 = (bf16[128,2048]{1,0:T(8,128)(2,1)S(1)}, bf16[128,2048]{1,0:T(8,128)(2,1)}, u32[]{:S(2)}, u32[]{:S(2)}) collective-permute-start(bf16[128,2048]{1,0:T(8,128)(2,1)S(1)} %get-tuple-element.152.refs_1_), channel_id=1, source_target_pairs={{0,1},{1,0},{2,3},{3,2},{4,5},{5,4},{6,7},{7,6},{8,9},{9,8},{10,11... | collective-permute-start | bytes 1572872 | tf_op jit(solution)/shard_map/ppermute | solution.py:22
  38.3 26.1 %collective-permute-start.16 = (bf16[256,2048]{1,0:T(8,128)(2,1)}, bf16[256,2048]{1,0:T(8,128)(2,1)}, u32[]{:S(2)}, u32[]{:S(2)}) collective-permute-start(bf16[256,2048]{1,0:T(8,128)(2,1)} %slice.330.refs_0_), channel_id=1, source_target_pairs={{0,2},{1,3},{2,0},{3,1},{4,6},{5,7},{6,4},{7,5},{8,10},{9,11},{10,... | collective-permute-start | bytes 3145736 | tf_op jit(solution)/shard_map/ppermute | solution.py:22
  42.8 28.5 %collective-permute-start.10 = (bf16[128,2048]{1,0:T(8,128)(2,1)}, bf16[128,2048]{1,0:T(8,128)(2,1)}, u32[]{:S(2)}, u32[]{:S(2)}) collective-permute-start(bf16[128,2048]{1,0:T(8,128)(2,1)} %copy-done.13), channel_id=1, source_target_pairs={{0,1},{1,0},{2,3},{3,2},{4,5},{5,4},{6,7},{7,6},{8,9},{9,8},{10,11... | collective-permute-start | bytes 1572872 | tf_op jit(solution)/shard_map/ppermute | solution.py:22
  64.4 48.8 %collective-permute-start.23 = (bf16[512,1024]{1,0:T(8,128)(2,1)}, bf16[512,1024]{1,0:T(8,128)(2,1)}, u32[]{:S(2)}, u32[]{:S(2)}) collective-permute-start(bf16[512,1024]{1,0:T(8,128)(2,1)} %param.27), channel_id=1, source_target_pairs={{0,2},{1,3},{2,0},{3,1},{4,6},{5,7},{6,4},{7,5},{8,10},{9,11},{10,... | collective-permute-start | bytes 3145736 | tf_op jit(solution)/shard_map/ppermute | solution.py:22
  70.8 52.6 %collective-permute-start.15 = (bf16[256,2048]{1,0:T(8,128)(2,1)}, bf16[256,2048]{1,0:T(8,128)(2,1)}, u32[]{:S(2)}, u32[]{:S(2)}) collective-permute-start(bf16[256,2048]{1,0:T(8,128)(2,1)} %slice.330.refs_0_), channel_id=1, source_target_pairs={{0,1},{1,0},{2,3},{3,2},{4,5},{5,4},{6,7},{7,6},{8,9},{9,8},{10,11... | collective-permute-start | bytes 3145736 | tf_op jit(solution)/shard_map/ppermute | solution.py:22
  89.5 34.3 %collective-permute-start.17 = (bf16[256,2048]{1,0:T(8,128)(2,1)}, bf16[256,2048]{1,0:T(8,128)(2,1)S(1)}, u32[]{:S(2)}, u32[]{:S(2)}) collective-permute-start(bf16[256,2048]{1,0:T(8,128)(2,1)} %collective-permute-done.16.refs_2_), channel_id=1, source_target_pairs={{0,1},{1,0},{2,3},{3,2},{4,5},{5,4},{6,7},{7,6},{8,9},{9,8},{10,11... | collective-permute-start | bytes 3145736 | tf_op jit(solution)/shard_map/ppermute | solution.py:22
  112.7 28.9 %collective-permute-start.22 = (bf16[512,1024]{1,0:T(8,128)(2,1)}, bf16[512,1024]{1,0:T(8,128)(2,1)}, u32[]{:S(2)}, u32[]{:S(2)}) collective-permute-start(bf16[512,1024]{1,0:T(8,128)(2,1)} %param.27), channel_id=1, source_target_pairs={{0,1},{1,0},{2,3},{3,2},{4,5},{5,4},{6,7},{7,6},{8,9},{9,8},{10,11... | collective-permute-start | bytes 3145736 | tf_op jit(solution)/shard_map/ppermute | solution.py:22
  113.3 29.0 %collective-permute-start.24 = (bf16[512,1024]{1,0:T(8,128)(2,1)}, bf16[512,1024]{1,0:T(8,128)(2,1)}, u32[]{:S(2)}, u32[]{:S(2)}) collective-permute-start(bf16[512,1024]{1,0:T(8,128)(2,1)} %collective-permute-done.23), channel_id=1, source_target_pairs={{0,1},{1,0},{2,3},{3,2},{4,5},{5,4},{6,7},{7,6},{8,9},{9,8},{10,11... | collective-permute-start | bytes 3145736 | tf_op jit(solution)/shard_map/ppermute | solution.py:22
  217.7 18.5 %collective-permute-start.25 = (bf16[32,2048]{1,0:T(8,128)(2,1)}, bf16[32,2048]{1,0:T(8,128)(2,1)S(1)}, u32[]{:S(2)}, u32[]{:S(2)}) collective-permute-start(bf16[32,2048]{1,0:T(8,128)(2,1)} %get-tuple-element.188), channel_id=1, source_target_pairs={{0,8},{4,12},{8,0},{12,4},{16,24},{20,28},{24,16},{28,20},{1,9},{5... | collective-permute-start | bytes 393224 | tf_op jit(solution)/shard_map/ppermute | solution.py:22
  260.4 36.1 %collective-permute-start.34 = (bf16[1,512,1024]{2,1,0:T(8,128)(2,1)}, bf16[1,512,1024]{2,1,0:T(8,128)(2,1)}, u32[]{:S(2)}, u32[]{:S(2)}) collective-permute-start(bf16[1,512,1024]{2,1,0:T(8,128)(2,1)} %slice.434), channel_id=1, source_target_pairs={{0,2},{1,3},{2,0},{3,1},{4,6},{5,7},{6,4},{7,5},{8,10},{9,11},{10,... | collective-permute-start | bytes 3145736 | tf_op jit(solution)/shard_map/ppermute | solution.py:22
  262.0 34.5 %collective-permute-start.35 = (bf16[2,128,2048]{2,1,0:T(8,128)(2,1)}, bf16[2,128,2048]{2,1,0:T(8,128)(2,1)S(1)}, u32[]{:S(2)}, u32[]{:S(2)}) collective-permute-start(bf16[2,128,2048]{2,1,0:T(8,128)(2,1)} %broadcast_select_fusion), channel_id=1, source_target_pairs={{0,8},{4,12},{8,0},{12,4},{16,24},{20,28},{24,16},{28,20},{1,9},{5... | collective-permute-start | bytes 3145736 | tf_op jit(solution)/shard_map/ppermute | solution.py:22
  300.5 43.1 %collective-permute-start.36 = (bf16[1,256,1024]{2,1,0:T(8,128)(2,1)}, bf16[1,256,1024]{2,1,0:T(8,128)(2,1)}, u32[]{:S(2)}, u32[]{:S(2)}) collective-permute-start(bf16[1,256,1024]{2,1,0:T(8,128)(2,1)} %broadcast_select_fusion.7), channel_id=1, source_target_pairs={{0,4},{4,0},{8,12},{12,8},{16,20},{20,16},{24,28},{28,24},{1,5},{5... | collective-permute-start | bytes 1572872 | tf_op jit(solution)/shard_map/ppermute | solution.py:22
  304.3 39.2 %collective-permute-start.37 = (bf16[2,64,2048]{2,1,0:T(8,128)(2,1)}, bf16[2,64,2048]{2,1,0:T(8,128)(2,1)}, u32[]{:S(2)}, u32[]{:S(2)}) collective-permute-start(bf16[2,64,2048]{2,1,0:T(8,128)(2,1)} %broadcast_select_fusion.4), channel_id=1, source_target_pairs={{0,16},{4,20},{8,24},{12,28},{16,0},{20,4},{24,8},{28,12},{1,17},{... | collective-permute-start | bytes 1572872 | tf_op jit(solution)/shard_map/ppermute | solution.py:22
  345.7 23.0 %collective-permute-start.38 = (bf16[1,128,1024]{2,1,0:T(8,128)(2,1)}, bf16[1,128,1024]{2,1,0:T(8,128)(2,1)}, u32[]{:S(2)}, u32[]{:S(2)}) collective-permute-start(bf16[1,128,1024]{2,1,0:T(8,128)(2,1)} %broadcast_select_fusion.19), channel_id=1, source_target_pairs={{0,8},{4,12},{8,0},{12,4},{16,24},{20,28},{24,16},{28,20},{1,9},{5... | collective-permute-start | bytes 786440 | tf_op jit(solution)/shard_map/ppermute | solution.py:22
  348.3 20.4 %collective-permute-start.39 = (bf16[2,32,2048]{2,1,0:T(8,128)(2,1)}, bf16[2,32,2048]{2,1,0:T(8,128)(2,1)}, u32[]{:S(2)}, u32[]{:S(2)}) collective-permute-start(bf16[2,32,2048]{2,1,0:T(8,128)(2,1)} %broadcast_select_fusion.16), channel_id=1, source_target_pairs={{0,4},{4,0},{8,12},{12,8},{16,20},{20,16},{24,28},{28,24},{1,5},{5... | collective-permute-start | bytes 786440 | tf_op jit(solution)/shard_map/ppermute | solution.py:22
  368.8 19.8 %collective-permute-start.42 = (bf16[2,256,1024]{2,1,0:T(8,128)(2,1)}, bf16[2,256,1024]{2,1,0:T(8,128)(2,1)}, u32[]{:S(2)}, u32[]{:S(2)}) collective-permute-start(bf16[2,256,1024]{2,1,0:T(8,128)(2,1)} %get-tuple-element.248), channel_id=1, source_target_pairs={{0,1},{1,0},{2,3},{3,2},{4,5},{5,4},{6,7},{7,6},{8,9},{9,8},{10,11... | collective-permute-start | bytes 3145736 | tf_op jit(solution)/shard_map/ppermute | solution.py:22
  374.8 19.4 %collective-permute-start.60 = (bf16[104,512]{1,0:T(8,128)(2,1)}, bf16[104,512]{1,0:T(8,128)(2,1)}, u32[]{:S(2)}, u32[]{:S(2)}) collective-permute-start(bf16[104,512]{1,0:T(8,128)(2,1)} %broadcast_select_fusion.31), channel_id=1, source_target_pairs={{0,1},{1,0},{2,3},{3,2},{4,5},{5,4},{6,7},{7,6},{8,9},{9,8},{10,11... | collective-permute-start | bytes 319496 | tf_op jit(solution)/shard_map/ppermute | solution.py:22
  413.7 23.8 %collective-permute-start.55 = (bf16[1,256,1024]{2,1,0:T(8,128)(2,1)S(1)}, bf16[1,256,1024]{2,1,0:T(8,128)(2,1)S(1)}, u32[]{:S(2)}, u32[]{:S(2)}) collective-permute-start(bf16[1,256,1024]{2,1,0:T(8,128)(2,1)S(1)} %slice.464), channel_id=1, source_target_pairs={{0,2},{1,3},{2,0},{3,1},{4,6},{5,7},{6,4},{7,5},{8,10},{9,11},{10,... | collective-permute-start | bytes 1572872 | tf_op jit(solution)/shard_map/ppermute | solution.py:22
  415.4 21.7 %collective-permute-start.56 = (bf16[1,128,1024]{2,1,0:T(8,128)(2,1)S(1)}, bf16[1,128,1024]{2,1,0:T(8,128)(2,1)S(1)}, u32[]{:S(2)}, u32[]{:S(2)}) collective-permute-start(bf16[1,128,1024]{2,1,0:T(8,128)(2,1)S(1)} %pad_maximum_fusion.7), channel_id=1, source_target_pairs={{0,8},{4,12},{8,0},{12,4},{16,24},{20,28},{24,16},{28,20},{1,9},{5... | collective-permute-start | bytes 786440 | tf_op jit(solution)/shard_map/ppermute | solution.py:22
  417.0 20.1 %collective-permute-start.57 = (bf16[1,64,2048]{2,1,0:T(8,128)(2,1)S(1)}, bf16[1,64,2048]{2,1,0:T(8,128)(2,1)S(1)}, u32[]{:S(2)}, u32[]{:S(2)}) collective-permute-start(bf16[1,64,2048]{2,1,0:T(8,128)(2,1)S(1)} %pad_maximum_fusion.8), channel_id=1, source_target_pairs={{0,16},{4,20},{8,24},{12,28},{16,0},{20,4},{24,8},{28,12},{1,17},{... | collective-permute-start | bytes 786440 | tf_op jit(solution)/shard_map/ppermute | solution.py:22
  439.8 20.8 %collective-permute-start.63 = (bf16[1,256,1024]{2,1,0:T(8,128)(2,1)S(1)}, bf16[1,256,1024]{2,1,0:T(8,128)(2,1)S(1)}, u32[]{:S(2)}, u32[]{:S(2)}) collective-permute-start(bf16[1,256,1024]{2,1,0:T(8,128)(2,1)S(1)} %pad_maximum_fusion.3), channel_id=1, source_target_pairs={{0,4},{4,0},{8,12},{12,8},{16,20},{20,16},{24,28},{28,24},{1,5},{5... | collective-permute-start | bytes 1572872 | tf_op jit(solution)/shard_map/ppermute | solution.py:22
  440.5 20.0 %collective-permute-start.64 = (bf16[1,128,2048]{2,1,0:T(8,128)(2,1)S(1)}, bf16[1,128,2048]{2,1,0:T(8,128)(2,1)S(1)}, u32[]{:S(2)}, u32[]{:S(2)}) collective-permute-start(bf16[1,128,2048]{2,1,0:T(8,128)(2,1)S(1)} %pad_maximum_fusion.4), channel_id=1, source_target_pairs={{0,8},{4,12},{8,0},{12,4},{16,24},{20,28},{24,16},{28,20},{1,9},{5... | collective-permute-start | bytes 1572872 | tf_op jit(solution)/shard_map/ppermute | solution.py:22
  444.1 20.8 %collective-permute-start.54 = (f32[1152]{0:T(1024)S(1)}, f32[1152]{0:T(1024)S(1)}, u32[]{:S(2)}, u32[]{:S(2)}) collective-permute-start(f32[1152]{0:T(1024)S(1)} %fusion.21), channel_id=1, source_target_pairs={{0,2},{1,3},{2,0},{3,1},{4,6},{5,7},{6,4},{7,5},{8,10},{9,11},{10,... | collective-permute-start | bytes 13832 | tf_op jit(solution)/shard_map/ppermute | solution.py:22
  (125 other events, 1231.2 us)

commit v3 on v2

--- a/solution.py
+++ b/solution.py
@@ -15,6 +15,16 @@
 HALO = 16
 HEAD = 16
 VMEM_LIMIT = 60 * 1024 * 1024
+LIMITS = {
+    "inputs": 20,
+    "gates": 20,
+    "end_states": 28,
+    "forward_states": 60,
+    "first_grads": 60,
+    "gate_grads": 60,
+    "backward_states": 60,
+    "tail_grads": 60,
+}
 
 
 def swap(values, axis, bit):
@@ -43,8 +53,10 @@
     return [values] + [swap(values, "ctx", j) for j in range(2, size, 2)]
 
 
-def gather_near(far):
-    return [block for own in far for block in (own, swap(own, "ctx", 1))]
+def gather_near(far, beside=()):
+    blocks = [block for own in far[:2] for block in (own, swap(own, "ctx", 1))]
+    rest, beside = together(far[2:], beside)
+    return blocks + [block for own in rest for block in (own, swap(own, "ctx", 1))], beside
 
 
 def together(*trees):
@@ -100,6 +112,16 @@
         return jnp.concatenate([jnp.where(up, other, own), jnp.where(up, own, other)], axis=1)
 
     return lambda values: (values, swap(values, "ctx", bit), finish)
+
+
+def gather_step(bit):
+    return lambda values: (
+        values, swap(values, "ctx", bit), lambda own, other: jnp.concatenate([own, other], axis=0)
+    )
+
+
+def sum_step(bit):
+    return lambda values: (values, swap(values, "fsdp", bit), lambda own, other: own + other)
 
 
 def reduce_steps(ctx_first, turn=0):
@@ -172,14 +194,28 @@
     return slice(j * LANES, (j + 1) * LANES)
 
 
-def input_kernel(scal, normed_ref, *refs, count, piece):
-    weights, (s_ref, x_ref, conv_ref, xs_ref, proj_ref) = refs[:count], refs[count:]
-    depth = weights[0].shape[0]
-    width = weights[0].shape[1]
-    mixed = dot(normed_ref[:, 0:depth], weights[0][...])
-    for r in range(1, count):
-        mixed = mixed + dot(normed_ref[:, r * depth : (r + 1) * depth], weights[r][...])
-    x_low = mixed.astype(BF16).reshape(2, HALO + piece, width)
+def input_kernel(scal, normed_ref, *refs, count, piece, is_upper):
+    lows, highs = refs[:count], refs[count : 2 * count]
+    s_ref, x_ref, conv_ref, xs_ref, proj_ref, mixed_ref = refs[2 * count :]
+    depth = lows[0].shape[0]
+    width = lows[0].shape[1]
+    upper = is_upper(pl.program_id(0), scal)
+
+    def mix(weights):
+        mixed = dot(normed_ref[:, 0:depth], weights[0][...])
+        for r in range(1, count):
+            mixed = mixed + dot(normed_ref[:, r * depth : (r + 1) * depth], weights[r][...])
+        mixed_ref[...] = mixed
+
+    @pl.when(upper)
+    def from_high():
+        mix(highs)
+
+    @pl.when(jnp.logical_not(upper))
+    def from_low():
+        mix(lows)
+
+    x_low = mixed_ref[...].astype(BF16).reshape(2, HALO + piece, width)
     x_ref[...] = x_low
     x = x_low.astype(F32)
     head = s_ref[0:HEAD, :].astype(F32)
@@ -214,7 +250,7 @@
 
 
 def end_kernel(
-    scal, proj_ref, s_ref, xs_ref, b_ref, step_ref, end_ref, log_ref, drive_ref, *, tiles, groups, rank
+    scal, proj_ref, s_ref, xs_ref, b_ref, step_ref, end_ref, drive_ref, *, tiles, groups, rank
 ):
     piece = groups * 8
     width = tiles * LANES
@@ -223,12 +259,18 @@
     delta = proj_ref[:, 0:rank].astype(BF16)
     pre = dot(delta, s_ref[HEAD : HEAD + rank, :]) + head[5:6]
     row = lax.broadcasted_iota(jnp.int32, (piece, width), 0)
+    logs = []
     for h in range(2):
         step = softplus(pre[h * piece : (h + 1) * piece])
         step = jnp.where(row < scal[1 + h], step, 0.0)
-        log_ref[h : h + 1, :] = jnp.sum(step, axis=0, keepdims=True)
+        logs.append(jnp.sum(step, axis=0, keepdims=True))
         step_ref[h] = step.reshape(groups, 8, width)
         drive_ref[h] = (step * xs_ref[h].astype(F32)).reshape(groups, 8, width)
+    logs = jnp.concatenate(logs, axis=0)
+    parts = [part.astype(F32) for part in three_parts(logs)]
+    end_ref[2 * states : 2 * states + 8, :] = jnp.concatenate(
+        parts + [jnp.zeros_like(logs)], axis=0
+    ).astype(BF16)
     rate2 = -jnp.exp(s_ref[80 : 80 + states, :].astype(F32)) * LOG2E
     rates = [rate2[:, tile_cols(j)] for j in range(tiles)]
 
@@ -251,34 +293,64 @@
             end_ref[h * states : (h + 1) * states, tile_cols(j)] = held[h * tiles + j].astype(BF16)
 
 
-def carried(ends, log_ref, rate2, h, ctx, states, cols):
+def span_logs(ends, plan_ref, h, ctx, states):
+    rows = []
+    for j in range(1, ctx):
+        parts = ends[j - 1][2 * states : 2 * states + 8, :].astype(F32)
+        rows.append(parts[h : h + 1] + parts[2 + h : 3 + h] + parts[4 + h : 5 + h])
+    logs = jnp.concatenate([jnp.zeros_like(rows[0])] + rows, axis=0)
+    inside = plan_ref[h * ctx : (h + 1) * ctx, 0:ctx]
+    outside = plan_ref[(2 + h) * ctx : (3 + h) * ctx, 0:1]
+    return outside + lax.dot_general(
+        inside, logs, (((1,), (0,)), ((), ())), precision=lax.Precision.HIGHEST, preferred_element_type=F32
+    )
+
+
+def diagonal_maps(proj_ref, first, states):
+    rows = proj_ref.shape[0]
+    k = lax.broadcasted_iota(jnp.int32, (proj_ref.shape[1], 16 * states), 0)
+    n = lax.broadcasted_iota(jnp.int32, (proj_ref.shape[1], 16 * states), 1) % states
+    spread = dot(proj_ref[...].astype(BF16), (k == n + first).astype(F32).astype(BF16))
+    row = lax.broadcasted_iota(jnp.int32, (rows, 16 * states), 0) % 16
+    col = lax.broadcasted_iota(jnp.int32, (rows, 16 * states), 1) // states
+    return jnp.where(row == col, spread, 0.0).astype(BF16)
+
+
+def carried(ends, logs, rate2, h, ctx, states, cols):
     value = jnp.zeros((states, LANES), F32)
     for j in range(1, ctx):
-        decay = jnp.exp2(rate2 * log_ref[h * ctx + j : h * ctx + j + 1, cols])
+        decay = jnp.exp2(rate2 * logs[j : j + 1, cols])
         value = value + decay * ends[j - 1][h * states : (h + 1) * states, cols].astype(F32)
     return value
 
 
 def forward_kernel(scal, *refs, tiles, groups, ctx, features):
     ends = refs[: ctx - 1]
-    log_ref, s_ref, step_ref, xs_ref, gate_ref, b_ref, cdiag_ref, weight_ref = refs[ctx - 1 : ctx + 7]
+    plan_ref, s_ref, step_ref, xs_ref, gate_ref, b_ref, proj_ref, weight_ref = refs[ctx - 1 : ctx + 7]
     rest = refs[ctx + 7 :]
     scale_ref, tokens_ref, teacher_ref = rest[:3]
     ssm_ref, branch_ref, hidden_ref, start_ref, out_ref, gout_ref, dout_ref, square_ref = rest[3:11]
-    drive_ref, read_ref, odd_ref, even_ref, acc_ref = rest[11:]
+    drive_ref, read_ref, odd_ref, even_ref, acc_ref, cdiag_ref = rest[11:]
     piece = groups * 8
     width = tiles * LANES
     states = b_ref.shape[2]
     i = pl.program_id(0)
     head = s_ref[0:HEAD, :].astype(F32)
+
+    @pl.when(i == 0)
+    def maps():
+        values = diagonal_maps(proj_ref, proj_ref.shape[1] - states, states)
+        cdiag_ref[...] = values.reshape(cdiag_ref.shape)
+
     for h in range(2):
         drive_ref[h] = step_ref[h] * xs_ref[h].astype(F32).reshape(groups, 8, width)
     rate2 = -jnp.exp(s_ref[80 : 80 + states, :].astype(F32)) * LOG2E
     rates = [rate2[:, tile_cols(j)] for j in range(tiles)]
     held = []
     for h in range(2):
+        logs = span_logs(ends, plan_ref, h, ctx, states)
         for j in range(tiles):
-            held.append(carried(ends, log_ref, rates[j], h, ctx, states, tile_cols(j)))
+            held.append(carried(ends, logs, rates[j], h, ctx, states, tile_cols(j)))
             start_ref[h, :, tile_cols(j)] = held[-1]
 
     def scan(t, held, keep_ref):
@@ -414,16 +486,20 @@
         cols = slice(r * depth, (r + 1) * depth)
         target = send_ref if r % 2 else keep_ref
         target[r // 2] = rows_dot(own[:, cols], d_gate).astype(BF16)
-        dnormed_ref[:, cols] += back_dot(d_gate, weights[r][...])
+        back = back_dot(d_gate, weights[r][...])
+        for h in range(2):
+            rows = slice(h * (HALO + piece) + HALO, (h + 1) * (HALO + piece))
+            dnormed_ref[rows, cols] += back[h * piece : (h + 1) * piece]
 
 
 def backward_kernel(scal, *refs, tiles, groups, ctx, rank):
     grads = refs[: ctx - 1]
+    ends = refs[ctx - 1 : 2 * ctx - 2]
     (
-        log_ref, proj_ref, s_ref, step_ref, xs_ref, c_ref, bdiag_ref, start_ref, dssm_ref, hidden_ref,
+        plan_ref, proj_ref, s_ref, step_ref, xs_ref, c_ref, start_ref, dssm_ref, hidden_ref,
         dxs_ref, small_ref, ddelta_ref, db_ref, dc_ref,
-        adj_ref, dstep_ref, dbs_ref, dcs_ref, adj_odd, adj_even, term_odd, term_even,
-    ) = refs[ctx - 1 :]
+        adj_ref, dstep_ref, dbs_ref, dcs_ref, adj_odd, adj_even, term_odd, term_even, bdiag_ref,
+    ) = refs[2 * ctx - 2 :]
     piece = groups * 8
     width = tiles * LANES
     states = c_ref.shape[2]
@@ -435,6 +511,7 @@
     def clear():
         dbs_ref[...] = jnp.zeros_like(dbs_ref)
         dcs_ref[...] = jnp.zeros_like(dcs_ref)
+        bdiag_ref[...] = diagonal_maps(proj_ref, rank, states).reshape(bdiag_ref.shape)
         ddelta_ref[...] = jnp.zeros_like(ddelta_ref)
 
     rate = -jnp.exp(s_ref[80 : 80 + states, :].astype(F32))
@@ -499,11 +576,11 @@
         scan(t - 1, False, later, sums, adj_odd, term_odd)
         return tuple(later + sums)
 
-    later = [
-        carried(grads, log_ref, rates2[j], h, ctx, states, tile_cols(j))
-        for h in range(2)
-        for j in range(tiles)
-    ]
+    later = []
+    for h in range(2):
+        logs = span_logs(ends, plan_ref, h, ctx, states)
+        for j in range(tiles):
+            later.append(carried(grads, logs, rates2[j], h, ctx, states, tile_cols(j)))
     sums = [jnp.zeros((states, LANES), F32)] * tiles
     scan(blocks - 1, False, later, sums, adj_odd, term_odd)
     both = lax.fori_loop(0, blocks // 2 - 1, body, tuple(later + sums))
@@ -543,9 +620,8 @@
     scal, dproj_ref, s_ref, dlow_ref, dhigh_ref, conv_ref, x_ref, xs_ref, normed_ref, before_ref, *refs,
     count, piece, is_upper
 ):
-    weights, (small_ref, keep_ref, send_ref, dnormed_ref, pad_ref) = refs[: 2 * count], refs[2 * count :]
-    half = weights[0].shape[0]
-    depth = 2 * half
+    weights, (small_ref, keep_ref, send_ref, dnormed_ref, pad_ref) = refs[:count], refs[count:]
+    depth = weights[0].shape[0]
     width = weights[0].shape[1]
     ext = HALO + piece
 
@@ -583,8 +659,7 @@
         cols = slice(r * depth, (r + 1) * depth)
         target = send_ref if r % 2 else keep_ref
         target[r // 2] = rows_dot(normed_ref[:, cols], low).astype(BF16)
-    for r in range(2 * count):
-        dnormed_ref[:, r * half : (r + 1) * half] += back_dot(low, weights[r][...])
+        dnormed_ref[:, cols] += back_dot(low, weights[r][...])
 
 
 def shape(dims, dtype=F32):
@@ -606,7 +681,7 @@
         ),
         out_shape=out_shape,
         name=name,
-        compiler_params=pltpu.CompilerParams(vmem_limit_bytes=VMEM_LIMIT),
+        compiler_params=pltpu.CompilerParams(vmem_limit_bytes=LIMITS[name] * 2**20),
         cost_estimate=pl.CostEstimate(flops=flops, bytes_accessed=size, transcendentals=exps),
     )(scal, *args)
 
@@ -668,17 +743,31 @@
     behind = places > own[:, None]
     has_before = jnp.stack([pair_id > 0, pair_id < ctx - 1])
     has_after = jnp.stack([pair_id < ctx - 1, pair_id > 0])
-    lower = pair_owner[jnp.maximum(pair_id - 1, 0)] ^ me_ctx
-    upper = pair_owner[jnp.minimum(pair_id + 1, ctx - 1)] ^ me_ctx
+    lower_owner = pair_owner[jnp.maximum(pair_id - 1, 0)]
+    upper_owner = pair_owner[jnp.minimum(pair_id + 1, ctx - 1)]
+    lower, upper = lower_owner ^ me_ctx, upper_owner ^ me_ctx
+
+    def plan_of(inside, wanted):
+        inside = jnp.pad(inside.astype(F32), ((0, 0), (0, 0), (0, LANES - ctx)))
+        outside = jnp.broadcast_to(jnp.where(wanted, 0.0, 1e30)[..., None], (2, ctx, LANES))
+        return jnp.concatenate([inside, outside], axis=0).reshape(4 * ctx, LANES).astype(F32)
+
+    plan_before = plan_of(between, before)
+    plan_behind = plan_of(between_back, behind)
+
+    def to_blocks(values, size):
+        axis = values.ndim - 1
+        return jnp.concatenate(
+            [
+                lax.dynamic_slice_in_dim(values, (me_fsdp ^ r) * size, size, axis=axis)
+                for r in range(fsdp)
+            ],
+            axis=axis,
+        )
 
     own_rows = tokens[0]
     valid_slots = jnp.minimum(lengths[0], 2 * ctx * piece)
     coded = jnp.concatenate([valid_slots // 128, valid_slots % 128]).astype(BF16)[None]
-    first, second = jnp.split(in_proj[:, :width], 2, axis=0)
-    x_first = gather_fsdp(first)
-    second, coded, last_rows, _ = lax.optimization_barrier(
-        (second, coded, own_rows.reshape(2, piece, features)[:, piece - 3 :], x_first[fsdp // 2])
-    )
     rows_head = jnp.concatenate(
         [
             conv_weight,
@@ -694,27 +783,23 @@
         ],
         axis=0,
     )
+    half = width // 2
+    to_send = in_proj[:, :half]
+    x_far = [to_send] + [swap(to_send, "fsdp", bit) for bit in range(2, fsdp, 2)]
+    last_rows = to_blocks(own_rows.reshape(2, piece, features)[:, piece - 3 :], depth)
+    last_rows = jnp.broadcast_to(last_rows[None], (ctx, 2, 3, features))
+    token_rel = to_blocks(own_rows, depth).reshape(2, piece, features)
+    tails = lax.all_to_all(last_rows, "ctx", 0, 0)
+    x_far, second, rows_head, tails, token_rel, scal, plan_before, plan_behind = together(
+        x_far, in_proj[:, half:width], rows_head, tails, token_rel, scal, plan_before, plan_behind
+    )
+    x_first = [block for own in x_far for block in (own, swap(own, "fsdp", 1))]
     small_blocks = gather_fsdp(rows_head)
     small = jnp.concatenate(small_blocks, axis=1)
     gain = jnp.concatenate([block[7, :depth] for block in small_blocks]).astype(F32)
     x_second = gather_fsdp(second)
-    x_blocks = [piece_now for pair in zip(x_first, x_second) for piece_now in pair]
-    gate_blocks = gather_fsdp(after(in_proj[:, width:], x_second[fsdp // 2]))
-    out_blocks = gather_fsdp(after(out_proj, gate_blocks[fsdp // 2]))
-
-    def to_blocks(values, size):
-        axis = values.ndim - 1
-        return jnp.concatenate(
-            [
-                lax.dynamic_slice_in_dim(values, (me_fsdp ^ r) * size, size, axis=axis)
-                for r in range(fsdp)
-            ],
-            axis=axis,
-        )
-
-    token_rel = to_blocks(own_rows, depth).reshape(2, piece, features)
-    tails = gather_small_ctx(to_blocks(last_rows, depth))
-    before_rows = jnp.stack([tails[lower, 0], tails[upper, 1]])
+
+    before_rows = jnp.stack([tails[lower_owner, 0], tails[upper_owner, 1]])
     before_rows = jnp.where(has_before[:, None, None], before_rows, jnp.zeros_like(before_rows))
     rows_ext = jnp.concatenate(
         [jnp.zeros((2, HALO - 3, features), BF16), before_rows, token_rel], axis=1
@@ -742,11 +827,21 @@
     cb = min(256, part)
     steps = width // cb
     weight_specs = [pl.BlockSpec((depth, cb), cols_at(cb)) for _ in range(fsdp)]
-    half_specs = [pl.BlockSpec((depth // 2, cb), cols_at(cb)) for _ in range(2 * fsdp)]
+    half_blocks = half // cb
+
+    def upper_place(i, scal):
+        return cols_at(cb)(i, scal)[1] >= half_blocks
+
+    low_spec = pl.BlockSpec(
+        (depth, cb), lambda i, scal: (0, jnp.minimum(cols_at(cb)(i, scal)[1], half_blocks - 1))
+    )
+    high_spec = pl.BlockSpec(
+        (depth, cb), lambda i, scal: (0, jnp.maximum(cols_at(cb)(i, scal)[1] - half_blocks, 0))
+    )
     x_ext, conv, xs, proj = call(
-        functools.partial(input_kernel, count=2 * fsdp, piece=piece),
-        "inputs", steps, scal, (normed, *x_blocks, small),
-        [whole_spec((2 * ext, features)), *half_specs, spec_small(cb)],
+        functools.partial(input_kernel, count=fsdp, piece=piece, is_upper=upper_place),
+        "inputs", steps, scal, (normed, *x_first, *x_second, small),
+        [whole_spec((2 * ext, features)), *([low_spec] * fsdp), *([high_spec] * fsdp), spec_small(cb)],
         [
             pl.BlockSpec((2, ext, cb), lambda i, scal: (0, 0, i)),
             spec_rows(cb),
@@ -759,41 +854,41 @@
             shape((2, piece, width), BF16),
             shape((rows_all, rank + 2 * states)),
         ],
-        [], 2 * rows_all * features * width,
-    )
+        [pltpu.VMEM((2 * ext, cb), F32)], 2 * rows_all * features * width,
+    )
+    gate_first = after(in_proj[:, width:], x_second[fsdp // 2])
+    gate_far = [gate_first] + [swap(gate_first, "fsdp", bit) for bit in range(2, fsdp, 2)]
+    gate_far, proj = together(gate_far, proj)
+    gate_blocks = [block for own in gate_far for block in (own, swap(own, "fsdp", 1))]
+    out_first = after(out_proj, gate_far[-1])
+    out_far = [out_first] + [swap(out_first, "fsdp", bit) for bit in range(2, fsdp, 2)]
     wide_dims = (2, piece, states, LANES)
     maps = proj[:, rank:].reshape(2, piece, 2 * states, 1)
     b_wide = jnp.broadcast_to(maps[:, :, :states], wide_dims)
 
     tiles = 4
     block = tiles * LANES
-    half = width // 2
     per_half = half // block
     group_spec = spec_groups(block)
     state_row = pl.BlockSpec((2 * states, block), lambda i, scal: (0, i))
-    log_spec = pl.BlockSpec((2 * ctx, block), lambda i, scal: (0, i))
+    sent_row = pl.BlockSpec((2 * states + 8, block), lambda i, scal: (0, i))
+    plan_spec = whole_spec((4 * ctx, LANES))
     row_spec = whole_spec((rows_all, features))
     wide_spec = whole_spec(wide_dims)
-    diag_spec = whole_spec((2, piece // 16, 16, 16 * states))
+    diag_space = pltpu.VMEM((2, piece // 16, 16, 16 * states), BF16)
     hidden_spec = pl.BlockSpec((tiles, 2, piece, states, LANES), lambda i, scal: (i, 0, 0, 0, 0))
     start_spec = pl.BlockSpec((2, states, block), lambda i, scal: (0, 0, i))
     keep_spaces = [pltpu.VMEM((2, tiles, 16 * states, LANES), BF16)]
     group_space = pltpu.VMEM((2, groups, 8, block), F32)
 
-    step, ends, logs = call(
+    step, sent = call(
         functools.partial(end_kernel, tiles=tiles, groups=groups, rank=rank),
         "end_states", width // block, scal, (proj, small, xs, b_wide),
         [whole_spec(proj.shape), spec_small(block), spec_rows(block), wide_spec],
-        [group_spec, state_row, pl.BlockSpec((2, block), lambda i, scal: (0, i))],
-        [shape((2, groups, 8, width)), shape((2 * states, width), BF16), shape((2, width))],
+        [group_spec, pl.BlockSpec((2 * states + 8, block), lambda i, scal: (0, i))],
+        [shape((2, groups, 8, width)), shape((2 * states + 8, width), BF16)],
         [group_space], 5 * elements, elements,
     )
-    sent = jnp.concatenate([ends, *three_parts(logs), jnp.zeros((2, width), BF16)], axis=0)
-
-    def diagonal(values):
-        values = values.reshape(2, piece // 16, 1, 16, states).astype(BF16)
-        same = jnp.eye(16, dtype=BF16)[None, None, :, :, None]
-        return (values * same).reshape(2, piece // 16, 16, 16 * states)
 
     far = gather_far(sent)
     (gate,) = call(
@@ -802,28 +897,20 @@
         [whole_spec((2 * ext, features)), *weight_specs], [spec_rows(cb)],
         [shape((2, piece, width))], [], 2 * rows_all * features * width,
     )
-    far, gate = together(far, gate)
-    near = gather_near(far)
     c_wide = jnp.broadcast_to(maps[:, :, states:], wide_dims)
-    b_diag = diagonal(maps[:, :, :states])
-    c_diag = diagonal(maps[:, :, states:])
+    far, gate, out_far = together(far, gate, out_far)
+    near, c_wide = gather_near(far, c_wide)
+    out_blocks = [block for own in out_far for block in (own, swap(own, "fsdp", 1))]
     weight_out = jnp.concatenate(out_blocks, axis=0)
-    near, c_wide, b_diag, c_diag, weight_out = together(near, c_wide, b_diag, c_diag, weight_out)
-    parts = jnp.stack([b[2 * states : 2 * states + 6] for b in near]).astype(F32)
-    logs = (parts[:, 0:2] + parts[:, 2:4] + parts[:, 4:6]).transpose(1, 0, 2)
-
-    def spans(inside, wanted):
-        summed = jnp.sum(jnp.where(inside[..., None], logs[:, None], 0.0), axis=2)
-        return jnp.where(wanted[..., None], summed, 1e30).reshape(2 * ctx, width)
-
+    near, weight_out = together(near, weight_out)
     ssm, branch, hidden, starts, out_low, g_out, d_out, squares = call(
         functools.partial(forward_kernel, tiles=tiles, groups=groups, ctx=ctx, features=features),
         "forward_states", width // block, scal,
-        (*near[1:], spans(between, before), small, step, xs, gate, b_wide, c_diag, weight_out,
+        (*near[1:], plan_before, small, step, xs, gate, b_wide, proj, weight_out,
          scale, own_rows, teacher[0]),
         [
-            *([state_row] * (ctx - 1)), log_spec, spec_small(block), group_spec, spec_rows(block),
-            spec_rows(block), wide_spec, diag_spec,
+            *([sent_row] * (ctx - 1)), plan_spec, spec_small(block), group_spec, spec_rows(block),
+            spec_rows(block), wide_spec, whole_spec(proj.shape),
             pl.BlockSpec((block, features), lambda i, scal: (i, 0)),
             pl.BlockSpec(memory_space=pltpu.SMEM), row_spec, row_spec,
         ],
@@ -841,7 +928,7 @@
             shape((rows_all, features), BF16),
             shape((8, features)),
         ],
-        [group_space] * 2 + keep_spaces * 2 + [pltpu.VMEM((rows_all, features), F32)],
+        [group_space] * 2 + keep_spaces * 2 + [pltpu.VMEM((rows_all, features), F32), diag_space],
         10 * elements, elements,
     )
     d_ssm, d_gate, grad_skip, grads_first = call(
@@ -864,20 +951,16 @@
     back_far = gather_far(grads_first)
 
     pairs = fsdp // 2
-    half_blocks = half // cb
     pair_spec = pl.BlockSpec((pairs, depth, cb), lambda i, scal: (0, 0, i))
     pair_at = pl.BlockSpec((pairs, depth, cb), lambda i, scal: (0, 0, cols_at(cb)(i, scal)[1]))
     keep_gate, send_gate, d_normed_gate = call(
         functools.partial(gate_grad_kernel, count=fsdp, piece=piece),
         "gate_grads", steps, scal, (normed, d_gate, *gate_blocks),
         [whole_spec((2 * ext, features)), spec_rows(cb), *weight_specs],
-        [pair_at, pair_at, row_spec],
-        [shape((pairs, depth, width), BF16)] * 2 + [shape((rows_all, features))],
+        [pair_at, pair_at, whole_spec((2 * ext, features))],
+        [shape((pairs, depth, width), BF16)] * 2 + [shape((2 * ext, features))],
         [], 4 * rows_all * features * width,
     )
-    back_far, keep_gate, send_gate = together(back_far, keep_gate, send_gate)
-    back_near = gather_near(back_far)
-    got_gate = swap(send_gate, "fsdp", 1)
     subs = part // cb
     branch_rows = branch.reshape(rows_all, width)
     keep_out, send_out = pl.pallas_call(
@@ -896,12 +979,14 @@
             flops=2 * rows_all * width * features, bytes_accessed=9 * 2**20, transcendentals=0
         ),
     )(branch_rows, branch_rows, d_out)
-    got_gate, keep_out, send_out = together(got_gate, keep_out, send_out)
-    got_out = swap(send_out, "fsdp", 1)
-    core_gate = joined(keep_gate, got_gate)
-    back_near, got_out, core_gate = together(back_near, got_out, core_gate)
-    chains = [(reduce_steps(False), joined(keep_out, got_out)), (reduce_steps(True, 1), core_gate)]
-    log_behind = spans(between_back, behind)
+    back_far, keep_gate, send_gate, keep_out, send_out = together(
+        back_far, keep_gate, send_gate, keep_out, send_out
+    )
+    back_near, _ = gather_near(back_far)
+    core_gate = joined(keep_gate, swap(send_gate, "fsdp", 1))
+    core_out = joined(keep_out, swap(send_out, "fsdp", 1))
+    back_near, core_out, core_gate = together(back_near, core_out, core_gate)
+    chains = [(reduce_steps(False), core_out), (reduce_steps(True, 1), core_gate)]
 
     def backward(c):
         def at(i):
@@ -910,13 +995,14 @@
         return call(
             functools.partial(backward_kernel, tiles=tiles, groups=groups, ctx=ctx, rank=rank),
             "backward_states", per_half, scal,
-            (*back_near[1:], log_behind, proj, small, step, xs, c_wide, b_diag, starts, d_ssm, hidden),
+            (*back_near[1:], *near[1:], plan_behind, proj, small, step, xs, c_wide, starts, d_ssm, hidden),
             [
                 *([pl.BlockSpec((2 * states, block), lambda i, scal: (0, at(i)))] * (ctx - 1)),
-                pl.BlockSpec((2 * ctx, block), lambda i, scal: (0, at(i))),
+                *([pl.BlockSpec((2 * states + 8, block), lambda i, scal: (0, at(i)))] * (ctx - 1)),
+                plan_spec,
                 whole_spec(proj.shape), spec_small(block, c * per_half),
                 pl.BlockSpec((2, groups, 8, block), lambda i, scal: (0, 0, 0, at(i))),
-                spec_rows(block, c * per_half), wide_spec, diag_spec,
+                spec_rows(block, c * per_half), wide_spec,
                 pl.BlockSpec((2, states, block), lambda i, scal: (0, 0, at(i))),
                 pl.BlockSpec((2, groups, 8, block), lambda i, scal: (0, 0, 0, at(i))),
                 pl.BlockSpec((tiles, 2, piece, states, LANES), lambda i, scal: (at(i), 0, 0, 0, 0)),
@@ -933,7 +1019,8 @@
                 shape((2, piece // 16, 16 * states)),
                 shape((2, piece // 16, 16 * states)),
             ],
-            [group_space] * 2 + [pltpu.VMEM((2, piece // 16, 16, 16 * states), F32)] * 2 + keep_spaces * 4,
+            [group_space] * 2 + [pltpu.VMEM((2, piece // 16, 16, 16 * states), F32)] * 2 + keep_spaces * 4
+            + [diag_space],
             16 * elements // 2, elements // 2,
         )
 
@@ -972,7 +1059,8 @@
                 is_upper=lambda i, scal: place(i, scal) >= half_blocks,
             ),
             "tail_grads", half_steps, scal,
-            (d_proj, small, back_first[0], back_second[0], conv, x_ext, xs, normed, d_before, *x_blocks),
+            (d_proj, small, back_first[0], back_second[0], conv, x_ext, xs, normed, d_before,
+             *(x_second if c else x_first)),
             [
                 whole_spec(d_proj.shape),
                 pl.BlockSpec((small.shape[0], cb), lambda i, scal: (0, place(i, scal))),
@@ -984,7 +1072,7 @@
                 ),
                 at_rows(piece), at_rows(ext), at_rows(piece),
                 whole_spec((2 * ext, features)), whole_spec((2 * ext, features)),
-                *([pl.BlockSpec((depth // 2, cb), lambda i, scal: (0, i + base))] * (2 * fsdp)),
+                *([pl.BlockSpec((depth, cb), lambda i, scal: (0, i))] * fsdp),
             ],
             [
                 pl.BlockSpec((104, cb), lambda i, scal: (0, i)),
@@ -1000,9 +1088,7 @@
             4 * rows_all * features * half,
         )
 
-    d_before = jnp.pad(
-        d_normed_gate.reshape(2, piece, features), ((0, 0), (HALO, 0), (0, 0))
-    ).reshape(2 * ext, features)
+    d_before = d_normed_gate
     d_proj, d_before, _ = together(d_proj, d_before, [values for _, values in chains])
     chains, tail_first = advance(chains, tail(0, d_proj, d_before))
     got_ahead = swap(tail_first[2], "fsdp", 1)
@@ -1014,6 +1100,24 @@
         chains, (tail(1, d_proj, tail_first[3]), got_ahead, small_now)
     )
     ahead = joined(tail_first[1], got_ahead)
+    def halo_start(d_ext, squares):
+        d_normed = d_ext.reshape(2, ext, features)
+        unit = rows_ext * inv_rms
+        grad_gain = jnp.sum(d_normed[:, HALO - 3 :] * unit[:, HALO - 3 :], axis=(0, 1))
+        square = jnp.pad(jnp.stack(three_parts(jnp.sum(squares))), (0, features - 3))
+        halo_rows = d_normed[:, HALO - 3 : HALO].reshape(6, features)
+        return jnp.concatenate(
+            [halo_rows.astype(BF16), square[None], grad_gain.astype(BF16)[None]]
+        )[None]
+
+    def halo_vector(halo_got):
+        return jnp.concatenate(
+            [
+                to_blocks(jnp.sum(halo_got[:, 7], axis=0)[None], depth)[0],
+                jnp.pad(jnp.sum(halo_got[:, 6, 0:3])[None], (0, LANES - 1)),
+            ]
+        )
+
     tail_rows = [
         values[:, k * part : (k + 1) * part].astype(BF16)
         for values in (tail_first[0], tail_second[0])
@@ -1022,18 +1126,27 @@
     lines = small_now[0].shape[0] // 2
     lines_tail = tail_rows[0].shape[0] // 2
     got_last = swap(tail_second[2], "fsdp", 1)
-    chains, (got_last, d_ext, squares) = advance(
-        [*chains, (reduce_steps(True), ahead)], (got_last, tail_second[3], squares)
-    )
+    lead = [(reduce_steps(True), ahead)]
+    lead, (got_last, d_ext, squares) = advance(lead, (got_last, tail_second[3], squares))
+    chains = chains + lead
     last = joined(tail_second[1], got_last)
     last_steps = reduce_steps(False)
     n_fsdp = len(bits_of(fsdp)) - 1
     for bit in bits_of(fsdp):
         tail_rows = fsdp_selected(tail_rows, bit)
+    for_halo = None
+    halo_steps = [gather_step(bit) for bit in bits_of(ctx)]
+    sum_steps = [sum_step(bit) for bit in bits_of(fsdp)]
     while last_steps:
         for_last = [([last_steps.pop(0)], last)]
-        chains, tail_rows = advance([*for_last, *chains], tail_rows)
+        more = [(halo_steps or sum_steps, for_halo)] if for_halo is not None else []
+        chains, tail_rows = advance([*for_last, *chains, *more], tail_rows)
         last = chains.pop(0)[1]
+        if more:
+            for_halo = chains.pop()[1]
+            if not halo_steps and halo_got is None:
+                halo_got = for_halo.astype(F32)
+                for_halo = halo_vector(halo_got)
         n_fsdp -= 1
         if n_fsdp == 0:
             extra = jnp.concatenate(
@@ -1045,8 +1158,17 @@
                 axis=0,
             ).reshape(1, -1, half)
             last = jnp.concatenate([last, extra], axis=1)
+        if n_fsdp == -1:
+            last, d_ext, squares = together(last, d_ext, squares)
+            for_halo, halo_got = halo_start(d_ext, squares), None
     while any(steps_left for steps_left, _ in chains):
         chains, _ = advance(chains)
+    while halo_steps or sum_steps:
+        [(_, for_halo)], _ = advance([(halo_steps or sum_steps, for_halo)])
+        if not halo_steps and halo_got is None:
+            halo_got = for_halo.astype(F32)
+            for_halo = halo_vector(halo_got)
+    vector = for_halo
     out_now, gate_now, ahead = [values for _, values in chains]
     sum_x = [ahead[0], last[0, :depth]]
     extra = last[0, depth:].reshape(128, 2 * part)
@@ -1054,21 +1176,6 @@
     sum_tail = one_above(extra[lines : lines + lines_tail], part).astype(F32)
 
     d_normed = d_ext.reshape(2, ext, features)
-    halo_grad = d_normed[:, HALO - 3 : HALO]
-    unit = rows_ext * inv_rms
-    grad_gain = jnp.sum(d_normed[:, HALO - 3 :] * unit[:, HALO - 3 :], axis=(0, 1))
-    square = jnp.pad(jnp.stack(three_parts(jnp.sum(squares))), (0, features - 3))
-    halo_sent = jnp.concatenate(
-        [halo_grad.reshape(6, features).astype(BF16), square[None], grad_gain.astype(BF16)[None]]
-    )
-    halo_got = gather_small_ctx(halo_sent).astype(F32)
-    vector = jnp.concatenate(
-        [
-            to_blocks(jnp.sum(halo_got[:, 7], axis=0)[None], depth)[0],
-            jnp.pad(jnp.sum(halo_got[:, 6, 0:3])[None], (0, LANES - 1)),
-        ]
-    )
-    vector = total(vector, ("fsdp",))
     sum_gain = lax.dynamic_slice_in_dim(vector, me_fsdp * depth, depth)
     loss = vector[features] / (count * features)
     halo_all = halo_got[:, 0:6].reshape(ctx, 2, 3, features)

time: 514 us -> 471 us (0.916)
  waiting for transfers between devices: 105 us -> 73.6 us
  Pallas kernels: 213 us -> 204 us
    ppermute x75 -> x72, waiting for transfers between devices: 105 us -> 73.6 us  [swap(): return lax.ppermute(values, axis, [(i, i ^ bit) for i in range(size)])]
    unnamed x155 -> x201, local copies, waits for them, and re-layouts: 4.48 us -> 14.8 us
    ppermute x75 -> x72, starting transfers between devices: 78.7 us -> 69.4 us  [swap(): return lax.ppermute(values, axis, [(i, i ^ bit) for i in range(size)])]
    pallas_call x10, Pallas kernels: 207 us -> 198 us  [call(): pl.pallas_call(kernel, grid_spec=pltpu.PrefetchScalarGridSpec(num_scalar_...]
    all_to_all x0 -> x1, starting transfers between devices: none -> 5.81 us  [local(): tails = lax.all_to_all(last_rows, 'ctx', 0, 0)]
  transfers between devices with their start and end apart: 75 -> 73, of which waited for: 25 -> 17; matrix products, arithmetic and copies ran while one was open for 15% -> 13% of each run, Pallas kernels for 30% -> 31%
where the time goes in v3:
time: 471 us; the launch traced here: 463 us
  Pallas kernels  204 us (43%)
  starting transfers between devices  75.2 us (16%)
  waiting for transfers between devices  73.6 us (16%)
  other arithmetic  62 us (13%)
  local copies, waits for them, and re-layouts  35 us (7%)
  between operations  13 us (3%)
    pallas_call x10, Pallas kernels, call(): pl.pallas_call(kernel, grid_spec=pltpu.PrefetchScalarGridSpec(num_scalar_...  198 us
    ppermute x72, waiting for transfers between devices, swap(): return lax.ppermute(values, axis, [(i, i ^ bit) for i in range(size)])  73.6 us
    ppermute x72, starting transfers between devices, swap(): return lax.ppermute(values, axis, [(i, i ^ bit) for i in range(size)])  69.4 us
    convert_element_type x23, other arithmetic, joined(): return (kept.astype(F32) + received.astype(F32)).astype(BF16)  15.6 us
    unnamed x201, local copies, waits for them, and re-layouts  14.8 us
  transfers between devices with their start and end apart: 73, of which 17 were waited for; matrix products, arithmetic and copies ran while one was open for 13% of the time, Pallas kernels for 31%

profile of v3, /device:TPU:0, one launch (start us, length us, event | category | flops | bytes accessed | tf_op | source)
XLA Modules:
  0.0 462.7 jit_solution(760314515814893567)
XLA Ops:
  5.9 5.8 %all-to-all-start = ((bf16[8,2,3,1024]{3,1,2,0:T(2,128)(2,1)}), bf16[8,2,3,1024]{3,1,2,0:T(2,128)(2,1)S(1)}, u32[]{:S(2)}, u32[]{:S(2)}) async-start(bf16[8,2,3,1024]{3,1,2,0:T(2,128)(2,1)} %broadcast_in_dim.127), calls=%async_computation | async-start | bytes 196608 | tf_op jit(solution)/shard_map/all_to_all | solution.py:792
  20.6 3.1 concatenate.171
  32.2 10.3 %collective-permute-done.1.refs_6_.refs_2_ = bf16[256,1024]{1,0:T(8,128)(2,1)S(1)} collective-permute-done((bf16[256,1024]{1,0:T(8,128)(2,1)S(1)}, bf16[256,1024]{1,0:T(8,128)(2,1)S(1)}, u32[]{:S(2)}, u32[]{:S(2)}) %collective-permute-start.1) | collective-permute-done | bytes 524320 | tf_op jit(solution)/shard_map/ppermute | solution.py:32
  47.6 13.3 %inputs.1 = (bf16[2,272,2048]{2,1,0:T(8,128)(2,1)S(1)}, f32[2,256,2048]{2,1,0:T(8,128)S(1)}, bf16[2,256,2048]{2,1,0:T(8,128)(2,1)S(1)}, f32[512,96]{1,0:T(8,128)S(1)}) custom-call(s32[3]{0:T(128)S(1)} %pad_add_fusion.3.scal, bf16[544,1024]{1,0:T(8,128)(2,1)S(1)} %fusion.1.normed_ref, bf16[256,1024]{1,0:T(8,128)(2,1)S(1)} %copy-done.12, ...), custom_call_target="tpu_custom_call" | custom-call | flops 2147483648 | bytes 14811136 | tf_op jit(solution)/shard_map/inputs/pallas_call | solution.py:673
  64.3 3.3 collective-permute-done.2.refs_2_
  70.6 16.3 %end_states.1 = (f32[2,32,8,2048]{3,2,1,0:T(8,128)S(1)}, bf16[40,2048]{1,0:T(8,128)(2,1)S(1)}) custom-call(s32[3]{0:T(128)S(1)} %pad_add_fusion.3.scal, f32[512,96]{1,0:T(8,128)S(1)} %get-tuple-element.178.proj_ref.refs_13_.refs_15_, bf16[192,2048]{1,0:T(8,128)(2,1)S(1)} %constant_dynamic-update-slice_fusion.refs_8_.s_ref.refs_16_, ...), custom_call_target="tpu_custom_call" | custom-call | flops 83886080 | bytes 11632640 | tf_op jit(solution)/shard_map/end_states/pallas_call | solution.py:673
  91.4 6.8 %gates.1.refs_11_.gate_ref = f32[2,256,2048]{2,1,0:T(8,128)S(1)} custom-call(s32[3]{0:T(128)S(1)} %pad_add_fusion.3.scal, bf16[544,1024]{1,0:T(8,128)(2,1)S(1)} %fusion.1.normed_ref, bf16[256,2048]{1,0:T(8,128)(2,1)} %slice.295.refs_0_, bf16[256,2048]{1,0:T(8,128)(2,1)S(1)} %collective-permute-done.13.refs_1_, ...), custom_call_target="tpu_custom_call" | custom-call | flops 2147483648 | bytes 9502720 | tf_op jit(solution)/shard_map/gates/pallas_call | solution.py:673
  100.3 3.8 collective-permute-done.11.refs_3_.refs_10_
  114.2 3.4 pad_maximum_fusion.refs_14_.weight_ref
  118.1 3.5 collective-permute-done.18.refs_4_.refs_11_
  124.9 36.7 %forward_states.1 = (f32[2,256,2048]{2,1,0:T(8,128)}, bf16[2,256,2048]{2,1,0:T(8,128)(2,1)}, bf16[16,2,256,16,128]{4,3,2,1,0:T(8,128)(2,1)}, f32[2,16,2048]{2,1,...) custom-call(s32[3]{0:T(128)} %copy-done.23, ...), custom_call_target="tpu_custom_call" | custom-call | flops 167772160 | bytes 67452928 | tf_op jit(solution)/shard_map/forward_states/pallas_call | solution.py:673
  161.6 22.6 %first_grads.1 = (f32[2,32,8,2048]{3,2,1,0:T(8,128)}, bf16[2,256,2048]{2,1,0:T(8,128)(2,1)}, f32[1,2048]{1,0:T(1,128)}, bf16[32,2048]{1,0:T(8,128)(2,1)}) custom-call(s32[3]{0:T(128)} %copy-done.23, bf16[512,1024]{1,0:T(8,128)(2,1)} %get-tuple-element.204.dout_ref, bf16[2048,1024]{1,0:T(8,128)(2,1)} %pad_maximum_fusion.refs_14_.weight_ref, ...), custom_call_target="tpu_custom_call" | custom-call | flops 100663296 | bytes 31334400 | tf_op jit(solution)/shard_map/first_grads/pallas_call | solution.py:673
  189.1 11.9 %gate_grads.1 = (bf16[2,256,2048]{2,1,0:T(8,128)(2,1)}, bf16[2,256,2048]{2,1,0:T(8,128)(2,1)}, f32[544,1024]{1,0:T(8,128)}) custom-call(s32[3]{0:T(128)} %copy-done.23, bf16[544,1024]{1,0:T(8,128)(2,1)} %copy-done.1, bf16[2,256,2048]{2,1,0:T(8,128)(2,1)} %get-tuple-element.208.dgate_ref, bf16[256,2048]{1,0:T(8,128)(2,1)} %slice.295.refs_0_, ...), custom_call_target="tpu_custom_call" | custom-call | flops 4294967296 | bytes 13828096 | tf_op jit(solution)/shard_map/gate_grads/pallas_call | solution.py:673
  201.1 5.8 %out_grads.1 = (bf16[2,512,1024]{2,1,0:T(8,128)(2,1)}, bf16[2,512,1024]{2,1,0:T(8,128)(2,1)}) custom-call(bf16[512,2048]{1,0:T(8,128)(2,1)} %bitcast.125, bf16[512,2048]{1,0:T(8,128)(2,1)} %bitcast.126, bf16[512,1024]{1,0:T(8,128)(2,1)} %get-tuple-element.204.dout_ref), custom_call_target="tpu_custom_call" | custom-call | flops 2147483648 | bytes 9437184 | tf_op jit(solution)/shard_map/out_grads/pallas_call | solution.py:966
  226.1 32.8 %backward_states.2 = (f32[2,256,1024]{2,1,0:T(8,128)}, f32[88,1024]{1,0:T(8,128)}, f32[512,64]{1,0:T(8,128)}, f32[2,16,256]{2,1,0:T(8,128)}, f32[2,16,256]{2,1,0:T(8,128)}) custom-call(s32[3]{0:T(128)} %copy-done.23, bf16[32,2048]{1,0:T(8,128)(2,1)} %copy-done.58, bf16[32,2048]{1,0:T(8,128)(2,1)} %copy-done.55, bf16[32,2048]{1,0:T(8,128)(2,1)} %copy-done.59, ...), custom_call_target="tpu_custom_call" | custom-call | flops 134217728 | bytes 54214656 | tf_op jit(solution)/shard_map/backward_states/pallas_call | solution.py:673
  268.6 32.7 %backward_states.3 = (f32[2,256,1024]{2,1,0:T(8,128)}, f32[88,1024]{1,0:T(8,128)}, f32[512,64]{1,0:T(8,128)}, f32[2,16,256]{2,1,0:T(8,128)}, f32[2,16,256]{2,1,0:T(8,128)}) custom-call(s32[3]{0:T(128)} %copy-done.23, bf16[32,2048]{1,0:T(8,128)(2,1)} %copy-done.58, bf16[32,2048]{1,0:T(8,128)(2,1)} %copy-done.55, bf16[32,2048]{1,0:T(8,128)(2,1)} %copy-done.59, ...), custom_call_target="tpu_custom_call" | custom-call | flops 134217728 | bytes 54214656 | tf_op jit(solution)/shard_map/backward_states/pallas_call | solution.py:673
  310.2 12.6 %tail_grads.2 = (f32[104,1024]{1,0:T(8,128)}, bf16[2,256,1024]{2,1,0:T(8,128)(2,1)}, bf16[2,256,1024]{2,1,0:T(8,128)(2,1)}, f32[544,1024]{1,0:T(8,128)}) custom-call(s32[3]{0:T(128)} %copy-done.23, bf16[512,96]{1,0:T(8,128)(2,1)} %pad_maximum_fusion.14.dproj_ref, bf16[192,2048]{1,0:T(8,128)(2,1)} %copy-done.4, f32[2,256,1024]{2,1,0:T(8,128)} %get-tuple-element.260.dlow_ref, ...), custom_call_target="tpu_custom_call" | custom-call | flops 2147483648 | bytes 23789568 | tf_op jit(solution)/shard_map/tail_grads/pallas_call | solution.py:673
  327.6 12.5 %tail_grads.3 = (f32[104,1024]{1,0:T(8,128)}, bf16[2,256,1024]{2,1,0:T(8,128)(2,1)}, bf16[2,256,1024]{2,1,0:T(8,128)(2,1)}, f32[544,1024]{1,0:T(8,128)}) custom-call(s32[3]{0:T(128)} %copy-done.23, bf16[512,96]{1,0:T(8,128)(2,1)} %pad_maximum_fusion.14.dproj_ref, bf16[192,2048]{1,0:T(8,128)(2,1)} %copy-done.4, f32[2,256,1024]{2,1,0:T(8,128)} %get-tuple-element.260.dlow_ref, ...), custom_call_target="tpu_custom_call" | custom-call | flops 2147483648 | bytes 23789568 | tf_op jit(solution)/shard_map/tail_grads/pallas_call | solution.py:673
  346.8 8.7 %collective-permute-done.43 = bf16[2,128,1024]{2,1,0:T(8,128)(2,1)S(1)} collective-permute-done((bf16[2,128,1024]{2,1,0:T(8,128)(2,1)S(1)}, bf16[2,128,1024]{2,1,0:T(8,128)(2,1)S(1)}, u32[]{:S(2)}, u32[]{:S(2)}) %collective-permute-start.43) | collective-permute-done | bytes 524320 | tf_op jit(solution)/shard_map/ppermute | solution.py:32
  358.8 5.8 %collective-permute-done.48 = bf16[2,64,1024]{2,1,0:T(8,128)(2,1)S(1)} collective-permute-done((bf16[2,64,1024]{2,1,0:T(8,128)(2,1)S(1)}, bf16[2,64,1024]{2,1,0:T(8,128)(2,1)S(1)}, u32[]{:S(2)}, u32[]{:S(2)}) %collective-permute-start.48) | collective-permute-done | bytes 262176 | tf_op jit(solution)/shard_map/ppermute | solution.py:32
  364.6 4.2 collective-permute-done.45
  377.4 13.0 %collective-permute-done.55 = bf16[2,32,1024]{2,1,0:T(8,128)(2,1)S(1)} collective-permute-done((bf16[2,32,1024]{2,1,0:T(8,128)(2,1)S(1)}, bf16[2,32,1024]{2,1,0:T(8,128)(2,1)S(1)}, u32[]{:S(2)}, u32[]{:S(2)}) %collective-permute-start.55) | collective-permute-done | bytes 131104 | tf_op jit(solution)/shard_map/ppermute | solution.py:32
  427.4 3.2 collective-permute-done.66
  446.7 6.1 %collective-permute-done.70 = bf16[1,192,1024]{2,1,0:T(8,128)(2,1)S(1)} collective-permute-done((bf16[1,192,1024]{2,1,0:T(8,128)(2,1)S(1)}, bf16[1,192,1024]{2,1,0:T(8,128)(2,1)S(1)}, u32[]{:S(2)}, u32[]{:S(2)}) %collective-permute-start.70) | collective-permute-done | bytes 393248 | tf_op jit(solution)/shard_map/ppermute | solution.py:32
  (527 shorter events, 171.7 us)
Async XLA Ops:
  2.1 22.8 %collective-permute-start = (bf16[256,1024]{1,0:T(8,128)(2,1)S(1)}, bf16[256,1024]{1,0:T(8,128)(2,1)S(1)}, u32[]{:S(2)}, u32[]{:S(2)}) collective-permute-start(bf16[256,1024]{1,0:T(8,128)(2,1)S(1)} %get-tuple-element.175.refs_0_), channel_id=1, source_target_pairs={{0,2},{1,3},{2,0},{3,1},{4,6},{5,7},{6,4},{7,5},{8,10},{9,11},{10,... | collective-permute-start | bytes 1572872 | tf_op jit(solution)/shard_map/ppermute | solution.py:32
  5.9 18.9 %all-to-all-start = ((bf16[8,2,3,1024]{3,1,2,0:T(2,128)(2,1)}), bf16[8,2,3,1024]{3,1,2,0:T(2,128)(2,1)S(1)}, u32[]{:S(2)}, u32[]{:S(2)}) async-start(bf16[8,2,3,1024]{3,1,2,0:T(2,128)(2,1)} %broadcast_in_dim.127), calls=%async_computation | async-start | bytes 196608 | tf_op jit(solution)/shard_map/all_to_all | solution.py:792
  29.3 16.8 %collective-permute-start.8 = (bf16[256,1024]{1,0:T(8,128)(2,1)S(1)}, bf16[256,1024]{1,0:T(8,128)(2,1)}, u32[]{:S(2)}, u32[]{:S(2)}) collective-permute-start(bf16[256,1024]{1,0:T(8,128)(2,1)S(1)} %get-tuple-element.170.refs_4_.refs_0_), channel_id=1, source_target_pairs={{0,1},{1,0},{2,3},{3,2},{4,5},{5,4},{6,7},{7,6},{8,9},{9,8},{10,11... | collective-permute-start | bytes 1572872 | tf_op jit(solution)/shard_map/ppermute | solution.py:32
  42.5 25.1 %collective-permute-start.2 = (bf16[256,2048]{1,0:T(8,128)(2,1)}, bf16[256,2048]{1,0:T(8,128)(2,1)S(1)}, u32[]{:S(2)}, u32[]{:S(2)}) collective-permute-start(bf16[256,2048]{1,0:T(8,128)(2,1)} %slice.295.refs_0_), channel_id=1, source_target_pairs={{0,2},{1,3},{2,0},{3,1},{4,6},{5,7},{6,4},{7,5},{8,10},{9,11},{10,... | collective-permute-start | bytes 3145736 | tf_op jit(solution)/shard_map/ppermute | solution.py:32
  67.5 23.8 %collective-permute-start.13 = (bf16[256,2048]{1,0:T(8,128)(2,1)}, bf16[256,2048]{1,0:T(8,128)(2,1)S(1)}, u32[]{:S(2)}, u32[]{:S(2)}) collective-permute-start(bf16[256,2048]{1,0:T(8,128)(2,1)} %slice.295.refs_0_), channel_id=1, source_target_pairs={{0,1},{1,0},{2,3},{3,2},{4,5},{5,4},{6,7},{7,6},{8,9},{9,8},{10,11... | collective-permute-start | bytes 3145736 | tf_op jit(solution)/shard_map/ppermute | solution.py:32
  67.5 23.9 %collective-permute-start.14 = (bf16[256,2048]{1,0:T(8,128)(2,1)S(1)}, bf16[256,2048]{1,0:T(8,128)(2,1)S(1)}, u32[]{:S(2)}, u32[]{:S(2)}) collective-permute-start(bf16[256,2048]{1,0:T(8,128)(2,1)S(1)} %collective-permute-done.2.refs_2_), channel_id=1, source_target_pairs={{0,1},{1,0},{2,3},{3,2},{4,5},{5,4},{6,7},{7,6},{8,9},{9,8},{10,11... | collective-permute-start | bytes 3145736 | tf_op jit(solution)/shard_map/ppermute | solution.py:32
  68.1 36.0 %collective-permute-start.15 = (bf16[512,1024]{1,0:T(8,128)(2,1)S(1)}, bf16[512,1024]{1,0:T(8,128)(2,1)}, u32[]{:S(2)}, u32[]{:S(2)}) collective-permute-start(bf16[512,1024]{1,0:T(8,128)(2,1)S(1)} %copy-done.46), channel_id=1, source_target_pairs={{0,2},{1,3},{2,0},{3,1},{4,6},{5,7},{6,4},{7,5},{8,10},{9,11},{10,... | collective-permute-start | bytes 3145736 | tf_op jit(solution)/shard_map/ppermute | solution.py:32
  184.2 22.7 %collective-permute-start.22 = (bf16[32,2048]{1,0:T(8,128)(2,1)}, bf16[32,2048]{1,0:T(8,128)(2,1)S(1)}, u32[]{:S(2)}, u32[]{:S(2)}) collective-permute-start(bf16[32,2048]{1,0:T(8,128)(2,1)} %get-tuple-element.214), channel_id=1, source_target_pairs={{0,8},{4,12},{8,0},{12,4},{16,24},{20,28},{24,16},{28,20},{1,9},{5... | collective-permute-start | bytes 393224 | tf_op jit(solution)/shard_map/ppermute | solution.py:32
  186.7 20.2 %collective-permute-start.23 = (bf16[32,2048]{1,0:T(8,128)(2,1)}, bf16[32,2048]{1,0:T(8,128)(2,1)S(1)}, u32[]{:S(2)}, u32[]{:S(2)}) collective-permute-start(bf16[32,2048]{1,0:T(8,128)(2,1)} %get-tuple-element.214), channel_id=1, source_target_pairs={{0,16},{4,20},{8,24},{12,28},{16,0},{20,4},{24,8},{28,12},{1,17},{... | collective-permute-start | bytes 393224 | tf_op jit(solution)/shard_map/ppermute | solution.py:32
  187.7 19.2 %collective-permute-start.24 = (bf16[32,2048]{1,0:T(8,128)(2,1)}, bf16[32,2048]{1,0:T(8,128)(2,1)S(1)}, u32[]{:S(2)}, u32[]{:S(2)}) collective-permute-start(bf16[32,2048]{1,0:T(8,128)(2,1)} %get-tuple-element.214), channel_id=1, source_target_pairs={{0,24},{4,28},{8,16},{12,20},{16,8},{20,12},{24,0},{28,4},{1,25},{... | collective-permute-start | bytes 393224 | tf_op jit(solution)/shard_map/ppermute | solution.py:32
  223.2 35.7 %collective-permute-start.31 = (bf16[1,512,1024]{2,1,0:T(8,128)(2,1)}, bf16[1,512,1024]{2,1,0:T(8,128)(2,1)}, u32[]{:S(2)}, u32[]{:S(2)}) collective-permute-start(bf16[1,512,1024]{2,1,0:T(8,128)(2,1)} %slice.311), channel_id=1, source_target_pairs={{0,2},{1,3},{2,0},{3,1},{4,6},{5,7},{6,4},{7,5},{8,10},{9,11},{10,... | collective-permute-start | bytes 3145736 | tf_op jit(solution)/shard_map/ppermute | solution.py:32
  225.0 33.9 %collective-permute-start.32 = (bf16[2,128,2048]{2,1,0:T(8,128)(2,1)}, bf16[2,128,2048]{2,1,0:T(8,128)(2,1)S(1)}, u32[]{:S(2)}, u32[]{:S(2)}) collective-permute-start(bf16[2,128,2048]{2,1,0:T(8,128)(2,1)} %broadcast_select_fusion), channel_id=1, source_target_pairs={{0,8},{4,12},{8,0},{12,4},{16,24},{20,28},{24,16},{28,20},{1,9},{5... | collective-permute-start | bytes 3145736 | tf_op jit(solution)/shard_map/ppermute | solution.py:32
  262.8 38.4 %collective-permute-start.33 = (bf16[1,256,1024]{2,1,0:T(8,128)(2,1)}, bf16[1,256,1024]{2,1,0:T(8,128)(2,1)}, u32[]{:S(2)}, u32[]{:S(2)}) collective-permute-start(bf16[1,256,1024]{2,1,0:T(8,128)(2,1)} %broadcast_select_fusion.7), channel_id=1, source_target_pairs={{0,4},{4,0},{8,12},{12,8},{16,20},{20,16},{24,28},{28,24},{1,5},{5... | collective-permute-start | bytes 1572872 | tf_op jit(solution)/shard_map/ppermute | solution.py:32
  265.4 35.9 %collective-permute-start.34 = (bf16[2,64,2048]{2,1,0:T(8,128)(2,1)S(1)}, bf16[2,64,2048]{2,1,0:T(8,128)(2,1)S(1)}, u32[]{:S(2)}, u32[]{:S(2)}) collective-permute-start(bf16[2,64,2048]{2,1,0:T(8,128)(2,1)S(1)} %broadcast_select_fusion.4), channel_id=1, source_target_pairs={{0,16},{4,20},{8,24},{12,28},{16,0},{20,4},{24,8},{28,12},{1,17},{... | collective-permute-start | bytes 1572872 | tf_op jit(solution)/shard_map/ppermute | solution.py:32
  304.3 18.6 %collective-permute-start.35 = (bf16[1,128,1024]{2,1,0:T(8,128)(2,1)}, bf16[1,128,1024]{2,1,0:T(8,128)(2,1)}, u32[]{:S(2)}, u32[]{:S(2)}) collective-permute-start(bf16[1,128,1024]{2,1,0:T(8,128)(2,1)} %broadcast_select_fusion.19), channel_id=1, source_target_pairs={{0,8},{4,12},{8,0},{12,4},{16,24},{20,28},{24,16},{28,20},{1,9},{5... | collective-permute-start | bytes 786440 | tf_op jit(solution)/shard_map/ppermute | solution.py:32
  305.6 17.2 %collective-permute-start.36 = (bf16[2,32,2048]{2,1,0:T(8,128)(2,1)S(1)}, bf16[2,32,2048]{2,1,0:T(8,128)(2,1)S(1)}, u32[]{:S(2)}, u32[]{:S(2)}) collective-permute-start(bf16[2,32,2048]{2,1,0:T(8,128)(2,1)S(1)} %broadcast_select_fusion.16), channel_id=1, source_target_pairs={{0,4},{4,0},{8,12},{12,8},{16,20},{20,16},{24,28},{28,24},{1,5},{5... | collective-permute-start | bytes 786440 | tf_op jit(solution)/shard_map/ppermute | solution.py:32
  323.5 16.6 %collective-permute-start.39 = (bf16[2,256,1024]{2,1,0:T(8,128)(2,1)}, bf16[2,256,1024]{2,1,0:T(8,128)(2,1)S(1)}, u32[]{:S(2)}, u32[]{:S(2)}) collective-permute-start(bf16[2,256,1024]{2,1,0:T(8,128)(2,1)} %get-tuple-element.277), channel_id=1, source_target_pairs={{0,1},{1,0},{2,3},{3,2},{4,5},{5,4},{6,7},{7,6},{8,9},{9,8},{10,11... | collective-permute-start | bytes 3145736 | tf_op jit(solution)/shard_map/ppermute | solution.py:32
  327.5 16.7 %collective-permute-start.50 = (bf16[104,512]{1,0:T(8,128)(2,1)S(1)}, bf16[104,512]{1,0:T(8,128)(2,1)S(1)}, u32[]{:S(2)}, u32[]{:S(2)}) collective-permute-start(bf16[104,512]{1,0:T(8,128)(2,1)S(1)} %broadcast_select_fusion.31), channel_id=1, source_target_pairs={{0,1},{1,0},{2,3},{3,2},{4,5},{5,4},{6,7},{7,6},{8,9},{9,8},{10,11... | collective-permute-start | bytes 319496 | tf_op jit(solution)/shard_map/ppermute | solution.py:32
  341.8 17.0 %collective-permute-start.46 = (bf16[1,64,1024]{2,1,0:T(8,128)(2,1)S(1)}, bf16[1,64,1024]{2,1,0:T(8,128)(2,1)S(1)}, u32[]{:S(2)}, u32[]{:S(2)}) collective-permute-start(bf16[1,64,1024]{2,1,0:T(8,128)(2,1)S(1)} %add_convert_fusion.17), channel_id=1, source_target_pairs={{0,16},{4,20},{8,24},{12,28},{16,0},{20,4},{24,8},{28,12},{1,17},{... | collective-permute-start | bytes 393224 | tf_op jit(solution)/shard_map/ppermute | solution.py:32
  369.3 21.7 %collective-permute-start.52 = (bf16[1,192,1024]{2,1,0:T(8,128)(2,1)S(1)}, bf16[1,192,1024]{2,1,0:T(8,128)(2,1)S(1)}, u32[]{:S(2)}, u32[]{:S(2)}) collective-permute-start(bf16[1,192,1024]{2,1,0:T(8,128)(2,1)S(1)} %broadcast_select_fusion.10), channel_id=1, source_target_pairs={{0,4},{4,0},{8,12},{12,8},{16,20},{20,16},{24,28},{28,24},{1,5},{5... | collective-permute-start | bytes 1179656 | tf_op jit(solution)/shard_map/ppermute | solution.py:32
  370.3 20.0 %collective-permute-start.53 = (bf16[1,128,1024]{2,1,0:T(8,128)(2,1)S(1)}, bf16[1,128,1024]{2,1,0:T(8,128)(2,1)}, u32[]{:S(2)}, u32[]{:S(2)}) collective-permute-start(bf16[1,128,1024]{2,1,0:T(8,128)(2,1)S(1)} %pad_maximum_fusion.7), channel_id=1, source_target_pairs={{0,8},{4,12},{8,0},{12,4},{16,24},{20,28},{24,16},{28,20},{1,9},{5... | collective-permute-start | bytes 786440 | tf_op jit(solution)/shard_map/ppermute | solution.py:32
  372.2 18.1 %collective-permute-start.54 = (bf16[1,64,2048]{2,1,0:T(8,128)(2,1)}, bf16[1,64,2048]{2,1,0:T(8,128)(2,1)}, u32[]{:S(2)}, u32[]{:S(2)}) collective-permute-start(bf16[1,64,2048]{2,1,0:T(8,128)(2,1)} %pad_maximum_fusion.8), channel_id=1, source_target_pairs={{0,16},{4,20},{8,24},{12,28},{16,0},{20,4},{24,8},{28,12},{1,17},{... | collective-permute-start | bytes 786440 | tf_op jit(solution)/shard_map/ppermute | solution.py:32
  391.9 19.2 %collective-permute-start.56 = (bf16[1,96,1024]{2,1,0:T(8,128)(2,1)}, bf16[1,96,1024]{2,1,0:T(8,128)(2,1)}, u32[]{:S(2)}, u32[]{:S(2)}) collective-permute-start(bf16[1,96,1024]{2,1,0:T(8,128)(2,1)} %broadcast_select_fusion.22), channel_id=1, source_target_pairs={{0,8},{4,12},{8,0},{12,4},{16,24},{20,28},{24,16},{28,20},{1,9},{5... | collective-permute-start | bytes 589832 | tf_op jit(solution)/shard_map/ppermute | solution.py:32
  394.0 17.1 %collective-permute-start.57 = (bf16[1,256,1024]{2,1,0:T(8,128)(2,1)}, bf16[1,256,1024]{2,1,0:T(8,128)(2,1)}, u32[]{:S(2)}, u32[]{:S(2)}) collective-permute-start(bf16[1,256,1024]{2,1,0:T(8,128)(2,1)} %pad_maximum_fusion.3), channel_id=1, source_target_pairs={{0,4},{4,0},{8,12},{12,8},{16,20},{20,16},{24,28},{28,24},{1,5},{5... | collective-permute-start | bytes 1572872 | tf_op jit(solution)/shard_map/ppermute | solution.py:32
  (145 other events, 1339.9 us)

commit v4 on v3

--- a/solution.py
+++ b/solution.py
@@ -330,7 +330,7 @@
     rest = refs[ctx + 7 :]
     scale_ref, tokens_ref, teacher_ref = rest[:3]
     ssm_ref, branch_ref, hidden_ref, start_ref, out_ref, gout_ref, dout_ref, square_ref = rest[3:11]
-    drive_ref, read_ref, odd_ref, even_ref, acc_ref, cdiag_ref = rest[11:]
+    drive_ref, read_ref, acc_ref, cdiag_ref = rest[11:]
     piece = groups * 8
     width = tiles * LANES
     states = b_ref.shape[2]
@@ -353,7 +353,7 @@
             held.append(carried(ends, logs, rates[j], h, ctx, states, tile_cols(j)))
             start_ref[h, :, tile_cols(j)] = held[-1]
 
-    def scan(t, held, keep_ref):
+    def scan(t, held):
         held = list(held)
         for s in range(16):
             p = t * 16 + s
@@ -365,31 +365,24 @@
                     drive = drive_ref[h, t * 2 + s // 8, s % 8 : s % 8 + 1, cols]
                     k = h * tiles + j
                     held[k] = jnp.exp2(step * rates[j]) * held[k] + drive * b
-                    low = held[k].astype(BF16)
-                    hidden_ref[j, h, p] = low
-                    keep_ref[h, j, s * states : (s + 1) * states, :] = low
+                    hidden_ref[j, h, p] = held[k].astype(BF16)
         return tuple(held)
 
-    def read(t, keep_ref):
+    def read(t):
         for h in range(2):
             for j in range(tiles):
-                out = dot(cdiag_ref[h, t], keep_ref[h, j])
+                low = hidden_ref[j, h, pl.ds(t * 16, 16)].reshape(16 * states, LANES)
+                out = dot(cdiag_ref[h, t], low)
                 read_ref[h, t * 2, :, tile_cols(j)] = out[0:8]
                 read_ref[h, t * 2 + 1, :, tile_cols(j)] = out[8:16]
 
-    def body(k, held):
-        t = 2 * k + 1
-        read(t - 1, even_ref)
-        held = scan(t, held, odd_ref)
-        read(t, odd_ref)
-        return scan(t + 1, held, even_ref)
+    def body(t, held):
+        read(t - 1)
+        return scan(t, held)
 
     blocks = groups // 2
-    held = scan(0, held, even_ref)
-    held = lax.fori_loop(0, blocks // 2 - 1, body, held)
-    read(blocks - 2, even_ref)
-    scan(blocks - 1, held, odd_ref)
-    read(blocks - 1, odd_ref)
+    lax.fori_loop(1, blocks, body, scan(0, tuple(held)))
+    read(blocks - 1)
     branches = []
     for h in range(2):
         ssm = read_ref[h].reshape(piece, width) + head[6:7] * xs_ref[h].astype(F32)
@@ -498,7 +491,7 @@
     (
         plan_ref, proj_ref, s_ref, step_ref, xs_ref, c_ref, start_ref, dssm_ref, hidden_ref,
         dxs_ref, small_ref, ddelta_ref, db_ref, dc_ref,
-        adj_ref, dstep_ref, dbs_ref, dcs_ref, adj_odd, adj_even, term_odd, term_even, bdiag_ref,
+        adj_ref, dstep_ref, dbs_ref, dcs_ref, bdiag_ref,
     ) = refs[2 * ctx - 2 :]
     piece = groups * 8
     width = tiles * LANES
@@ -522,8 +515,10 @@
     same = (col16 // states == row16).astype(F32)
     same_low = same.astype(BF16)
 
-    def scan(t, first, later, sums, adj_keep, term_keep):
+    def work(t, first, later, sums):
         for h in range(2):
+            adjoints = [[None] * 16 for _ in range(tiles)]
+            terms = [[None] * 16 for _ in range(tiles)]
             for s in range(15, -1, -1):
                 p = t * 16 + s
                 c = c_ref[h, p]
@@ -540,20 +535,16 @@
                     later[k] = jnp.exp2(step * rates2[j]) * adjoint
                     term = later[k] * before
                     sums[j] = sums[j] + term * step
-                    place = slice(s * states, (s + 1) * states)
-                    adj_keep[h, j, place, :] = adjoint.astype(BF16)
-                    term_keep[h, j, place, :] = (term * rates[j]).astype(BF16)
-
-    def products(t, adj_keep, term_keep):
-        for h in range(2):
+                    adjoints[j][s] = adjoint.astype(BF16)
+                    terms[j][s] = (term * rates[j]).astype(BF16)
             db = dc = None
             for j in range(tiles):
                 cols = tile_cols(j)
-                adjoint = adj_keep[h, j]
+                adjoint = jnp.concatenate(adjoints[j], axis=0)
                 out = dot(bdiag_ref[h, t], adjoint)
                 adj_ref[h, t * 2, :, cols] = out[0:8]
                 adj_ref[h, t * 2 + 1, :, cols] = out[8:16]
-                out = dot(same_low, term_keep[h, j])
+                out = dot(same_low, jnp.concatenate(terms[j], axis=0))
                 dstep_ref[h, t * 2, :, cols] = out[0:8]
                 dstep_ref[h, t * 2 + 1, :, cols] = out[8:16]
                 step = step_ref[h, pl.ds(t * 2, 2), :, cols].reshape(16, LANES)
@@ -569,11 +560,7 @@
 
     def body(k, both):
         later, sums = list(both[: 2 * tiles]), list(both[2 * tiles :])
-        t = blocks - 2 - 2 * k
-        products(t + 1, adj_odd, term_odd)
-        scan(t, False, later, sums, adj_even, term_even)
-        products(t, adj_even, term_even)
-        scan(t - 1, False, later, sums, adj_odd, term_odd)
+        work(blocks - 1 - k, False, later, sums)
         return tuple(later + sums)
 
     later = []
@@ -582,12 +569,9 @@
         for j in range(tiles):
             later.append(carried(grads, logs, rates2[j], h, ctx, states, tile_cols(j)))
     sums = [jnp.zeros((states, LANES), F32)] * tiles
-    scan(blocks - 1, False, later, sums, adj_odd, term_odd)
-    both = lax.fori_loop(0, blocks // 2 - 1, body, tuple(later + sums))
+    both = lax.fori_loop(0, blocks - 1, body, tuple(later + sums))
     later, sums = list(both[: 2 * tiles]), list(both[2 * tiles :])
-    products(1, adj_odd, term_odd)
-    scan(0, True, later, sums, adj_even, term_even)
-    products(0, adj_even, term_even)
+    work(0, True, later, sums)
     for j in range(tiles):
         small_ref[rank : rank + states, tile_cols(j)] = sums[j] * rates[j]
     delta = proj_ref[:, 0:rank].astype(BF16)
@@ -617,8 +601,8 @@
 
 
 def tail_kernel(
-    scal, dproj_ref, s_ref, dlow_ref, dhigh_ref, conv_ref, x_ref, xs_ref, normed_ref, before_ref, *refs,
-    count, piece, is_upper
+    scal, dproj_ref, s_ref, dxs_ref, conv_ref, x_ref, xs_ref, normed_ref, before_ref, *refs,
+    count, piece
 ):
     weights, (small_ref, keep_ref, send_ref, dnormed_ref, pad_ref) = refs[:count], refs[count:]
     depth = weights[0].shape[0]
@@ -632,7 +616,6 @@
             pad_ref[h, 0:HALO, :] = jnp.zeros((HALO, width), F32)
             pad_ref[h, ext : ext + 8, :] = jnp.zeros((8, width), F32)
 
-    upper = is_upper(pl.program_id(0), scal)
     head = s_ref[0:HEAD, :].astype(F32)
     small_ref[8:104, :] = rows_dot(dproj_ref[...], xs_ref[...].reshape(2 * piece, width))
     d_xs = dot(dproj_ref[...], s_ref[96:192, :])
@@ -641,8 +624,7 @@
     for h in range(2):
         conv = conv_ref[h]
         sig = sigmoid(conv)
-        dxs = jnp.where(upper, dhigh_ref[h], dlow_ref[h])
-        d_conv = (dxs + d_xs[h * piece : (h + 1) * piece]) * (sig * (1.0 + conv * (1.0 - sig)))
+        d_conv = (dxs_ref[h] + d_xs[h * piece : (h + 1) * piece]) * (sig * (1.0 + conv * (1.0 - sig)))
         pad_ref[h, HALO:ext, :] = d_conv
         x = x_ref[h].astype(F32)
         for k in range(4):
@@ -878,7 +860,6 @@
     diag_space = pltpu.VMEM((2, piece // 16, 16, 16 * states), BF16)
     hidden_spec = pl.BlockSpec((tiles, 2, piece, states, LANES), lambda i, scal: (i, 0, 0, 0, 0))
     start_spec = pl.BlockSpec((2, states, block), lambda i, scal: (0, 0, i))
-    keep_spaces = [pltpu.VMEM((2, tiles, 16 * states, LANES), BF16)]
     group_space = pltpu.VMEM((2, groups, 8, block), F32)
 
     step, sent = call(
@@ -928,7 +909,7 @@
             shape((rows_all, features), BF16),
             shape((8, features)),
         ],
-        [group_space] * 2 + keep_spaces * 2 + [pltpu.VMEM((rows_all, features), F32), diag_space],
+        [group_space] * 2 + [pltpu.VMEM((rows_all, features), F32), diag_space],
         10 * elements, elements,
     )
     d_ssm, d_gate, grad_skip, grads_first = call(
@@ -988,21 +969,21 @@
     back_near, core_out, core_gate = together(back_near, core_out, core_gate)
     chains = [(reduce_steps(False), core_out), (reduce_steps(True, 1), core_gate)]
 
-    def backward(c):
+    def backward():
         def at(i):
-            return i + c * per_half
+            return i
 
         return call(
             functools.partial(backward_kernel, tiles=tiles, groups=groups, ctx=ctx, rank=rank),
-            "backward_states", per_half, scal,
+            "backward_states", width // block, scal,
             (*back_near[1:], *near[1:], plan_behind, proj, small, step, xs, c_wide, starts, d_ssm, hidden),
             [
                 *([pl.BlockSpec((2 * states, block), lambda i, scal: (0, at(i)))] * (ctx - 1)),
                 *([pl.BlockSpec((2 * states + 8, block), lambda i, scal: (0, at(i)))] * (ctx - 1)),
                 plan_spec,
-                whole_spec(proj.shape), spec_small(block, c * per_half),
+                whole_spec(proj.shape), spec_small(block),
                 pl.BlockSpec((2, groups, 8, block), lambda i, scal: (0, 0, 0, at(i))),
-                spec_rows(block, c * per_half), wide_spec,
+                spec_rows(block), wide_spec,
                 pl.BlockSpec((2, states, block), lambda i, scal: (0, 0, at(i))),
                 pl.BlockSpec((2, groups, 8, block), lambda i, scal: (0, 0, 0, at(i))),
                 pl.BlockSpec((tiles, 2, piece, states, LANES), lambda i, scal: (at(i), 0, 0, 0, 0)),
@@ -1013,34 +994,23 @@
                 whole_spec((2, piece // 16, 16 * states)), whole_spec((2, piece // 16, 16 * states)),
             ],
             [
-                shape((2, piece, half)),
-                shape((rank + states + 8, half)),
+                shape((2, piece, width)),
+                shape((rank + states + 8, width)),
                 shape((rows_all, rank)),
                 shape((2, piece // 16, 16 * states)),
                 shape((2, piece // 16, 16 * states)),
             ],
-            [group_space] * 2 + [pltpu.VMEM((2, piece // 16, 16, 16 * states), F32)] * 2 + keep_spaces * 4
-            + [diag_space],
-            16 * elements // 2, elements // 2,
+            [group_space] * 2 + [pltpu.VMEM((2, piece // 16, 16, 16 * states), F32)] * 2 + [diag_space],
+            16 * elements, elements,
         )
 
-    chains, back_first = advance(chains, backward(0))
-    step, _ = together(step, [values for _, values in chains])
-    chains, back_second = advance(chains, backward(1))
-
-    def small_part(c, back):
-        rows = jnp.concatenate(
-            [back[1], grad_skip[:, c * half : (c + 1) * half], jnp.zeros((7, half), F32)], axis=0
-        ).astype(BF16)
-        return [rows[:, k * part : (k + 1) * part] for k in range(fsdp // 2)]
-
+    chains, back = advance(chains, backward())
+
+    small_rows = jnp.concatenate(
+        [back[1], grad_skip, jnp.zeros((7, width), F32)], axis=0
+    ).astype(BF16)
     d_proj = jnp.concatenate(
-        [
-            back_first[2] + back_second[2],
-            (back_first[3] + back_second[3]).reshape(rows_all, states),
-            (back_first[4] + back_second[4]).reshape(rows_all, states),
-        ],
-        axis=1,
+        [back[2], back[3].reshape(rows_all, states), back[4].reshape(rows_all, states)], axis=1
     ).astype(BF16)
     half_steps = steps // 2
 
@@ -1054,23 +1024,14 @@
             return pl.BlockSpec((2, dims, cb), lambda i, scal: (0, 0, place(i, scal)))
 
         return call(
-            functools.partial(
-                tail_kernel, count=fsdp, piece=piece,
-                is_upper=lambda i, scal: place(i, scal) >= half_blocks,
-            ),
+            functools.partial(tail_kernel, count=fsdp, piece=piece),
             "tail_grads", half_steps, scal,
-            (d_proj, small, back_first[0], back_second[0], conv, x_ext, xs, normed, d_before,
+            (d_proj, small, back[0], conv, x_ext, xs, normed, d_before,
              *(x_second if c else x_first)),
             [
                 whole_spec(d_proj.shape),
                 pl.BlockSpec((small.shape[0], cb), lambda i, scal: (0, place(i, scal))),
-                pl.BlockSpec(
-                    (2, piece, cb), lambda i, scal: (0, 0, jnp.minimum(place(i, scal), half_blocks - 1))
-                ),
-                pl.BlockSpec(
-                    (2, piece, cb), lambda i, scal: (0, 0, jnp.maximum(place(i, scal) - half_blocks, 0))
-                ),
-                at_rows(piece), at_rows(ext), at_rows(piece),
+                at_rows(piece), at_rows(piece), at_rows(ext), at_rows(piece),
                 whole_spec((2 * ext, features)), whole_spec((2 * ext, features)),
                 *([pl.BlockSpec((depth, cb), lambda i, scal: (0, i))] * fsdp),
             ],
@@ -1092,7 +1053,7 @@
     d_proj, d_before, _ = together(d_proj, d_before, [values for _, values in chains])
     chains, tail_first = advance(chains, tail(0, d_proj, d_before))
     got_ahead = swap(tail_first[2], "fsdp", 1)
-    small_now = small_part(0, back_first) + small_part(1, back_second)
+    small_now = [small_rows[:, k * part : (k + 1) * part] for k in range(fsdp)]
     for small_now in fsdp_blocks(small_now):
         pass
     d_proj, _ = together(d_proj, [values for _, values in chains])

time: 471 us -> 465 us (0.987)
    unnamed x201 -> x181, local copies, waits for them, and re-layouts: 14.8 us -> 11.4 us
    pallas_call x10 -> x9, Pallas kernels: 198 us -> 195 us  [call(): pl.pallas_call(kernel, grid_spec=pltpu.PrefetchScalarGridSpec(num_scalar_...]
  transfers between devices with their start and end apart: 73 -> 73, of which waited for: 17 -> 21; matrix products, arithmetic and copies ran while one was open for 13% -> 13% of each run, Pallas kernels for 31% -> 32%
where the time goes in v4:
time: 465 us; the launch traced here: 457 us
  Pallas kernels  201 us (43%)
  waiting for transfers between devices  77.8 us (17%)
  starting transfers between devices  72.8 us (16%)
  other arithmetic  61.1 us (13%)
  local copies, waits for them, and re-layouts  31.2 us (7%)
  between operations  12.6 us (3%)
    pallas_call x9, Pallas kernels, call(): pl.pallas_call(kernel, grid_spec=pltpu.PrefetchScalarGridSpec(num_scalar_...  195 us
    ppermute x72, waiting for transfers between devices, swap(): return lax.ppermute(values, axis, [(i, i ^ bit) for i in range(size)])  77.8 us
    ppermute x72, starting transfers between devices, swap(): return lax.ppermute(values, axis, [(i, i ^ bit) for i in range(size)])  67 us
    convert_element_type x23, other arithmetic, joined(): return (kept.astype(F32) + received.astype(F32)).astype(BF16)  18 us
    unnamed x181, local copies, waits for them, and re-layouts  11.4 us
  transfers between devices with their start and end apart: 73, of which 21 were waited for; matrix products, arithmetic and copies ran while one was open for 13% of the time, Pallas kernels for 32%

profile of v4, /device:TPU:0, one launch (start us, length us, event | category | flops | bytes accessed | tf_op | source)
XLA Modules:
  0.0 456.8 jit_solution(8122262702570122815)
XLA Ops:
  2.1 3.0 collective-permute-start
  5.9 5.8 %all-to-all-start = ((bf16[8,2,3,1024]{3,1,2,0:T(2,128)(2,1)}), bf16[8,2,3,1024]{3,1,2,0:T(2,128)(2,1)S(1)}, u32[]{:S(2)}, u32[]{:S(2)}) async-start(bf16[8,2,3,1024]{3,1,2,0:T(2,128)(2,1)} %broadcast_in_dim.130), calls=%async_computation | async-start | bytes 196608 | tf_op jit(solution)/shard_map/all_to_all | solution.py:774
  21.2 3.1 concatenate.167
  33.1 10.8 %collective-permute-done.1.refs_6_.refs_2_ = bf16[256,1024]{1,0:T(8,128)(2,1)S(1)} collective-permute-done((bf16[256,1024]{1,0:T(8,128)(2,1)S(1)}, bf16[256,1024]{1,0:T(8,128)(2,1)S(1)}, u32[]{:S(2)}, u32[]{:S(2)}) %collective-permute-start.1) | collective-permute-done | bytes 524320 | tf_op jit(solution)/shard_map/ppermute | solution.py:32
  49.4 13.3 %inputs.1 = (bf16[2,272,2048]{2,1,0:T(8,128)(2,1)S(1)}, f32[2,256,2048]{2,1,0:T(8,128)S(1)}, bf16[2,256,2048]{2,1,0:T(8,128)(2,1)S(1)}, f32[512,96]{1,0:T(8,128)S(1)}) custom-call(s32[3]{0:T(128)S(1)} %pad_add_fusion.3.scal, bf16[544,1024]{1,0:T(8,128)(2,1)S(1)} %fusion.1.normed_ref, bf16[256,1024]{1,0:T(8,128)(2,1)S(1)} %copy-done.11, ...), custom_call_target="tpu_custom_call" | custom-call | flops 2147483648 | bytes 14811136 | tf_op jit(solution)/shard_map/inputs/pallas_call | solution.py:655
  72.4 16.3 %end_states.1 = (f32[2,32,8,2048]{3,2,1,0:T(8,128)S(1)}, bf16[40,2048]{1,0:T(8,128)(2,1)S(1)}) custom-call(s32[3]{0:T(128)S(1)} %pad_add_fusion.3.scal, f32[512,96]{1,0:T(8,128)S(1)} %get-tuple-element.167.proj_ref.refs_13_.refs_15_, bf16[192,2048]{1,0:T(8,128)(2,1)S(1)} %constant_dynamic-update-slice_fusion.refs_8_.s_ref.refs_16_, ...), custom_call_target="tpu_custom_call" | custom-call | flops 83886080 | bytes 11632640 | tf_op jit(solution)/shard_map/end_states/pallas_call | solution.py:655
  93.3 6.8 %gates.1.refs_11_.gate_ref = f32[2,256,2048]{2,1,0:T(8,128)S(1)} custom-call(s32[3]{0:T(128)S(1)} %pad_add_fusion.3.scal, bf16[544,1024]{1,0:T(8,128)(2,1)S(1)} %fusion.1.normed_ref, bf16[256,2048]{1,0:T(8,128)(2,1)} %slice.287.refs_0_, bf16[256,2048]{1,0:T(8,128)(2,1)S(1)} %collective-permute-done.13.refs_1_, ...), custom_call_target="tpu_custom_call" | custom-call | flops 2147483648 | bytes 9502720 | tf_op jit(solution)/shard_map/gates/pallas_call | solution.py:655
  102.2 3.7 collective-permute-done.11.refs_3_.refs_10_
  115.2 3.4 pad_maximum_fusion.refs_14_.weight_ref
  119.1 3.5 collective-permute-done.18.refs_4_.refs_11_
  125.9 33.8 %forward_states.1 = (f32[2,256,2048]{2,1,0:T(8,128)}, bf16[2,256,2048]{2,1,0:T(8,128)(2,1)}, bf16[16,2,256,16,128]{4,3,2,1,0:T(8,128)(2,1)}, f32[2,16,2048]{2,1,...) custom-call(s32[3]{0:T(128)} %copy-done.23, ...), custom_call_target="tpu_custom_call" | custom-call | flops 167772160 | bytes 67452928 | tf_op jit(solution)/shard_map/forward_states/pallas_call | solution.py:655
  159.7 22.9 %first_grads.1 = (f32[2,32,8,2048]{3,2,1,0:T(8,128)}, bf16[2,256,2048]{2,1,0:T(8,128)(2,1)}, f32[1,2048]{1,0:T(1,128)}, bf16[32,2048]{1,0:T(8,128)(2,1)}) custom-call(s32[3]{0:T(128)} %copy-done.23, bf16[512,1024]{1,0:T(8,128)(2,1)} %get-tuple-element.193.dout_ref, bf16[2048,1024]{1,0:T(8,128)(2,1)} %pad_maximum_fusion.refs_14_.weight_ref, ...), custom_call_target="tpu_custom_call" | custom-call | flops 100663296 | bytes 31334400 | tf_op jit(solution)/shard_map/first_grads/pallas_call | solution.py:655
  187.5 12.0 %gate_grads.1 = (bf16[2,256,2048]{2,1,0:T(8,128)(2,1)}, bf16[2,256,2048]{2,1,0:T(8,128)(2,1)}, f32[544,1024]{1,0:T(8,128)}) custom-call(s32[3]{0:T(128)} %copy-done.23, bf16[544,1024]{1,0:T(8,128)(2,1)} %copy-done.1, bf16[2,256,2048]{2,1,0:T(8,128)(2,1)} %get-tuple-element.197.dgate_ref, bf16[256,2048]{1,0:T(8,128)(2,1)} %slice.287.refs_0_, ...), custom_call_target="tpu_custom_call" | custom-call | flops 4294967296 | bytes 13828096 | tf_op jit(solution)/shard_map/gate_grads/pallas_call | solution.py:655
  199.5 5.8 %out_grads.1 = (bf16[2,512,1024]{2,1,0:T(8,128)(2,1)}, bf16[2,512,1024]{2,1,0:T(8,128)(2,1)}) custom-call(bf16[512,2048]{1,0:T(8,128)(2,1)} %bitcast.125, bf16[512,2048]{1,0:T(8,128)(2,1)} %bitcast.126, bf16[512,1024]{1,0:T(8,128)(2,1)} %get-tuple-element.193.dout_ref), custom_call_target="tpu_custom_call" | custom-call | flops 2147483648 | bytes 9437184 | tf_op jit(solution)/shard_map/out_grads/pallas_call | solution.py:947
  225.1 54.8 %backward_states.1 = (f32[2,256,2048]{2,1,0:T(8,128)}, f32[88,2048]{1,0:T(8,128)}, f32[512,64]{1,0:T(8,128)}, f32[2,16,256]{2,1,0:T(8,128)}, f32[2,16,256]{2,1,0:T(8,128)}) custom-call(s32[3]{0:T(128)} %copy-done.23, bf16[32,2048]{1,0:T(8,128)(2,1)} %copy-done.60, bf16[32,2048]{1,0:T(8,128)(2,1)} %copy-done.57, bf16[32,2048]{1,0:T(8,128)(2,1)} %copy-done.61, ...), custom_call_target="tpu_custom_call" | custom-call | flops 268435456 | bytes 56672256 | tf_op jit(solution)/shard_map/backward_states/pallas_call | solution.py:655
  292.5 23.1 %tail_grads.2 = (f32[104,1024]{1,0:T(8,128)}, bf16[2,256,1024]{2,1,0:T(8,128)(2,1)}, bf16[2,256,1024]{2,1,0:T(8,128)(2,1)}, f32[544,1024]{1,0:T(8,128)}) custom-call(s32[3]{0:T(128)} %copy-done.23, bf16[512,96]{1,0:T(8,128)(2,1)} %pad_maximum_fusion.14.dproj_ref, bf16[192,2048]{1,0:T(8,128)(2,1)} %copy-done.4, f32[2,256,2048]{2,1,0:T(8,128)} %get-tuple-element.238.dxs_ref, ...), custom_call_target="tpu_custom_call" | custom-call | flops 2147483648 | bytes 23789568 | tf_op jit(solution)/shard_map/tail_grads/pallas_call | solution.py:655
  320.0 12.5 %tail_grads.3 = (f32[104,1024]{1,0:T(8,128)}, bf16[2,256,1024]{2,1,0:T(8,128)(2,1)}, bf16[2,256,1024]{2,1,0:T(8,128)(2,1)}, f32[544,1024]{1,0:T(8,128)}) custom-call(s32[3]{0:T(128)} %copy-done.23, bf16[512,96]{1,0:T(8,128)(2,1)} %pad_maximum_fusion.14.dproj_ref, bf16[192,2048]{1,0:T(8,128)(2,1)} %copy-done.4, f32[2,256,2048]{2,1,0:T(8,128)} %get-tuple-element.238.dxs_ref, ...), custom_call_target="tpu_custom_call" | custom-call | flops 2147483648 | bytes 23789568 | tf_op jit(solution)/shard_map/tail_grads/pallas_call | solution.py:655
  339.3 9.1 %collective-permute-done.41 = bf16[2,128,1024]{2,1,0:T(8,128)(2,1)S(1)} collective-permute-done((bf16[2,128,1024]{2,1,0:T(8,128)(2,1)S(1)}, bf16[2,128,1024]{2,1,0:T(8,128)(2,1)S(1)}, u32[]{:S(2)}, u32[]{:S(2)}) %collective-permute-start.41) | collective-permute-done | bytes 524320 | tf_op jit(solution)/shard_map/ppermute | solution.py:32
  350.9 6.2 %collective-permute-done.46 = bf16[2,64,1024]{2,1,0:T(8,128)(2,1)S(1)} collective-permute-done((bf16[2,64,1024]{2,1,0:T(8,128)(2,1)S(1)}, bf16[2,64,1024]{2,1,0:T(8,128)(2,1)S(1)}, u32[]{:S(2)}, u32[]{:S(2)}) %collective-permute-start.46) | collective-permute-done | bytes 262176 | tf_op jit(solution)/shard_map/ppermute | solution.py:32
  357.1 5.0 %collective-permute-done.43 = bf16[1,256,1024]{2,1,0:T(8,128)(2,1)S(1)} collective-permute-done((bf16[1,256,1024]{2,1,0:T(8,128)(2,1)S(1)}, bf16[1,256,1024]{2,1,0:T(8,128)(2,1)S(1)}, u32[]{:S(2)}, u32[]{:S(2)}) %collective-permute-start.43) | collective-permute-done | bytes 524320 | tf_op jit(solution)/shard_map/ppermute | solution.py:32
  368.1 6.6 %collective-permute-done.51 = bf16[1,64,1024]{2,1,0:T(8,128)(2,1)S(1)} collective-permute-done((bf16[1,64,1024]{2,1,0:T(8,128)(2,1)S(1)}, bf16[1,64,1024]{2,1,0:T(8,128)(2,1)S(1)}, u32[]{:S(2)}, u32[]{:S(2)}) %collective-permute-start.51) | collective-permute-done | bytes 131104 | tf_op jit(solution)/shard_map/ppermute | solution.py:32
  391.2 3.8 collective-permute-done.55
  409.6 7.6 %collective-permute-done.63 = bf16[2,8,1024]{2,1,0:T(8,128)(2,1)S(1)} collective-permute-done((bf16[2,8,1024]{2,1,0:T(8,128)(2,1)}, bf16[2,8,1024]{2,1,0:T(8,128)(2,1)S(1)}, u32[]{:S(2)}, u32[]{:S(2)}) %collective-permute-start.63) | collective-permute-done | bytes 32800 | tf_op jit(solution)/shard_map/ppermute | solution.py:32
  441.3 5.8 %collective-permute-done.70 = bf16[1,192,1024]{2,1,0:T(8,128)(2,1)S(1)} collective-permute-done((bf16[1,192,1024]{2,1,0:T(8,128)(2,1)S(1)}, bf16[1,192,1024]{2,1,0:T(8,128)(2,1)S(1)}, u32[]{:S(2)}, u32[]{:S(2)}) %collective-permute-start.70) | collective-permute-done | bytes 393248 | tf_op jit(solution)/shard_map/ppermute | solution.py:32
  (503 shorter events, 165.4 us)
Async XLA Ops:
  2.1 23.4 %collective-permute-start = (bf16[256,1024]{1,0:T(8,128)(2,1)S(1)}, bf16[256,1024]{1,0:T(8,128)(2,1)S(1)}, u32[]{:S(2)}, u32[]{:S(2)}) collective-permute-start(bf16[256,1024]{1,0:T(8,128)(2,1)S(1)} %get-tuple-element.164.refs_0_), channel_id=1, source_target_pairs={{0,2},{1,3},{2,0},{3,1},{4,6},{5,7},{6,4},{7,5},{8,10},{9,11},{10,... | collective-permute-start | bytes 1572872 | tf_op jit(solution)/shard_map/ppermute | solution.py:32
  5.9 19.5 %all-to-all-start = ((bf16[8,2,3,1024]{3,1,2,0:T(2,128)(2,1)}), bf16[8,2,3,1024]{3,1,2,0:T(2,128)(2,1)S(1)}, u32[]{:S(2)}, u32[]{:S(2)}) async-start(bf16[8,2,3,1024]{3,1,2,0:T(2,128)(2,1)} %broadcast_in_dim.130), calls=%async_computation | async-start | bytes 196608 | tf_op jit(solution)/shard_map/all_to_all | solution.py:774
  31.1 16.8 %collective-permute-start.8 = (bf16[256,1024]{1,0:T(8,128)(2,1)S(1)}, bf16[256,1024]{1,0:T(8,128)(2,1)}, u32[]{:S(2)}, u32[]{:S(2)}) collective-permute-start(bf16[256,1024]{1,0:T(8,128)(2,1)S(1)} %get-tuple-element.159.refs_4_.refs_0_), channel_id=1, source_target_pairs={{0,1},{1,0},{2,3},{3,2},{4,5},{5,4},{6,7},{7,6},{8,9},{9,8},{10,11... | collective-permute-start | bytes 1572872 | tf_op jit(solution)/shard_map/ppermute | solution.py:32
  32.0 15.9 %collective-permute-start.6 = (bf16[256,1024]{1,0:T(8,128)(2,1)S(1)}, bf16[256,1024]{1,0:T(8,128)(2,1)S(1)}, u32[]{:S(2)}, u32[]{:S(2)}) collective-permute-start(bf16[256,1024]{1,0:T(8,128)(2,1)S(1)} %get-tuple-element.164.refs_0_), channel_id=1, source_target_pairs={{0,1},{1,0},{2,3},{3,2},{4,5},{5,4},{6,7},{7,6},{8,9},{9,8},{10,11... | collective-permute-start | bytes 1572872 | tf_op jit(solution)/shard_map/ppermute | solution.py:32
  32.3 15.5 %collective-permute-start.7 = (bf16[256,1024]{1,0:T(8,128)(2,1)S(1)}, bf16[256,1024]{1,0:T(8,128)(2,1)S(1)}, u32[]{:S(2)}, u32[]{:S(2)}) collective-permute-start(bf16[256,1024]{1,0:T(8,128)(2,1)S(1)} %collective-permute-done.refs_2_), channel_id=1, source_target_pairs={{0,1},{1,0},{2,3},{3,2},{4,5},{5,4},{6,7},{7,6},{8,9},{9,8},{10,11... | collective-permute-start | bytes 1572872 | tf_op jit(solution)/shard_map/ppermute | solution.py:32
  43.9 25.0 %collective-permute-start.2 = (bf16[256,2048]{1,0:T(8,128)(2,1)}, bf16[256,2048]{1,0:T(8,128)(2,1)S(1)}, u32[]{:S(2)}, u32[]{:S(2)}) collective-permute-start(bf16[256,2048]{1,0:T(8,128)(2,1)} %slice.287.refs_0_), channel_id=1, source_target_pairs={{0,2},{1,3},{2,0},{3,1},{4,6},{5,7},{6,4},{7,5},{8,10},{9,11},{10,... | collective-permute-start | bytes 3145736 | tf_op jit(solution)/shard_map/ppermute | solution.py:32
  68.9 24.2 %collective-permute-start.13 = (bf16[256,2048]{1,0:T(8,128)(2,1)}, bf16[256,2048]{1,0:T(8,128)(2,1)S(1)}, u32[]{:S(2)}, u32[]{:S(2)}) collective-permute-start(bf16[256,2048]{1,0:T(8,128)(2,1)} %slice.287.refs_0_), channel_id=1, source_target_pairs={{0,1},{1,0},{2,3},{3,2},{4,5},{5,4},{6,7},{7,6},{8,9},{9,8},{10,11... | collective-permute-start | bytes 3145736 | tf_op jit(solution)/shard_map/ppermute | solution.py:32
  68.9 24.3 %collective-permute-start.14 = (bf16[256,2048]{1,0:T(8,128)(2,1)S(1)}, bf16[256,2048]{1,0:T(8,128)(2,1)S(1)}, u32[]{:S(2)}, u32[]{:S(2)}) collective-permute-start(bf16[256,2048]{1,0:T(8,128)(2,1)S(1)} %collective-permute-done.2.refs_2_), channel_id=1, source_target_pairs={{0,1},{1,0},{2,3},{3,2},{4,5},{5,4},{6,7},{7,6},{8,9},{9,8},{10,11... | collective-permute-start | bytes 3145736 | tf_op jit(solution)/shard_map/ppermute | solution.py:32
  69.4 36.4 %collective-permute-start.15 = (bf16[512,1024]{1,0:T(8,128)(2,1)S(1)}, bf16[512,1024]{1,0:T(8,128)(2,1)}, u32[]{:S(2)}, u32[]{:S(2)}) collective-permute-start(bf16[512,1024]{1,0:T(8,128)(2,1)S(1)} %copy-done.39), channel_id=1, source_target_pairs={{0,2},{1,3},{2,0},{3,1},{4,6},{5,7},{6,4},{7,5},{8,10},{9,11},{10,... | collective-permute-start | bytes 3145736 | tf_op jit(solution)/shard_map/ppermute | solution.py:32
  182.6 22.7 %collective-permute-start.22 = (bf16[32,2048]{1,0:T(8,128)(2,1)}, bf16[32,2048]{1,0:T(8,128)(2,1)S(1)}, u32[]{:S(2)}, u32[]{:S(2)}) collective-permute-start(bf16[32,2048]{1,0:T(8,128)(2,1)} %get-tuple-element.203), channel_id=1, source_target_pairs={{0,8},{4,12},{8,0},{12,4},{16,24},{20,28},{24,16},{28,20},{1,9},{5... | collective-permute-start | bytes 393224 | tf_op jit(solution)/shard_map/ppermute | solution.py:32
  185.1 20.2 %collective-permute-start.23 = (bf16[32,2048]{1,0:T(8,128)(2,1)}, bf16[32,2048]{1,0:T(8,128)(2,1)S(1)}, u32[]{:S(2)}, u32[]{:S(2)}) collective-permute-start(bf16[32,2048]{1,0:T(8,128)(2,1)} %get-tuple-element.203), channel_id=1, source_target_pairs={{0,16},{4,20},{8,24},{12,28},{16,0},{20,4},{24,8},{28,12},{1,17},{... | collective-permute-start | bytes 393224 | tf_op jit(solution)/shard_map/ppermute | solution.py:32
  186.1 19.3 %collective-permute-start.24 = (bf16[32,2048]{1,0:T(8,128)(2,1)}, bf16[32,2048]{1,0:T(8,128)(2,1)S(1)}, u32[]{:S(2)}, u32[]{:S(2)}) collective-permute-start(bf16[32,2048]{1,0:T(8,128)(2,1)} %get-tuple-element.203), channel_id=1, source_target_pairs={{0,24},{4,28},{8,16},{12,20},{16,8},{20,12},{24,0},{28,4},{1,25},{... | collective-permute-start | bytes 393224 | tf_op jit(solution)/shard_map/ppermute | solution.py:32
  221.7 58.2 %collective-permute-start.31 = (bf16[1,512,1024]{2,1,0:T(8,128)(2,1)}, bf16[1,512,1024]{2,1,0:T(8,128)(2,1)}, u32[]{:S(2)}, u32[]{:S(2)}) collective-permute-start(bf16[1,512,1024]{2,1,0:T(8,128)(2,1)} %slice.303), channel_id=1, source_target_pairs={{0,2},{1,3},{2,0},{3,1},{4,6},{5,7},{6,4},{7,5},{8,10},{9,11},{10,... | collective-permute-start | bytes 3145736 | tf_op jit(solution)/shard_map/ppermute | solution.py:32
  223.3 56.6 %collective-permute-start.32 = (bf16[2,128,2048]{2,1,0:T(8,128)(2,1)}, bf16[2,128,2048]{2,1,0:T(8,128)(2,1)S(1)}, u32[]{:S(2)}, u32[]{:S(2)}) collective-permute-start(bf16[2,128,2048]{2,1,0:T(8,128)(2,1)} %broadcast_select_fusion), channel_id=1, source_target_pairs={{0,8},{4,12},{8,0},{12,4},{16,24},{20,28},{24,16},{28,20},{1,9},{5... | collective-permute-start | bytes 3145736 | tf_op jit(solution)/shard_map/ppermute | solution.py:32
  283.4 32.3 %collective-permute-start.33 = (bf16[1,256,1024]{2,1,0:T(8,128)(2,1)}, bf16[1,256,1024]{2,1,0:T(8,128)(2,1)}, u32[]{:S(2)}, u32[]{:S(2)}) collective-permute-start(bf16[1,256,1024]{2,1,0:T(8,128)(2,1)} %broadcast_select_fusion.7), channel_id=1, source_target_pairs={{0,4},{4,0},{8,12},{12,8},{16,20},{20,16},{24,28},{28,24},{1,5},{5... | collective-permute-start | bytes 1572872 | tf_op jit(solution)/shard_map/ppermute | solution.py:32
  287.0 28.7 %collective-permute-start.34 = (bf16[2,64,2048]{2,1,0:T(8,128)(2,1)}, bf16[2,64,2048]{2,1,0:T(8,128)(2,1)S(1)}, u32[]{:S(2)}, u32[]{:S(2)}) collective-permute-start(bf16[2,64,2048]{2,1,0:T(8,128)(2,1)} %broadcast_select_fusion.4), channel_id=1, source_target_pairs={{0,16},{4,20},{8,24},{12,28},{16,0},{20,4},{24,8},{28,12},{1,17},{... | collective-permute-start | bytes 1572872 | tf_op jit(solution)/shard_map/ppermute | solution.py:32
  290.4 25.3 %collective-permute-start.38 = (bf16[96,512]{1,0:T(8,128)(2,1)S(1)}, bf16[96,512]{1,0:T(8,128)(2,1)S(1)}, u32[]{:S(2)}, u32[]{:S(2)}) collective-permute-start(bf16[96,512]{1,0:T(8,128)(2,1)S(1)} %get-tuple-element.336), channel_id=1, source_target_pairs={{0,1},{1,0},{2,3},{3,2},{4,5},{5,4},{6,7},{7,6},{8,9},{9,8},{10,11... | collective-permute-start | bytes 294920 | tf_op jit(solution)/shard_map/ppermute | solution.py:32
  290.9 24.8 %collective-permute-start.40 = (bf16[96,512]{1,0:T(8,128)(2,1)S(1)}, bf16[96,512]{1,0:T(8,128)(2,1)S(1)}, u32[]{:S(2)}, u32[]{:S(2)}) collective-permute-start(bf16[96,512]{1,0:T(8,128)(2,1)S(1)} %add_convert_fusion.23), channel_id=1, source_target_pairs={{0,2},{1,3},{2,0},{3,1},{4,6},{5,7},{6,4},{7,5},{8,10},{9,11},{10,... | collective-permute-start | bytes 294920 | tf_op jit(solution)/shard_map/ppermute | solution.py:32
  317.1 15.4 %collective-permute-start.35 = (bf16[1,128,1024]{2,1,0:T(8,128)(2,1)S(1)}, bf16[1,128,1024]{2,1,0:T(8,128)(2,1)S(1)}, u32[]{:S(2)}, u32[]{:S(2)}) collective-permute-start(bf16[1,128,1024]{2,1,0:T(8,128)(2,1)S(1)} %broadcast_select_fusion.19), channel_id=1, source_target_pairs={{0,8},{4,12},{8,0},{12,4},{16,24},{20,28},{24,16},{28,20},{1,9},{5... | collective-permute-start | bytes 786440 | tf_op jit(solution)/shard_map/ppermute | solution.py:32
  319.7 17.4 %collective-permute-start.48 = (bf16[104,512]{1,0:T(8,128)(2,1)S(1)}, bf16[104,512]{1,0:T(8,128)(2,1)S(1)}, u32[]{:S(2)}, u32[]{:S(2)}) collective-permute-start(bf16[104,512]{1,0:T(8,128)(2,1)S(1)} %broadcast_select_fusion.31), channel_id=1, source_target_pairs={{0,1},{1,0},{2,3},{3,2},{4,5},{5,4},{6,7},{7,6},{8,9},{9,8},{10,11... | collective-permute-start | bytes 319496 | tf_op jit(solution)/shard_map/ppermute | solution.py:32
  335.6 15.3 %collective-permute-start.44 = (bf16[1,64,1024]{2,1,0:T(8,128)(2,1)S(1)}, bf16[1,64,1024]{2,1,0:T(8,128)(2,1)S(1)}, u32[]{:S(2)}, u32[]{:S(2)}) collective-permute-start(bf16[1,64,1024]{2,1,0:T(8,128)(2,1)S(1)} %broadcast_select_fusion.30), channel_id=1, source_target_pairs={{0,16},{4,20},{8,24},{12,28},{16,0},{20,4},{24,8},{28,12},{1,17},{... | collective-permute-start | bytes 393224 | tf_op jit(solution)/shard_map/ppermute | solution.py:32
  377.6 17.5 %collective-permute-start.55 = (bf16[1,128,1024]{2,1,0:T(8,128)(2,1)S(1)}, bf16[1,128,1024]{2,1,0:T(8,128)(2,1)}, u32[]{:S(2)}, u32[]{:S(2)}) collective-permute-start(bf16[1,128,1024]{2,1,0:T(8,128)(2,1)S(1)} %pad_maximum_fusion.7), channel_id=1, source_target_pairs={{0,8},{4,12},{8,0},{12,4},{16,24},{20,28},{24,16},{28,20},{1,9},{5... | collective-permute-start | bytes 786440 | tf_op jit(solution)/shard_map/ppermute | solution.py:32
  396.7 20.5 %collective-permute-start.59 = (bf16[1,48,1024]{2,1,0:T(8,128)(2,1)}, bf16[1,48,1024]{2,1,0:T(8,128)(2,1)}, u32[]{:S(2)}, u32[]{:S(2)}) collective-permute-start(bf16[1,48,1024]{2,1,0:T(8,128)(2,1)} %broadcast_select_fusion.36), channel_id=1, source_target_pairs={{0,16},{4,20},{8,24},{12,28},{16,0},{20,4},{24,8},{28,12},{1,17},{... | collective-permute-start | bytes 294920 | tf_op jit(solution)/shard_map/ppermute | solution.py:32
  399.8 17.4 %collective-permute-start.60 = (bf16[1,256,1024]{2,1,0:T(8,128)(2,1)}, bf16[1,256,1024]{2,1,0:T(8,128)(2,1)}, u32[]{:S(2)}, u32[]{:S(2)}) collective-permute-start(bf16[1,256,1024]{2,1,0:T(8,128)(2,1)} %pad_maximum_fusion.3), channel_id=1, source_target_pairs={{0,4},{4,0},{8,12},{12,8},{16,20},{20,16},{24,28},{28,24},{1,5},{5... | collective-permute-start | bytes 1572872 | tf_op jit(solution)/shard_map/ppermute | solution.py:32
  (135 other events, 1294.0 us)

commit v5 on v4

--- a/solution.py
+++ b/solution.py
@@ -88,22 +88,37 @@
     return (kept.astype(F32) + received.astype(F32)).astype(BF16)
 
 
-def halves_of(values, bit):
-    half = values.shape[1] // 2
-    up = (lax.axis_index("ctx") & bit) != 0
-    return values[:, :half], values[:, half:], up
+def part_of(values, take):
+    if isinstance(values, tuple):
+        return joined(take(values[0]), take(values[1]))
+    return take(values)
+
+
+def pending(own, other):
+    return own, other
 
 
 def fsdp_step(bit):
-    return lambda values: (values[0::2], swap(values[1::2], "fsdp", bit), joined)
+    def ready(values):
+        return part_of(values, lambda v: v[0::2]), part_of(values, lambda v: v[1::2])
+
+    return ready, "fsdp", bit, pending
 
 
 def scatter_step(bit):
-    def run(values):
-        low, high, up = halves_of(values, bit)
-        return jnp.where(up, high, low), swap(jnp.where(up, low, high), "ctx", bit), joined
-
-    return run
+    def ready(values):
+        up = (lax.axis_index("ctx") & bit) != 0
+
+        def low(v):
+            return v[:, : v.shape[1] // 2]
+
+        def high(v):
+            return v[:, v.shape[1] // 2 :]
+
+        keep = jnp.where(up, part_of(values, high), part_of(values, low))
+        return keep, jnp.where(up, part_of(values, low), part_of(values, high))
+
+    return ready, "ctx", bit, pending
 
 
 def spread_step(bit):
@@ -111,17 +126,23 @@
         up = (lax.axis_index("ctx") & bit) != 0
         return jnp.concatenate([jnp.where(up, other, own), jnp.where(up, own, other)], axis=1)
 
-    return lambda values: (values, swap(values, "ctx", bit), finish)
+    def ready(values):
+        values = part_of(values, lambda v: v)
+        return values, values
+
+    return ready, "ctx", bit, finish
+
+
+def same_twice(values):
+    return values, values
 
 
 def gather_step(bit):
-    return lambda values: (
-        values, swap(values, "ctx", bit), lambda own, other: jnp.concatenate([own, other], axis=0)
-    )
+    return same_twice, "ctx", bit, lambda own, other: jnp.concatenate([own, other], axis=0)
 
 
 def sum_step(bit):
-    return lambda values: (values, swap(values, "fsdp", bit), lambda own, other: own + other)
+    return same_twice, "fsdp", bit, lambda own, other: own + other
 
 
 def reduce_steps(ctx_first, turn=0):
@@ -134,14 +155,22 @@
 
 
 def advance(chains, beside=()):
-    begun = [(steps.pop(0)(values) if steps else None, steps, values) for steps, values in chains]
-    received = [step[1] for step, _, _ in begun if step]
-    received, beside = together(received, beside)
+    begun = []
+    for steps, values in chains:
+        if steps:
+            ready, axis, bit, finish = steps.pop(0)
+            keep, send = ready(values)
+            values = (keep, swap(send, axis, bit), finish)
+            begun.append((steps, values))
+        else:
+            begun.append((None, values))
+    received, beside = together([values[1] for steps, values in begun if steps is not None], beside)
     after = []
-    for step, steps, values in begun:
-        if step:
-            values = step[2](step[0], received.pop(0))
-        after.append((steps, values))
+    for steps, values in begun:
+        if steps is None:
+            after.append(([], values))
+        else:
+            after.append((steps, values[2](values[0], received.pop(0))))
     return after, beside
 
 
@@ -964,10 +993,14 @@
         back_far, keep_gate, send_gate, keep_out, send_out
     )
     back_near, _ = gather_near(back_far)
-    core_gate = joined(keep_gate, swap(send_gate, "fsdp", 1))
-    core_out = joined(keep_out, swap(send_out, "fsdp", 1))
-    back_near, core_out, core_gate = together(back_near, core_out, core_gate)
-    chains = [(reduce_steps(False), core_out), (reduce_steps(True, 1), core_gate)]
+    core_gate = (keep_gate, swap(send_gate, "fsdp", 1))
+    core_out = (keep_out, swap(send_out, "fsdp", 1))
+    out_steps, gate_steps = reduce_steps(False), reduce_steps(True, 1)
+    out_ready, gate_ready = out_steps[0][0](core_out), gate_steps[0][0](core_gate)
+    back_near, out_ready, gate_ready = together(back_near, out_ready, gate_ready)
+    out_steps[0] = (lambda values: values, *out_steps[0][1:])
+    gate_steps[0] = (lambda values: values, *gate_steps[0][1:])
+    chains = [(out_steps, out_ready), (gate_steps, gate_ready)]
 
     def backward():
         def at(i):
@@ -1060,7 +1093,7 @@
     chains, (tail_second, got_ahead, small_now) = advance(
         chains, (tail(1, d_proj, tail_first[3]), got_ahead, small_now)
     )
-    ahead = joined(tail_first[1], got_ahead)
+    ahead = (tail_first[1], got_ahead)
     def halo_start(d_ext, squares):
         d_normed = d_ext.reshape(2, ext, features)
         unit = rows_ext * inv_rms
@@ -1090,7 +1123,7 @@
     lead = [(reduce_steps(True), ahead)]
     lead, (got_last, d_ext, squares) = advance(lead, (got_last, tail_second[3], squares))
     chains = chains + lead
-    last = joined(tail_second[1], got_last)
+    last = (tail_second[1], got_last)
     last_steps = reduce_steps(False)
     n_fsdp = len(bits_of(fsdp)) - 1
     for bit in bits_of(fsdp):
@@ -1118,7 +1151,7 @@
                 ],
                 axis=0,
             ).reshape(1, -1, half)
-            last = jnp.concatenate([last, extra], axis=1)
+            last = jnp.concatenate([part_of(last, lambda v: v), extra], axis=1)
         if n_fsdp == -1:
             last, d_ext, squares = together(last, d_ext, squares)
             for_halo, halo_got = halo_start(d_ext, squares), None

time: 465 us -> 460 us (0.989)
    convert_element_type x23 -> x12, other arithmetic: 18 us -> 6.82 us  [joined(): return (kept.astype(F32) + received.astype(F32)).astype(BF16)]
    select_n x12, other arithmetic: 4.61 us -> 11.9 us  [the longest x8 7.6 us: ready(): keep = jnp.where(up, part_of(values, high), part_of(values, low))]
    unnamed x181 -> x173, local copies, waits for them, and re-layouts: 11.4 us -> 10.9 us
  transfers between devices with their start and end apart: 73 -> 73, of which waited for: 21 -> 20; matrix products, arithmetic and copies ran while one was open for 13% -> 13% of each run, Pallas kernels for 32% -> 32%
where the time goes in v5:
time: 460 us; the launch traced here: 453 us
  Pallas kernels  201 us (44%)
  waiting for transfers between devices  80.1 us (17%)
  starting transfers between devices  72.8 us (16%)
  other arithmetic  58.8 us (13%)
  local copies, waits for them, and re-layouts  28.3 us (6%)
  between operations  12.4 us (3%)
    pallas_call x9, Pallas kernels, call(): pl.pallas_call(kernel, grid_spec=pltpu.PrefetchScalarGridSpec(num_scalar_...  195 us
    ppermute x72, waiting for transfers between devices, swap(): return lax.ppermute(values, axis, [(i, i ^ bit) for i in range(size)])  80.1 us
    ppermute x72, starting transfers between devices, swap(): return lax.ppermute(values, axis, [(i, i ^ bit) for i in range(size)])  67 us
    unnamed x173, local copies, waits for them, and re-layouts  10.9 us
  transfers between devices with their start and end apart: 73, of which 20 were waited for; matrix products, arithmetic and copies ran while one was open for 13% of the time, Pallas kernels for 32%

profile of v5, /device:TPU:0, one launch (start us, length us, event | category | flops | bytes accessed | tf_op | source)
XLA Modules:
  0.0 453.1 jit_solution(596148543541001025)
XLA Ops:
  5.9 5.8 %all-to-all-start = ((bf16[8,2,3,1024]{3,1,2,0:T(2,128)(2,1)}), bf16[8,2,3,1024]{3,1,2,0:T(2,128)(2,1)S(1)}, u32[]{:S(2)}, u32[]{:S(2)}) async-start(bf16[8,2,3,1024]{3,1,2,0:T(2,128)(2,1)} %broadcast_in_dim.130), calls=%async_computation | async-start | bytes 196608 | tf_op jit(solution)/shard_map/all_to_all | solution.py:803
  33.0 10.8 %collective-permute-done.1.refs_6_.refs_2_ = bf16[256,1024]{1,0:T(8,128)(2,1)S(1)} collective-permute-done((bf16[256,1024]{1,0:T(8,128)(2,1)S(1)}, bf16[256,1024]{1,0:T(8,128)(2,1)S(1)}, u32[]{:S(2)}, u32[]{:S(2)}) %collective-permute-start.1) | collective-permute-done | bytes 524320 | tf_op jit(solution)/shard_map/ppermute | solution.py:32
  49.4 13.3 %inputs.1 = (bf16[2,272,2048]{2,1,0:T(8,128)(2,1)S(1)}, f32[2,256,2048]{2,1,0:T(8,128)S(1)}, bf16[2,256,2048]{2,1,0:T(8,128)(2,1)S(1)}, f32[512,96]{1,0:T(8,128)S(1)}) custom-call(s32[3]{0:T(128)S(1)} %pad_add_fusion.3.scal, bf16[544,1024]{1,0:T(8,128)(2,1)S(1)} %fusion.1.normed_ref, bf16[256,1024]{1,0:T(8,128)(2,1)S(1)} %copy-done.11, ...), custom_call_target="tpu_custom_call" | custom-call | flops 2147483648 | bytes 14811136 | tf_op jit(solution)/shard_map/inputs/pallas_call | solution.py:684
  72.4 16.3 %end_states.1 = (f32[2,32,8,2048]{3,2,1,0:T(8,128)S(1)}, bf16[40,2048]{1,0:T(8,128)(2,1)S(1)}) custom-call(s32[3]{0:T(128)S(1)} %pad_add_fusion.3.scal, f32[512,96]{1,0:T(8,128)S(1)} %get-tuple-element.170.proj_ref.refs_13_.refs_15_, bf16[192,2048]{1,0:T(8,128)(2,1)S(1)} %constant_dynamic-update-slice_fusion.refs_8_.s_ref.refs_16_, ...), custom_call_target="tpu_custom_call" | custom-call | flops 83886080 | bytes 11632640 | tf_op jit(solution)/shard_map/end_states/pallas_call | solution.py:684
  93.2 6.8 %gates.1.refs_11_.gate_ref = f32[2,256,2048]{2,1,0:T(8,128)S(1)} custom-call(s32[3]{0:T(128)S(1)} %pad_add_fusion.3.scal, bf16[544,1024]{1,0:T(8,128)(2,1)S(1)} %fusion.1.normed_ref, bf16[256,2048]{1,0:T(8,128)(2,1)} %slice.431.refs_0_, bf16[256,2048]{1,0:T(8,128)(2,1)S(1)} %collective-permute-done.13.refs_1_, ...), custom_call_target="tpu_custom_call" | custom-call | flops 2147483648 | bytes 9502720 | tf_op jit(solution)/shard_map/gates/pallas_call | solution.py:684
  102.2 3.6 collective-permute-done.11.refs_3_.refs_10_
  115.2 3.4 pad_maximum_fusion.refs_14_.weight_ref
  119.1 3.5 collective-permute-done.18.refs_4_.refs_11_
  125.9 33.8 %forward_states.1 = (f32[2,256,2048]{2,1,0:T(8,128)}, bf16[2,256,2048]{2,1,0:T(8,128)(2,1)}, bf16[16,2,256,16,128]{4,3,2,1,0:T(8,128)(2,1)}, f32[2,16,2048]{2,1,...) custom-call(s32[3]{0:T(128)} %copy-done.23, ...), custom_call_target="tpu_custom_call" | custom-call | flops 167772160 | bytes 67452928 | tf_op jit(solution)/shard_map/forward_states/pallas_call | solution.py:684
  159.7 22.8 %first_grads.1 = (f32[2,32,8,2048]{3,2,1,0:T(8,128)}, bf16[2,256,2048]{2,1,0:T(8,128)(2,1)}, f32[1,2048]{1,0:T(1,128)}, bf16[32,2048]{1,0:T(8,128)(2,1)}) custom-call(s32[3]{0:T(128)} %copy-done.23, bf16[512,1024]{1,0:T(8,128)(2,1)} %get-tuple-element.196.dout_ref, bf16[2048,1024]{1,0:T(8,128)(2,1)} %pad_maximum_fusion.refs_14_.weight_ref, ...), custom_call_target="tpu_custom_call" | custom-call | flops 100663296 | bytes 31334400 | tf_op jit(solution)/shard_map/first_grads/pallas_call | solution.py:684
  187.5 12.0 %gate_grads.1 = (bf16[2,256,2048]{2,1,0:T(8,128)(2,1)}, bf16[2,256,2048]{2,1,0:T(8,128)(2,1)}, f32[544,1024]{1,0:T(8,128)}) custom-call(s32[3]{0:T(128)} %copy-done.23, bf16[544,1024]{1,0:T(8,128)(2,1)} %copy-done.1, bf16[2,256,2048]{2,1,0:T(8,128)(2,1)} %get-tuple-element.200.dgate_ref, bf16[256,2048]{1,0:T(8,128)(2,1)} %slice.431.refs_0_, ...), custom_call_target="tpu_custom_call" | custom-call | flops 4294967296 | bytes 13828096 | tf_op jit(solution)/shard_map/gate_grads/pallas_call | solution.py:684
  199.5 5.9 %out_grads.1 = (bf16[2,512,1024]{2,1,0:T(8,128)(2,1)}, bf16[2,512,1024]{2,1,0:T(8,128)(2,1)}) custom-call(bf16[512,2048]{1,0:T(8,128)(2,1)} %bitcast.125, bf16[512,2048]{1,0:T(8,128)(2,1)} %bitcast.126, bf16[512,1024]{1,0:T(8,128)(2,1)} %get-tuple-element.196.dout_ref), custom_call_target="tpu_custom_call" | custom-call | flops 2147483648 | bytes 9437184 | tf_op jit(solution)/shard_map/out_grads/pallas_call | solution.py:976
  211.4 3.3 broadcast_select_fusion
  214.8 3.5 add_convert_fusion.2
  222.7 54.8 %backward_states.1 = (f32[2,256,2048]{2,1,0:T(8,128)}, f32[88,2048]{1,0:T(8,128)}, f32[512,64]{1,0:T(8,128)}, f32[2,16,256]{2,1,0:T(8,128)}, f32[2,16,256]{2,1,0:T(8,128)}) custom-call(s32[3]{0:T(128)} %copy-done.23, bf16[32,2048]{1,0:T(8,128)(2,1)} %copy-done.59, bf16[32,2048]{1,0:T(8,128)(2,1)} %copy-done.56, bf16[32,2048]{1,0:T(8,128)(2,1)} %copy-done.60, ...), custom_call_target="tpu_custom_call" | custom-call | flops 268435456 | bytes 56672256 | tf_op jit(solution)/shard_map/backward_states/pallas_call | solution.py:684
  290.0 22.5 %tail_grads.2 = (f32[104,1024]{1,0:T(8,128)}, bf16[2,256,1024]{2,1,0:T(8,128)(2,1)}, bf16[2,256,1024]{2,1,0:T(8,128)(2,1)}, f32[544,1024]{1,0:T(8,128)}) custom-call(s32[3]{0:T(128)} %copy-done.23, bf16[512,96]{1,0:T(8,128)(2,1)} %pad_maximum_fusion.14.dproj_ref, bf16[192,2048]{1,0:T(8,128)(2,1)} %copy-done.4, f32[2,256,2048]{2,1,0:T(8,128)} %get-tuple-element.243.dxs_ref, ...), custom_call_target="tpu_custom_call" | custom-call | flops 2147483648 | bytes 23789568 | tf_op jit(solution)/shard_map/tail_grads/pallas_call | solution.py:684
  315.6 12.5 %tail_grads.3 = (f32[104,1024]{1,0:T(8,128)}, bf16[2,256,1024]{2,1,0:T(8,128)(2,1)}, bf16[2,256,1024]{2,1,0:T(8,128)(2,1)}, f32[544,1024]{1,0:T(8,128)}) custom-call(s32[3]{0:T(128)} %copy-done.23, bf16[512,96]{1,0:T(8,128)(2,1)} %pad_maximum_fusion.14.dproj_ref, bf16[192,2048]{1,0:T(8,128)(2,1)} %copy-done.4, f32[2,256,2048]{2,1,0:T(8,128)} %get-tuple-element.243.dxs_ref, ...), custom_call_target="tpu_custom_call" | custom-call | flops 2147483648 | bytes 23789568 | tf_op jit(solution)/shard_map/tail_grads/pallas_call | solution.py:684
  335.2 9.0 %collective-permute-done.41 = bf16[2,128,1024]{2,1,0:T(8,128)(2,1)S(1)} collective-permute-done((bf16[2,128,1024]{2,1,0:T(8,128)(2,1)S(1)}, bf16[2,128,1024]{2,1,0:T(8,128)(2,1)S(1)}, u32[]{:S(2)}, u32[]{:S(2)}) %collective-permute-start.41) | collective-permute-done | bytes 524320 | tf_op jit(solution)/shard_map/ppermute | solution.py:32
  346.4 6.4 %collective-permute-done.46 = bf16[2,64,1024]{2,1,0:T(8,128)(2,1)S(1)} collective-permute-done((bf16[2,64,1024]{2,1,0:T(8,128)(2,1)S(1)}, bf16[2,64,1024]{2,1,0:T(8,128)(2,1)S(1)}, u32[]{:S(2)}, u32[]{:S(2)}) %collective-permute-start.46) | collective-permute-done | bytes 262176 | tf_op jit(solution)/shard_map/ppermute | solution.py:32
  352.8 5.1 %collective-permute-done.43 = bf16[1,256,1024]{2,1,0:T(8,128)(2,1)S(1)} collective-permute-done((bf16[1,256,1024]{2,1,0:T(8,128)(2,1)S(1)}, bf16[1,256,1024]{2,1,0:T(8,128)(2,1)S(1)}, u32[]{:S(2)}, u32[]{:S(2)}) %collective-permute-start.43) | collective-permute-done | bytes 524320 | tf_op jit(solution)/shard_map/ppermute | solution.py:32
  364.0 7.0 %collective-permute-done.51 = bf16[1,64,1024]{2,1,0:T(8,128)(2,1)S(1)} collective-permute-done((bf16[1,64,1024]{2,1,0:T(8,128)(2,1)S(1)}, bf16[1,64,1024]{2,1,0:T(8,128)(2,1)S(1)}, u32[]{:S(2)}, u32[]{:S(2)}) %collective-permute-start.51) | collective-permute-done | bytes 131104 | tf_op jit(solution)/shard_map/ppermute | solution.py:32
  387.7 4.2 collective-permute-done.55
  404.2 8.1 %collective-permute-done.63 = bf16[2,8,1024]{2,1,0:T(8,128)(2,1)S(1)} collective-permute-done((bf16[2,8,1024]{2,1,0:T(8,128)(2,1)}, bf16[2,8,1024]{2,1,0:T(8,128)(2,1)S(1)}, u32[]{:S(2)}, u32[]{:S(2)}) %collective-permute-start.63) | collective-permute-done | bytes 32800 | tf_op jit(solution)/shard_map/ppermute | solution.py:32
  437.4 6.0 %collective-permute-done.70 = bf16[1,192,1024]{2,1,0:T(8,128)(2,1)S(1)} collective-permute-done((bf16[1,192,1024]{2,1,0:T(8,128)(2,1)S(1)}, bf16[1,192,1024]{2,1,0:T(8,128)(2,1)S(1)}, u32[]{:S(2)}, u32[]{:S(2)}) %collective-permute-start.70) | collective-permute-done | bytes 393248 | tf_op jit(solution)/shard_map/ppermute | solution.py:32
  (480 shorter events, 160.1 us)
Async XLA Ops:
  2.1 23.3 %collective-permute-start = (bf16[256,1024]{1,0:T(8,128)(2,1)S(1)}, bf16[256,1024]{1,0:T(8,128)(2,1)S(1)}, u32[]{:S(2)}, u32[]{:S(2)}) collective-permute-start(bf16[256,1024]{1,0:T(8,128)(2,1)S(1)} %get-tuple-element.167.refs_0_), channel_id=1, source_target_pairs={{0,2},{1,3},{2,0},{3,1},{4,6},{5,7},{6,4},{7,5},{8,10},{9,11},{10,... | collective-permute-start | bytes 1572872 | tf_op jit(solution)/shard_map/ppermute | solution.py:32
  5.9 19.4 %all-to-all-start = ((bf16[8,2,3,1024]{3,1,2,0:T(2,128)(2,1)}), bf16[8,2,3,1024]{3,1,2,0:T(2,128)(2,1)S(1)}, u32[]{:S(2)}, u32[]{:S(2)}) async-start(bf16[8,2,3,1024]{3,1,2,0:T(2,128)(2,1)} %broadcast_in_dim.130), calls=%async_computation | async-start | bytes 196608 | tf_op jit(solution)/shard_map/all_to_all | solution.py:803
  31.1 16.8 %collective-permute-start.8 = (bf16[256,1024]{1,0:T(8,128)(2,1)S(1)}, bf16[256,1024]{1,0:T(8,128)(2,1)}, u32[]{:S(2)}, u32[]{:S(2)}) collective-permute-start(bf16[256,1024]{1,0:T(8,128)(2,1)S(1)} %get-tuple-element.162.refs_4_.refs_0_), channel_id=1, source_target_pairs={{0,1},{1,0},{2,3},{3,2},{4,5},{5,4},{6,7},{7,6},{8,9},{9,8},{10,11... | collective-permute-start | bytes 1572872 | tf_op jit(solution)/shard_map/ppermute | solution.py:32
  32.0 15.9 %collective-permute-start.6 = (bf16[256,1024]{1,0:T(8,128)(2,1)S(1)}, bf16[256,1024]{1,0:T(8,128)(2,1)S(1)}, u32[]{:S(2)}, u32[]{:S(2)}) collective-permute-start(bf16[256,1024]{1,0:T(8,128)(2,1)S(1)} %get-tuple-element.167.refs_0_), channel_id=1, source_target_pairs={{0,1},{1,0},{2,3},{3,2},{4,5},{5,4},{6,7},{7,6},{8,9},{9,8},{10,11... | collective-permute-start | bytes 1572872 | tf_op jit(solution)/shard_map/ppermute | solution.py:32
  32.3 15.5 %collective-permute-start.7 = (bf16[256,1024]{1,0:T(8,128)(2,1)S(1)}, bf16[256,1024]{1,0:T(8,128)(2,1)S(1)}, u32[]{:S(2)}, u32[]{:S(2)}) collective-permute-start(bf16[256,1024]{1,0:T(8,128)(2,1)S(1)} %collective-permute-done.refs_2_), channel_id=1, source_target_pairs={{0,1},{1,0},{2,3},{3,2},{4,5},{5,4},{6,7},{7,6},{8,9},{9,8},{10,11... | collective-permute-start | bytes 1572872 | tf_op jit(solution)/shard_map/ppermute | solution.py:32
  43.9 25.0 %collective-permute-start.2 = (bf16[256,2048]{1,0:T(8,128)(2,1)}, bf16[256,2048]{1,0:T(8,128)(2,1)S(1)}, u32[]{:S(2)}, u32[]{:S(2)}) collective-permute-start(bf16[256,2048]{1,0:T(8,128)(2,1)} %slice.431.refs_0_), channel_id=1, source_target_pairs={{0,2},{1,3},{2,0},{3,1},{4,6},{5,7},{6,4},{7,5},{8,10},{9,11},{10,... | collective-permute-start | bytes 3145736 | tf_op jit(solution)/shard_map/ppermute | solution.py:32
  68.9 24.2 %collective-permute-start.13 = (bf16[256,2048]{1,0:T(8,128)(2,1)}, bf16[256,2048]{1,0:T(8,128)(2,1)S(1)}, u32[]{:S(2)}, u32[]{:S(2)}) collective-permute-start(bf16[256,2048]{1,0:T(8,128)(2,1)} %slice.431.refs_0_), channel_id=1, source_target_pairs={{0,1},{1,0},{2,3},{3,2},{4,5},{5,4},{6,7},{7,6},{8,9},{9,8},{10,11... | collective-permute-start | bytes 3145736 | tf_op jit(solution)/shard_map/ppermute | solution.py:32
  68.9 24.3 %collective-permute-start.14 = (bf16[256,2048]{1,0:T(8,128)(2,1)S(1)}, bf16[256,2048]{1,0:T(8,128)(2,1)S(1)}, u32[]{:S(2)}, u32[]{:S(2)}) collective-permute-start(bf16[256,2048]{1,0:T(8,128)(2,1)S(1)} %collective-permute-done.2.refs_2_), channel_id=1, source_target_pairs={{0,1},{1,0},{2,3},{3,2},{4,5},{5,4},{6,7},{7,6},{8,9},{9,8},{10,11... | collective-permute-start | bytes 3145736 | tf_op jit(solution)/shard_map/ppermute | solution.py:32
  69.4 36.4 %collective-permute-start.15 = (bf16[512,1024]{1,0:T(8,128)(2,1)S(1)}, bf16[512,1024]{1,0:T(8,128)(2,1)}, u32[]{:S(2)}, u32[]{:S(2)}) collective-permute-start(bf16[512,1024]{1,0:T(8,128)(2,1)S(1)} %copy-done.39), channel_id=1, source_target_pairs={{0,2},{1,3},{2,0},{3,1},{4,6},{5,7},{6,4},{7,5},{8,10},{9,11},{10,... | collective-permute-start | bytes 3145736 | tf_op jit(solution)/shard_map/ppermute | solution.py:32
  90.8 15.1 %collective-permute-start.11 = (bf16[40,2048]{1,0:T(8,128)(2,1)S(1)}, bf16[40,2048]{1,0:T(8,128)(2,1)S(1)}, u32[]{:S(2)}, u32[]{:S(2)}) collective-permute-start(bf16[40,2048]{1,0:T(8,128)(2,1)S(1)} %get-tuple-element.176), channel_id=1, source_target_pairs={{0,16},{4,20},{8,24},{12,28},{16,0},{20,4},{24,8},{28,12},{1,17},{... | collective-permute-start | bytes 491528 | tf_op jit(solution)/shard_map/ppermute | solution.py:32
  182.5 22.8 %collective-permute-start.22 = (bf16[32,2048]{1,0:T(8,128)(2,1)}, bf16[32,2048]{1,0:T(8,128)(2,1)S(1)}, u32[]{:S(2)}, u32[]{:S(2)}) collective-permute-start(bf16[32,2048]{1,0:T(8,128)(2,1)} %get-tuple-element.206), channel_id=1, source_target_pairs={{0,8},{4,12},{8,0},{12,4},{16,24},{20,28},{24,16},{28,20},{1,9},{5... | collective-permute-start | bytes 393224 | tf_op jit(solution)/shard_map/ppermute | solution.py:32
  185.0 20.3 %collective-permute-start.23 = (bf16[32,2048]{1,0:T(8,128)(2,1)}, bf16[32,2048]{1,0:T(8,128)(2,1)S(1)}, u32[]{:S(2)}, u32[]{:S(2)}) collective-permute-start(bf16[32,2048]{1,0:T(8,128)(2,1)} %get-tuple-element.206), channel_id=1, source_target_pairs={{0,16},{4,20},{8,24},{12,28},{16,0},{20,4},{24,8},{28,12},{1,17},{... | collective-permute-start | bytes 393224 | tf_op jit(solution)/shard_map/ppermute | solution.py:32
  186.0 19.4 %collective-permute-start.24 = (bf16[32,2048]{1,0:T(8,128)(2,1)}, bf16[32,2048]{1,0:T(8,128)(2,1)S(1)}, u32[]{:S(2)}, u32[]{:S(2)}) collective-permute-start(bf16[32,2048]{1,0:T(8,128)(2,1)} %get-tuple-element.206), channel_id=1, source_target_pairs={{0,24},{4,28},{8,16},{12,20},{16,8},{20,12},{24,0},{28,4},{1,25},{... | collective-permute-start | bytes 393224 | tf_op jit(solution)/shard_map/ppermute | solution.py:32
  220.1 57.4 %collective-permute-start.31 = (bf16[1,512,1024]{2,1,0:T(8,128)(2,1)}, bf16[1,512,1024]{2,1,0:T(8,128)(2,1)}, u32[]{:S(2)}, u32[]{:S(2)}) collective-permute-start(bf16[1,512,1024]{2,1,0:T(8,128)(2,1)} %get-tuple-element.217), channel_id=1, source_target_pairs={{0,2},{1,3},{2,0},{3,1},{4,6},{5,7},{6,4},{7,5},{8,10},{9,11},{10,... | collective-permute-start | bytes 3145736 | tf_op jit(solution)/shard_map/ppermute | solution.py:32
  220.7 56.8 %collective-permute-start.32 = (bf16[2,128,2048]{2,1,0:T(8,128)(2,1)}, bf16[2,128,2048]{2,1,0:T(8,128)(2,1)S(1)}, u32[]{:S(2)}, u32[]{:S(2)}) collective-permute-start(bf16[2,128,2048]{2,1,0:T(8,128)(2,1)} %get-tuple-element.218), channel_id=1, source_target_pairs={{0,8},{4,12},{8,0},{12,4},{16,24},{20,28},{24,16},{28,20},{1,9},{5... | collective-permute-start | bytes 3145736 | tf_op jit(solution)/shard_map/ppermute | solution.py:32
  281.0 31.6 %collective-permute-start.33 = (bf16[1,256,1024]{2,1,0:T(8,128)(2,1)}, bf16[1,256,1024]{2,1,0:T(8,128)(2,1)S(1)}, u32[]{:S(2)}, u32[]{:S(2)}) collective-permute-start(bf16[1,256,1024]{2,1,0:T(8,128)(2,1)} %get-tuple-element.331), channel_id=1, source_target_pairs={{0,4},{4,0},{8,12},{12,8},{16,20},{20,16},{24,28},{28,24},{1,5},{5... | collective-permute-start | bytes 1572872 | tf_op jit(solution)/shard_map/ppermute | solution.py:32
  283.7 29.0 %collective-permute-start.34 = (bf16[2,64,2048]{2,1,0:T(8,128)(2,1)}, bf16[2,64,2048]{2,1,0:T(8,128)(2,1)S(1)}, u32[]{:S(2)}, u32[]{:S(2)}) collective-permute-start(bf16[2,64,2048]{2,1,0:T(8,128)(2,1)} %get-tuple-element.329), channel_id=1, source_target_pairs={{0,16},{4,20},{8,24},{12,28},{16,0},{20,4},{24,8},{28,12},{1,17},{... | collective-permute-start | bytes 1572872 | tf_op jit(solution)/shard_map/ppermute | solution.py:32
  288.0 24.6 %collective-permute-start.38 = (bf16[96,512]{1,0:T(8,128)(2,1)S(1)}, bf16[96,512]{1,0:T(8,128)(2,1)S(1)}, u32[]{:S(2)}, u32[]{:S(2)}) collective-permute-start(bf16[96,512]{1,0:T(8,128)(2,1)S(1)} %get-tuple-element.364), channel_id=1, source_target_pairs={{0,1},{1,0},{2,3},{3,2},{4,5},{5,4},{6,7},{7,6},{8,9},{9,8},{10,11... | collective-permute-start | bytes 294920 | tf_op jit(solution)/shard_map/ppermute | solution.py:32
  288.5 24.1 %collective-permute-start.40 = (bf16[96,512]{1,0:T(8,128)(2,1)S(1)}, bf16[96,512]{1,0:T(8,128)(2,1)S(1)}, u32[]{:S(2)}, u32[]{:S(2)}) collective-permute-start(bf16[96,512]{1,0:T(8,128)(2,1)S(1)} %add_convert_fusion.36), channel_id=1, source_target_pairs={{0,2},{1,3},{2,0},{3,1},{4,6},{5,7},{6,4},{7,5},{8,10},{9,11},{10,... | collective-permute-start | bytes 294920 | tf_op jit(solution)/shard_map/ppermute | solution.py:32
  312.6 15.6 %collective-permute-start.37 = (bf16[2,256,1024]{2,1,0:T(8,128)(2,1)}, bf16[2,256,1024]{2,1,0:T(8,128)(2,1)}, u32[]{:S(2)}, u32[]{:S(2)}) collective-permute-start(bf16[2,256,1024]{2,1,0:T(8,128)(2,1)} %get-tuple-element.259), channel_id=1, source_target_pairs={{0,1},{1,0},{2,3},{3,2},{4,5},{5,4},{6,7},{7,6},{8,9},{9,8},{10,11... | collective-permute-start | bytes 3145736 | tf_op jit(solution)/shard_map/ppermute | solution.py:32
  315.5 17.4 %collective-permute-start.48 = (bf16[104,512]{1,0:T(8,128)(2,1)S(1)}, bf16[104,512]{1,0:T(8,128)(2,1)S(1)}, u32[]{:S(2)}, u32[]{:S(2)}) collective-permute-start(bf16[104,512]{1,0:T(8,128)(2,1)S(1)} %broadcast_select_fusion.41), channel_id=1, source_target_pairs={{0,1},{1,0},{2,3},{3,2},{4,5},{5,4},{6,7},{7,6},{8,9},{9,8},{10,11... | collective-permute-start | bytes 319496 | tf_op jit(solution)/shard_map/ppermute | solution.py:32
  374.1 17.8 %collective-permute-start.55 = (bf16[1,128,1024]{2,1,0:T(8,128)(2,1)S(1)}, bf16[1,128,1024]{2,1,0:T(8,128)(2,1)}, u32[]{:S(2)}, u32[]{:S(2)}) collective-permute-start(bf16[1,128,1024]{2,1,0:T(8,128)(2,1)S(1)} %pad_maximum_fusion.7), channel_id=1, source_target_pairs={{0,8},{4,12},{8,0},{12,4},{16,24},{20,28},{24,16},{28,20},{1,9},{5... | collective-permute-start | bytes 786440 | tf_op jit(solution)/shard_map/ppermute | solution.py:32
  392.6 19.8 %collective-permute-start.59 = (bf16[1,48,1024]{2,1,0:T(8,128)(2,1)}, bf16[1,48,1024]{2,1,0:T(8,128)(2,1)}, u32[]{:S(2)}, u32[]{:S(2)}) collective-permute-start(bf16[1,48,1024]{2,1,0:T(8,128)(2,1)} %broadcast_select_fusion.46), channel_id=1, source_target_pairs={{0,16},{4,20},{8,24},{12,28},{16,0},{20,4},{24,8},{28,12},{1,17},{... | collective-permute-start | bytes 294920 | tf_op jit(solution)/shard_map/ppermute | solution.py:32
  395.7 16.7 %collective-permute-start.60 = (bf16[1,256,1024]{2,1,0:T(8,128)(2,1)}, bf16[1,256,1024]{2,1,0:T(8,128)(2,1)}, u32[]{:S(2)}, u32[]{:S(2)}) collective-permute-start(bf16[1,256,1024]{2,1,0:T(8,128)(2,1)} %pad_maximum_fusion.3), channel_id=1, source_target_pairs={{0,4},{4,0},{8,12},{12,8},{16,20},{20,16},{24,28},{28,24},{1,5},{5... | collective-permute-start | bytes 1572872 | tf_op jit(solution)/shard_map/ppermute | solution.py:32
  (131 other events, 1286.3 us)

commit v6 on v5

--- a/solution.py
+++ b/solution.py
@@ -801,8 +801,8 @@
     last_rows = jnp.broadcast_to(last_rows[None], (ctx, 2, 3, features))
     token_rel = to_blocks(own_rows, depth).reshape(2, piece, features)
     tails = lax.all_to_all(last_rows, "ctx", 0, 0)
-    x_far, second, rows_head, tails, token_rel, scal, plan_before, plan_behind = together(
-        x_far, in_proj[:, half:width], rows_head, tails, token_rel, scal, plan_before, plan_behind
+    x_far, second, rows_head, tails, scal, plan_before, plan_behind = together(
+        x_far, in_proj[:, half:width], rows_head, tails, scal, plan_before, plan_behind
     )
     x_first = [block for own in x_far for block in (own, swap(own, "fsdp", 1))]
     small_blocks = gather_fsdp(rows_head)
@@ -821,6 +821,7 @@
     codes = jnp.stack([block[8, :4] for block in small_blocks]).astype(F32)
     count = jnp.sum(codes[:, 0:2] * 128.0 + codes[:, 2:4])
     scale = ((fsdp * rows_all * ctx) / count).reshape(1, 1)
+    normed, scale = together(normed, scale)
 
     def cols_at(block):
         per = part // block

time: 460 us -> 454 us (0.987)
    unnamed x173 -> x163, local copies, waits for them, and re-layouts: 10.9 us -> 12.3 us
  transfers between devices with their start and end apart: 73 -> 73, of which waited for: 20 -> 21; matrix products, arithmetic and copies ran while one was open for 13% -> 12% of each run, Pallas kernels for 32% -> 32%
where the time goes in v6:
time: 454 us; the launch traced here: 448 us
  Pallas kernels  201 us (44%)
  waiting for transfers between devices  81 us (18%)
  starting transfers between devices  71.8 us (16%)
  other arithmetic  54.6 us (12%)
  local copies, waits for them, and re-layouts  27 us (6%)
  between operations  12.3 us (3%)
    pallas_call x9, Pallas kernels, call(): pl.pallas_call(kernel, grid_spec=pltpu.PrefetchScalarGridSpec(num_scalar_...  195 us
    ppermute x72, waiting for transfers between devices, swap(): return lax.ppermute(values, axis, [(i, i ^ bit) for i in range(size)])  81 us
    ppermute x72, starting transfers between devices, swap(): return lax.ppermute(values, axis, [(i, i ^ bit) for i in range(size)])  66 us
    unnamed x163, local copies, waits for them, and re-layouts  12.3 us
  transfers between devices with their start and end apart: 73, of which 21 were waited for; matrix products, arithmetic and copies ran while one was open for 12% of the time, Pallas kernels for 32%

profile of v6, /device:TPU:0, one launch (start us, length us, event | category | flops | bytes accessed | tf_op | source)
XLA Modules:
  0.0 448.0 jit_solution(8214558685970846673)
XLA Ops:
  2.2 3.0 collective-permute-start
  6.8 5.8 %all-to-all-start = ((bf16[8,2,3,1024]{3,1,2,0:T(2,128)(2,1)}), bf16[8,2,3,1024]{3,1,2,0:T(2,128)(2,1)S(1)}, u32[]{:S(2)}, u32[]{:S(2)}) async-start(bf16[8,2,3,1024]{3,1,2,0:T(2,128)(2,1)} %broadcast_in_dim.130), calls=%async_computation | async-start | bytes 196608 | tf_op jit(solution)/shard_map/all_to_all | solution.py:803
  32.1 7.4 %collective-permute-done.1.refs_6_.refs_2_ = bf16[256,1024]{1,0:T(8,128)(2,1)} collective-permute-done((bf16[256,1024]{1,0:T(8,128)(2,1)S(1)}, bf16[256,1024]{1,0:T(8,128)(2,1)}, u32[]{:S(2)}, u32[]{:S(2)}) %collective-permute-start.1) | collective-permute-done | bytes 524320 | tf_op jit(solution)/shard_map/ppermute | solution.py:32
  47.7 13.5 %inputs.1 = (bf16[2,272,2048]{2,1,0:T(8,128)(2,1)S(1)}, f32[2,256,2048]{2,1,0:T(8,128)S(1)}, bf16[2,256,2048]{2,1,0:T(8,128)(2,1)S(1)}, f32[512,96]{1,0:T(8,128)S(1)}) custom-call(s32[3]{0:T(128)S(1)} %pad_add_fusion.3.scal, bf16[544,1024]{1,0:T(8,128)(2,1)S(1)} %fusion.1.normed_ref, bf16[256,1024]{1,0:T(8,128)(2,1)S(1)} %copy-done.13, ...), custom_call_target="tpu_custom_call" | custom-call | flops 2147483648 | bytes 14811136 | tf_op jit(solution)/shard_map/inputs/pallas_call | solution.py:684
  68.1 16.3 %end_states.1 = (f32[2,32,8,2048]{3,2,1,0:T(8,128)S(1)}, bf16[40,2048]{1,0:T(8,128)(2,1)S(1)}) custom-call(s32[3]{0:T(128)S(1)} %pad_add_fusion.3.scal, f32[512,96]{1,0:T(8,128)S(1)} %get-tuple-element.171.proj_ref.refs_13_.refs_15_, bf16[192,2048]{1,0:T(8,128)(2,1)S(1)} %copy-done.6, bf16[2,256,2048]{2,1,0:T(8,128)(2,1)S(1)} %get-tuple-element.172.xs_ref.refs_10_.refs_18_, ...), custom_call_target="tpu_custom_call" | custom-call | flops 83886080 | bytes 11632640 | tf_op jit(solution)/shard_map/end_states/pallas_call | solution.py:684
  88.9 7.1 %gates.1.refs_11_.gate_ref = f32[2,256,2048]{2,1,0:T(8,128)S(1)} custom-call(s32[3]{0:T(128)S(1)} %pad_add_fusion.3.scal, bf16[544,1024]{1,0:T(8,128)(2,1)S(1)} %fusion.1.normed_ref, bf16[256,2048]{1,0:T(8,128)(2,1)} %slice.431.refs_0_, bf16[256,2048]{1,0:T(8,128)(2,1)S(1)} %collective-permute-done.13.refs_1_, ...), custom_call_target="tpu_custom_call" | custom-call | flops 2147483648 | bytes 9502720 | tf_op jit(solution)/shard_map/gates/pallas_call | solution.py:684
  96.0 5.2 %collective-permute-done.11.refs_3_.refs_10_ = bf16[40,2048]{1,0:T(8,128)(2,1)S(1)} collective-permute-done((bf16[40,2048]{1,0:T(8,128)(2,1)S(1)}, bf16[40,2048]{1,0:T(8,128)(2,1)S(1)}, u32[]{:S(2)}, u32[]{:S(2)}) %collective-permute-start.11) | collective-permute-done | bytes 163872 | tf_op jit(solution)/shard_map/ppermute | solution.py:32
  112.4 3.5 collective-permute-done.18.refs_4_.refs_11_
  119.2 33.8 %forward_states.1 = (f32[2,256,2048]{2,1,0:T(8,128)}, bf16[2,256,2048]{2,1,0:T(8,128)(2,1)}, bf16[16,2,256,16,128]{4,3,2,1,0:T(8,128)(2,1)}, f32[2,16,2048]{2,1,...) custom-call(s32[3]{0:T(128)} %copy-done.18, ...), custom_call_target="tpu_custom_call" | custom-call | flops 167772160 | bytes 67452928 | tf_op jit(solution)/shard_map/forward_states/pallas_call | solution.py:684
  153.0 22.8 %first_grads.1 = (f32[2,32,8,2048]{3,2,1,0:T(8,128)}, bf16[2,256,2048]{2,1,0:T(8,128)(2,1)}, f32[1,2048]{1,0:T(1,128)}, bf16[32,2048]{1,0:T(8,128)(2,1)}) custom-call(s32[3]{0:T(128)} %copy-done.18, bf16[512,1024]{1,0:T(8,128)(2,1)} %get-tuple-element.198.dout_ref, bf16[2048,1024]{1,0:T(8,128)(2,1)} %pad_maximum_fusion.refs_14_.weight_ref, ...), custom_call_target="tpu_custom_call" | custom-call | flops 100663296 | bytes 31334400 | tf_op jit(solution)/shard_map/first_grads/pallas_call | solution.py:684
  181.2 12.0 %gate_grads.1 = (bf16[2,256,2048]{2,1,0:T(8,128)(2,1)}, bf16[2,256,2048]{2,1,0:T(8,128)(2,1)}, f32[544,1024]{1,0:T(8,128)}) custom-call(s32[3]{0:T(128)} %copy-done.18, bf16[544,1024]{1,0:T(8,128)(2,1)} %copy-done.1, bf16[2,256,2048]{2,1,0:T(8,128)(2,1)} %get-tuple-element.202.dgate_ref, bf16[256,2048]{1,0:T(8,128)(2,1)} %slice.431.refs_0_, ...), custom_call_target="tpu_custom_call" | custom-call | flops 4294967296 | bytes 13828096 | tf_op jit(solution)/shard_map/gate_grads/pallas_call | solution.py:684
  193.2 5.9 %out_grads.1 = (bf16[2,512,1024]{2,1,0:T(8,128)(2,1)}, bf16[2,512,1024]{2,1,0:T(8,128)(2,1)}) custom-call(bf16[512,2048]{1,0:T(8,128)(2,1)} %bitcast.125, bf16[512,2048]{1,0:T(8,128)(2,1)} %bitcast.126, bf16[512,1024]{1,0:T(8,128)(2,1)} %get-tuple-element.198.dout_ref), custom_call_target="tpu_custom_call" | custom-call | flops 2147483648 | bytes 9437184 | tf_op jit(solution)/shard_map/out_grads/pallas_call | solution.py:977
  205.1 3.3 broadcast_select_fusion
  208.5 3.5 add_convert_fusion.2
  216.2 54.9 %backward_states.1 = (f32[2,256,2048]{2,1,0:T(8,128)}, f32[88,2048]{1,0:T(8,128)}, f32[512,64]{1,0:T(8,128)}, f32[2,16,256]{2,1,0:T(8,128)}, f32[2,16,256]{2,1,0:T(8,128)}) custom-call(s32[3]{0:T(128)} %copy-done.18, bf16[32,2048]{1,0:T(8,128)(2,1)} %copy-done.53, bf16[32,2048]{1,0:T(8,128)(2,1)} %copy-done.50, bf16[32,2048]{1,0:T(8,128)(2,1)} %copy-done.54, ...), custom_call_target="tpu_custom_call" | custom-call | flops 268435456 | bytes 56672256 | tf_op jit(solution)/shard_map/backward_states/pallas_call | solution.py:684
  283.6 22.5 %tail_grads.2 = (f32[104,1024]{1,0:T(8,128)}, bf16[2,256,1024]{2,1,0:T(8,128)(2,1)}, bf16[2,256,1024]{2,1,0:T(8,128)(2,1)}, f32[544,1024]{1,0:T(8,128)}) custom-call(s32[3]{0:T(128)} %copy-done.18, bf16[512,96]{1,0:T(8,128)(2,1)} %pad_maximum_fusion.13.dproj_ref, bf16[192,2048]{1,0:T(8,128)(2,1)} %copy-done.4, f32[2,256,2048]{2,1,0:T(8,128)} %get-tuple-element.245.dxs_ref, ...), custom_call_target="tpu_custom_call" | custom-call | flops 2147483648 | bytes 23789568 | tf_op jit(solution)/shard_map/tail_grads/pallas_call | solution.py:684
  311.0 12.6 %tail_grads.3 = (f32[104,1024]{1,0:T(8,128)}, bf16[2,256,1024]{2,1,0:T(8,128)(2,1)}, bf16[2,256,1024]{2,1,0:T(8,128)(2,1)}, f32[544,1024]{1,0:T(8,128)}) custom-call(s32[3]{0:T(128)} %copy-done.18, bf16[512,96]{1,0:T(8,128)(2,1)} %pad_maximum_fusion.13.dproj_ref, bf16[192,2048]{1,0:T(8,128)(2,1)} %copy-done.4, f32[2,256,2048]{2,1,0:T(8,128)} %get-tuple-element.245.dxs_ref, ...), custom_call_target="tpu_custom_call" | custom-call | flops 2147483648 | bytes 23789568 | tf_op jit(solution)/shard_map/tail_grads/pallas_call | solution.py:684
  330.0 9.0 %collective-permute-done.41 = bf16[2,128,1024]{2,1,0:T(8,128)(2,1)S(1)} collective-permute-done((bf16[2,128,1024]{2,1,0:T(8,128)(2,1)S(1)}, bf16[2,128,1024]{2,1,0:T(8,128)(2,1)S(1)}, u32[]{:S(2)}, u32[]{:S(2)}) %collective-permute-start.41) | collective-permute-done | bytes 524320 | tf_op jit(solution)/shard_map/ppermute | solution.py:32
  341.1 6.4 %collective-permute-done.46 = bf16[2,64,1024]{2,1,0:T(8,128)(2,1)S(1)} collective-permute-done((bf16[2,64,1024]{2,1,0:T(8,128)(2,1)S(1)}, bf16[2,64,1024]{2,1,0:T(8,128)(2,1)S(1)}, u32[]{:S(2)}, u32[]{:S(2)}) %collective-permute-start.46) | collective-permute-done | bytes 262176 | tf_op jit(solution)/shard_map/ppermute | solution.py:32
  347.6 5.1 %collective-permute-done.43 = bf16[1,256,1024]{2,1,0:T(8,128)(2,1)S(1)} collective-permute-done((bf16[1,256,1024]{2,1,0:T(8,128)(2,1)S(1)}, bf16[1,256,1024]{2,1,0:T(8,128)(2,1)S(1)}, u32[]{:S(2)}, u32[]{:S(2)}) %collective-permute-start.43) | collective-permute-done | bytes 524320 | tf_op jit(solution)/shard_map/ppermute | solution.py:32
  358.8 7.0 %collective-permute-done.51 = bf16[1,64,1024]{2,1,0:T(8,128)(2,1)S(1)} collective-permute-done((bf16[1,64,1024]{2,1,0:T(8,128)(2,1)S(1)}, bf16[1,64,1024]{2,1,0:T(8,128)(2,1)S(1)}, u32[]{:S(2)}, u32[]{:S(2)}) %collective-permute-start.51) | collective-permute-done | bytes 131104 | tf_op jit(solution)/shard_map/ppermute | solution.py:32
  382.5 4.2 collective-permute-done.55
  399.1 8.2 %collective-permute-done.63 = bf16[2,8,1024]{2,1,0:T(8,128)(2,1)S(1)} collective-permute-done((bf16[2,8,1024]{2,1,0:T(8,128)(2,1)}, bf16[2,8,1024]{2,1,0:T(8,128)(2,1)S(1)}, u32[]{:S(2)}, u32[]{:S(2)}) %collective-permute-start.63) | collective-permute-done | bytes 32800 | tf_op jit(solution)/shard_map/ppermute | solution.py:32
  432.3 6.0 %collective-permute-done.70 = bf16[1,192,1024]{2,1,0:T(8,128)(2,1)S(1)} collective-permute-done((bf16[1,192,1024]{2,1,0:T(8,128)(2,1)S(1)}, bf16[1,192,1024]{2,1,0:T(8,128)(2,1)S(1)}, u32[]{:S(2)}, u32[]{:S(2)}) %collective-permute-start.70) | collective-permute-done | bytes 393248 | tf_op jit(solution)/shard_map/ppermute | solution.py:32
  (468 shorter events, 156.8 us)
Async XLA Ops:
  2.2 19.8 %collective-permute-start = (bf16[256,1024]{1,0:T(8,128)(2,1)S(1)}, bf16[256,1024]{1,0:T(8,128)(2,1)}, u32[]{:S(2)}, u32[]{:S(2)}) collective-permute-start(bf16[256,1024]{1,0:T(8,128)(2,1)S(1)} %get-tuple-element.168.refs_0_), channel_id=1, source_target_pairs={{0,2},{1,3},{2,0},{3,1},{4,6},{5,7},{6,4},{7,5},{8,10},{9,11},{10,... | collective-permute-start | bytes 1572872 | tf_op jit(solution)/shard_map/ppermute | solution.py:32
  6.8 15.1 %all-to-all-start = ((bf16[8,2,3,1024]{3,1,2,0:T(2,128)(2,1)}), bf16[8,2,3,1024]{3,1,2,0:T(2,128)(2,1)S(1)}, u32[]{:S(2)}, u32[]{:S(2)}) async-start(bf16[8,2,3,1024]{3,1,2,0:T(2,128)(2,1)} %broadcast_in_dim.130), calls=%async_computation | async-start | bytes 196608 | tf_op jit(solution)/shard_map/all_to_all | solution.py:803
  22.5 16.9 %collective-permute-start.1 = (bf16[256,1024]{1,0:T(8,128)(2,1)S(1)}, bf16[256,1024]{1,0:T(8,128)(2,1)}, u32[]{:S(2)}, u32[]{:S(2)}) collective-permute-start(bf16[256,1024]{1,0:T(8,128)(2,1)S(1)} %get-tuple-element.163.refs_4_.refs_0_), channel_id=1, source_target_pairs={{0,2},{1,3},{2,0},{3,1},{4,6},{5,7},{6,4},{7,5},{8,10},{9,11},{10,... | collective-permute-start | bytes 1572872 | tf_op jit(solution)/shard_map/ppermute | solution.py:32
  24.1 20.4 %collective-permute-start.8 = (bf16[256,1024]{1,0:T(8,128)(2,1)S(1)}, bf16[256,1024]{1,0:T(8,128)(2,1)}, u32[]{:S(2)}, u32[]{:S(2)}) collective-permute-start(bf16[256,1024]{1,0:T(8,128)(2,1)S(1)} %get-tuple-element.163.refs_4_.refs_0_), channel_id=1, source_target_pairs={{0,1},{1,0},{2,3},{3,2},{4,5},{5,4},{6,7},{7,6},{8,9},{9,8},{10,11... | collective-permute-start | bytes 1572872 | tf_op jit(solution)/shard_map/ppermute | solution.py:32
  26.9 17.5 %collective-permute-start.6 = (bf16[256,1024]{1,0:T(8,128)(2,1)S(1)}, bf16[256,1024]{1,0:T(8,128)(2,1)}, u32[]{:S(2)}, u32[]{:S(2)}) collective-permute-start(bf16[256,1024]{1,0:T(8,128)(2,1)S(1)} %get-tuple-element.168.refs_0_), channel_id=1, source_target_pairs={{0,1},{1,0},{2,3},{3,2},{4,5},{5,4},{6,7},{7,6},{8,9},{9,8},{10,11... | collective-permute-start | bytes 1572872 | tf_op jit(solution)/shard_map/ppermute | solution.py:32
  39.5 25.1 %collective-permute-start.2 = (bf16[256,2048]{1,0:T(8,128)(2,1)}, bf16[256,2048]{1,0:T(8,128)(2,1)}, u32[]{:S(2)}, u32[]{:S(2)}) collective-permute-start(bf16[256,2048]{1,0:T(8,128)(2,1)} %slice.431.refs_0_), channel_id=1, source_target_pairs={{0,2},{1,3},{2,0},{3,1},{4,6},{5,7},{6,4},{7,5},{8,10},{9,11},{10,... | collective-permute-start | bytes 3145736 | tf_op jit(solution)/shard_map/ppermute | solution.py:32
  64.5 24.0 %collective-permute-start.13 = (bf16[256,2048]{1,0:T(8,128)(2,1)}, bf16[256,2048]{1,0:T(8,128)(2,1)S(1)}, u32[]{:S(2)}, u32[]{:S(2)}) collective-permute-start(bf16[256,2048]{1,0:T(8,128)(2,1)} %slice.431.refs_0_), channel_id=1, source_target_pairs={{0,1},{1,0},{2,3},{3,2},{4,5},{5,4},{6,7},{7,6},{8,9},{9,8},{10,11... | collective-permute-start | bytes 3145736 | tf_op jit(solution)/shard_map/ppermute | solution.py:32
  65.1 23.8 %collective-permute-start.14 = (bf16[256,2048]{1,0:T(8,128)(2,1)}, bf16[256,2048]{1,0:T(8,128)(2,1)S(1)}, u32[]{:S(2)}, u32[]{:S(2)}) collective-permute-start(bf16[256,2048]{1,0:T(8,128)(2,1)} %collective-permute-done.2.refs_2_), channel_id=1, source_target_pairs={{0,1},{1,0},{2,3},{3,2},{4,5},{5,4},{6,7},{7,6},{8,9},{9,8},{10,11... | collective-permute-start | bytes 3145736 | tf_op jit(solution)/shard_map/ppermute | solution.py:32
  65.2 36.0 %collective-permute-start.15 = (bf16[512,1024]{1,0:T(8,128)(2,1)S(1)}, bf16[512,1024]{1,0:T(8,128)(2,1)S(1)}, u32[]{:S(2)}, u32[]{:S(2)}) collective-permute-start(bf16[512,1024]{1,0:T(8,128)(2,1)S(1)} %copy-done.33), channel_id=1, source_target_pairs={{0,2},{1,3},{2,0},{3,1},{4,6},{5,7},{6,4},{7,5},{8,10},{9,11},{10,... | collective-permute-start | bytes 3145736 | tf_op jit(solution)/shard_map/ppermute | solution.py:32
  86.2 15.0 %collective-permute-start.11 = (bf16[40,2048]{1,0:T(8,128)(2,1)S(1)}, bf16[40,2048]{1,0:T(8,128)(2,1)S(1)}, u32[]{:S(2)}, u32[]{:S(2)}) collective-permute-start(bf16[40,2048]{1,0:T(8,128)(2,1)S(1)} %get-tuple-element.177), channel_id=1, source_target_pairs={{0,16},{4,20},{8,24},{12,28},{16,0},{20,4},{24,8},{28,12},{1,17},{... | collective-permute-start | bytes 491528 | tf_op jit(solution)/shard_map/ppermute | solution.py:32
  175.8 23.3 %collective-permute-start.22 = (bf16[32,2048]{1,0:T(8,128)(2,1)}, bf16[32,2048]{1,0:T(8,128)(2,1)S(1)}, u32[]{:S(2)}, u32[]{:S(2)}) collective-permute-start(bf16[32,2048]{1,0:T(8,128)(2,1)} %get-tuple-element.208), channel_id=1, source_target_pairs={{0,8},{4,12},{8,0},{12,4},{16,24},{20,28},{24,16},{28,20},{1,9},{5... | collective-permute-start | bytes 393224 | tf_op jit(solution)/shard_map/ppermute | solution.py:32
  178.8 20.3 %collective-permute-start.23 = (bf16[32,2048]{1,0:T(8,128)(2,1)}, bf16[32,2048]{1,0:T(8,128)(2,1)S(1)}, u32[]{:S(2)}, u32[]{:S(2)}) collective-permute-start(bf16[32,2048]{1,0:T(8,128)(2,1)} %get-tuple-element.208), channel_id=1, source_target_pairs={{0,16},{4,20},{8,24},{12,28},{16,0},{20,4},{24,8},{28,12},{1,17},{... | collective-permute-start | bytes 393224 | tf_op jit(solution)/shard_map/ppermute | solution.py:32
  179.7 19.4 %collective-permute-start.24 = (bf16[32,2048]{1,0:T(8,128)(2,1)}, bf16[32,2048]{1,0:T(8,128)(2,1)S(1)}, u32[]{:S(2)}, u32[]{:S(2)}) collective-permute-start(bf16[32,2048]{1,0:T(8,128)(2,1)} %get-tuple-element.208), channel_id=1, source_target_pairs={{0,24},{4,28},{8,16},{12,20},{16,8},{20,12},{24,0},{28,4},{1,25},{... | collective-permute-start | bytes 393224 | tf_op jit(solution)/shard_map/ppermute | solution.py:32
  213.8 57.3 %collective-permute-start.31 = (bf16[1,512,1024]{2,1,0:T(8,128)(2,1)}, bf16[1,512,1024]{2,1,0:T(8,128)(2,1)}, u32[]{:S(2)}, u32[]{:S(2)}) collective-permute-start(bf16[1,512,1024]{2,1,0:T(8,128)(2,1)} %get-tuple-element.219), channel_id=1, source_target_pairs={{0,2},{1,3},{2,0},{3,1},{4,6},{5,7},{6,4},{7,5},{8,10},{9,11},{10,... | collective-permute-start | bytes 3145736 | tf_op jit(solution)/shard_map/ppermute | solution.py:32
  214.5 56.6 %collective-permute-start.32 = (bf16[2,128,2048]{2,1,0:T(8,128)(2,1)}, bf16[2,128,2048]{2,1,0:T(8,128)(2,1)S(1)}, u32[]{:S(2)}, u32[]{:S(2)}) collective-permute-start(bf16[2,128,2048]{2,1,0:T(8,128)(2,1)} %get-tuple-element.220), channel_id=1, source_target_pairs={{0,8},{4,12},{8,0},{12,4},{16,24},{20,28},{24,16},{28,20},{1,9},{5... | collective-permute-start | bytes 3145736 | tf_op jit(solution)/shard_map/ppermute | solution.py:32
  274.6 31.6 %collective-permute-start.33 = (bf16[1,256,1024]{2,1,0:T(8,128)(2,1)}, bf16[1,256,1024]{2,1,0:T(8,128)(2,1)S(1)}, u32[]{:S(2)}, u32[]{:S(2)}) collective-permute-start(bf16[1,256,1024]{2,1,0:T(8,128)(2,1)} %get-tuple-element.335), channel_id=1, source_target_pairs={{0,4},{4,0},{8,12},{12,8},{16,20},{20,16},{24,28},{28,24},{1,5},{5... | collective-permute-start | bytes 1572872 | tf_op jit(solution)/shard_map/ppermute | solution.py:32
  277.3 28.9 %collective-permute-start.34 = (bf16[2,64,2048]{2,1,0:T(8,128)(2,1)}, bf16[2,64,2048]{2,1,0:T(8,128)(2,1)S(1)}, u32[]{:S(2)}, u32[]{:S(2)}) collective-permute-start(bf16[2,64,2048]{2,1,0:T(8,128)(2,1)} %get-tuple-element.333), channel_id=1, source_target_pairs={{0,16},{4,20},{8,24},{12,28},{16,0},{20,4},{24,8},{28,12},{1,17},{... | collective-permute-start | bytes 1572872 | tf_op jit(solution)/shard_map/ppermute | solution.py:32
  281.6 24.6 %collective-permute-start.38 = (bf16[96,512]{1,0:T(8,128)(2,1)S(1)}, bf16[96,512]{1,0:T(8,128)(2,1)S(1)}, u32[]{:S(2)}, u32[]{:S(2)}) collective-permute-start(bf16[96,512]{1,0:T(8,128)(2,1)S(1)} %get-tuple-element.368), channel_id=1, source_target_pairs={{0,1},{1,0},{2,3},{3,2},{4,5},{5,4},{6,7},{7,6},{8,9},{9,8},{10,11... | collective-permute-start | bytes 294920 | tf_op jit(solution)/shard_map/ppermute | solution.py:32
  282.1 24.1 %collective-permute-start.40 = (bf16[96,512]{1,0:T(8,128)(2,1)S(1)}, bf16[96,512]{1,0:T(8,128)(2,1)S(1)}, u32[]{:S(2)}, u32[]{:S(2)}) collective-permute-start(bf16[96,512]{1,0:T(8,128)(2,1)S(1)} %add_convert_fusion.36), channel_id=1, source_target_pairs={{0,2},{1,3},{2,0},{3,1},{4,6},{5,7},{6,4},{7,5},{8,10},{9,11},{10,... | collective-permute-start | bytes 294920 | tf_op jit(solution)/shard_map/ppermute | solution.py:32
  307.0 16.6 %collective-permute-start.37 = (bf16[2,256,1024]{2,1,0:T(8,128)(2,1)}, bf16[2,256,1024]{2,1,0:T(8,128)(2,1)S(1)}, u32[]{:S(2)}, u32[]{:S(2)}) collective-permute-start(bf16[2,256,1024]{2,1,0:T(8,128)(2,1)} %get-tuple-element.261), channel_id=1, source_target_pairs={{0,1},{1,0},{2,3},{3,2},{4,5},{5,4},{6,7},{7,6},{8,9},{9,8},{10,11... | collective-permute-start | bytes 3145736 | tf_op jit(solution)/shard_map/ppermute | solution.py:32
  310.9 16.8 %collective-permute-start.48 = (bf16[104,512]{1,0:T(8,128)(2,1)S(1)}, bf16[104,512]{1,0:T(8,128)(2,1)S(1)}, u32[]{:S(2)}, u32[]{:S(2)}) collective-permute-start(bf16[104,512]{1,0:T(8,128)(2,1)S(1)} %broadcast_select_fusion.41), channel_id=1, source_target_pairs={{0,1},{1,0},{2,3},{3,2},{4,5},{5,4},{6,7},{7,6},{8,9},{9,8},{10,11... | collective-permute-start | bytes 319496 | tf_op jit(solution)/shard_map/ppermute | solution.py:32
  368.9 17.8 %collective-permute-start.55 = (bf16[1,128,1024]{2,1,0:T(8,128)(2,1)S(1)}, bf16[1,128,1024]{2,1,0:T(8,128)(2,1)}, u32[]{:S(2)}, u32[]{:S(2)}) collective-permute-start(bf16[1,128,1024]{2,1,0:T(8,128)(2,1)S(1)} %pad_maximum_fusion.6), channel_id=1, source_target_pairs={{0,8},{4,12},{8,0},{12,4},{16,24},{20,28},{24,16},{28,20},{1,9},{5... | collective-permute-start | bytes 786440 | tf_op jit(solution)/shard_map/ppermute | solution.py:32
  387.4 19.9 %collective-permute-start.59 = (bf16[1,48,1024]{2,1,0:T(8,128)(2,1)}, bf16[1,48,1024]{2,1,0:T(8,128)(2,1)}, u32[]{:S(2)}, u32[]{:S(2)}) collective-permute-start(bf16[1,48,1024]{2,1,0:T(8,128)(2,1)} %broadcast_select_fusion.46), channel_id=1, source_target_pairs={{0,16},{4,20},{8,24},{12,28},{16,0},{20,4},{24,8},{28,12},{1,17},{... | collective-permute-start | bytes 294920 | tf_op jit(solution)/shard_map/ppermute | solution.py:32
  390.6 16.7 %collective-permute-start.60 = (bf16[1,256,1024]{2,1,0:T(8,128)(2,1)}, bf16[1,256,1024]{2,1,0:T(8,128)(2,1)}, u32[]{:S(2)}, u32[]{:S(2)}) collective-permute-start(bf16[1,256,1024]{2,1,0:T(8,128)(2,1)} %pad_maximum_fusion.2), channel_id=1, source_target_pairs={{0,4},{4,0},{8,12},{12,8},{16,20},{20,16},{24,28},{28,24},{1,5},{5... | collective-permute-start | bytes 1572872 | tf_op jit(solution)/shard_map/ppermute | solution.py:32
  (126 other events, 1247.9 us)
